TPU v7x, 32 devices: a whole 2x2x4 slice. The times are simulated.
32 devices in a mesh: row: 8 (over z, x), col: 4 (over y, core).
Axes of the slice: x: 2, y: 2, z: 4, core: 2. Of those that a mesh axis runs over, the one named last changes fastest.
Arguments:
- inputs: bfloat16 [640, 12288], P('row', 'col'), may hold values from -6 to 6
- pre_act: bfloat16 [640, 24576], P('col', 'row'), may hold values from -6 to 6
- out_grad: bfloat16 [640, 12288], P('row', 'col'), may hold values from -6 to 6
- token_valid: int32 [640], P('row'), may hold values 0 or 1
- poison: int32 [8, 4], P('row', 'col'), may hold values 0 or 1
- w_up: bfloat16 [12288, 24576], P('col', 'row'), may hold values from -0.0546875 to 0.0546875
- w_down: bfloat16 [24576, 12288], P('row', 'col'), may hold values from -0.0390625 to 0.0390625
Outputs:
- input_grad: bfloat16 [640, 12288], P('row', 'col')
- grad_up: bfloat16 [12288, 24576], P('col', 'row')
- grad_down: bfloat16 [24576, 12288], P('row', 'col')
All inputs are finite; a program needn't handle non-finite values. No bound on the sum of `token_valid` or of `poison` on one device may be relied on, other than what follows from the above.
Results may differ from a plain program's by a relative error of at most 0.0051.
Values may be sent and summed in bfloat16 or wider, within the bound.
No kernel may reach another device: no remote copies, remote signals or barrier semaphores. Data moves between devices by JAX's collectives and lax.ppermute only.
A program may use at most 384 MiB of HBM per device.

v0:
```python
import math

import jax
import jax.numpy as jnp
from jax import lax
from jax.sharding import PartitionSpec as P


def gelu_value(hval):
    inner = math.sqrt(2.0 / math.pi) * (hval + 0.044715 * hval * hval * hval)
    return 0.5 * hval * (1.0 + jnp.tanh(inner))


def gelu_slope(hval):
    factor = math.sqrt(2.0 / math.pi)
    tanh_part = jnp.tanh(factor * (hval + 0.044715 * hval * hval * hval))
    return 0.5 * (1.0 + tanh_part) + 0.5 * hval * (1.0 - tanh_part * tanh_part) * factor * (
        1.0 + 3.0 * 0.044715 * hval * hval
    )


def on_device(inputs, pre_act, out_grad, token_valid, poison, w_up, w_down):
    n_row = lax.axis_size("row")
    n_col = lax.axis_size("col")
    keep_rows = token_valid.astype(jnp.bfloat16)[:, None]
    masked = out_grad * keep_rows
    inputs_all, masked_all = (
        lax.all_gather(inputs, "row", axis=0, tiled=True),
        lax.all_gather(masked, "row", axis=0, tiled=True),
    )
    contract_last = (((1,), (1,)), ((), ()))
    block = masked_all
    act_grad = lax.psum_scatter(
        lax.dot_general(block, w_down, contract_last, preferred_element_type=jnp.float32),
        "col",
        scatter_dimension=0,
        tiled=True,
    )
    hval = pre_act.astype(jnp.float32)
    activation = gelu_value(hval).astype(jnp.bfloat16)
    hidden_grad = (act_grad * gelu_slope(hval)).astype(jnp.bfloat16)
    act_all, hidden_all = (
        lax.all_gather(activation, "col", axis=0, tiled=True),
        lax.all_gather(hidden_grad, "col", axis=0, tiled=True),
    )
    contract_first = (((0,), (0,)), ((), ()))
    down_sum = lax.dot_general(
        act_all, masked_all, contract_first, preferred_element_type=jnp.float32
    )
    up_sum = lax.dot_general(
        inputs_all, hidden_all, contract_first, preferred_element_type=jnp.float32
    )
    block = hidden_all
    input_sum = lax.psum_scatter(
        lax.dot_general(block, w_up, contract_last, preferred_element_type=jnp.float32),
        "row",
        scatter_dimension=0,
        tiled=True,
    )
    first_col = (lax.axis_index("col") == 0).astype(jnp.float32)
    count_term = jnp.sum(token_valid.astype(jnp.float32)) * first_col
    flag_value = poison[0, 0].astype(jnp.float32)
    keep_block = 1.0 - flag_value
    square_term = keep_block * (jnp.sum(up_sum * up_sum) + jnp.sum(down_sum * down_sum))
    count_all, square_all, flag_all = lax.psum(
        (count_term, square_term, flag_value), ("row", "col")
    )
    token_total = jnp.maximum(count_all, 1.0)
    squares = square_all / (token_total * token_total)
    block_count = float(n_row * n_col)
    estimate = squares * block_count / jnp.maximum(block_count - flag_all, 1.0)
    total_tokens = inputs.shape[0] * n_row
    model_width = w_up.shape[0] * n_col
    hidden_width = w_up.shape[1] * n_row
    limit = 0.25 * math.sqrt(hidden_width * model_width / total_tokens)
    clip_factor = jnp.minimum(1.0, limit / jnp.sqrt(estimate + 1e-06))
    grad_up = (up_sum / token_total * (keep_block * clip_factor)).astype(jnp.bfloat16)
    grad_down = (down_sum / token_total * (keep_block * clip_factor)).astype(jnp.bfloat16)
    input_grad = (input_sum / token_total).astype(jnp.bfloat16)
    return (input_grad, grad_up, grad_down)


def solution(mesh):
    placed = (
        P("row", "col"),
        P("col", "row"),
        P("row", "col"),
        P("row"),
        P("row", "col"),
        P("col", "row"),
        P("row", "col"),
    )
    return jax.shard_map(
        on_device,
        mesh=mesh,
        in_specs=placed,
        out_specs=(P("row", "col"), P("col", "row"), P("row", "col")),
        check_vma=False,
    )
```

profile of v0, /device:TPU:0, one launch (start us, length us, event | category | flops | bytes accessed | tf_op | source)
XLA Modules:
  0.0 466.5 jit_solution(18234035663816908254)
XLA Ops:
  7.2 0.7 convert_element_type.34
  7.9 1.9 broadcast_multiply_fusion
  9.8 0.0 reduce-scatter.3.cloned.1.call-start
  9.9 73.7 %all-gather.5.cloned.1.call-done = bf16[640,3072]{1,0:T(8,128)(2,1)} async-done(((bf16[80,3072]{1,0:T(8,128)(2,1)}), bf16[640,3072]{1,0:T(8,128)(2,1)}) %all-gather.5.cloned.1.call-update) | async-done | bytes 3932176 | tf_op jit(solution)/shard_map/all_gather | solution.py:29
  83.6 18.2 %fusion.12 = f32[640,3072]{1,0:T(8,128)} fusion(bf16[640,3072]{1,0:T(8,128)(2,1)} %all-gather.5.cloned.1.call-done, bf16[3072,3072]{1,0:T(8,128)(2,1)} %param.13), kind=kOutput, calls=%fused_computation.26 | convolution fusion | flops 12079595520 | bytes 30670848 | tf_op jit(solution)/shard_map/dot_general | solution.py:34
  101.8 0.0 all-gather.7.cloned.1.call-start
  101.9 67.5 %reduce-scatter.3.cloned.1.call-done = f32[160,3072]{1,0:T(8,128)} async-done(((f32[640,3072]{1,0:T(8,128)}), f32[160,3072]{1,0:T(8,128)}) %reduce-scatter.3.cloned.1.call-update) | async-done | bytes 1966096 | tf_op jit(solution)/shard_map/reduce_scatter | solution.py:33
  169.3 4.2 fusion.8
  173.6 0.0 all-gather.9.cloned.1.call-start
  173.6 0.5 all-gather.9.cloned.1.call-update
  174.2 0.5 all-gather.11.cloned.1.call-update
  174.7 0.2 reduce-scatter.5.cloned.1.call-start
  175.0 31.8 %all-gather.7.cloned.1.call-done = bf16[640,3072]{1,0:T(8,128)(2,1)} async-done(((bf16[160,3072]{1,0:T(8,128)(2,1)}), bf16[640,3072]{1,0:T(8,128)(2,1)}) %all-gather.7.cloned.1.call-update) | async-done | bytes 3932176 | tf_op jit(solution)/shard_map/all_gather | solution.py:44
  206.7 18.2 %fusion.13 = f32[640,3072]{1,0:T(8,128)} fusion(bf16[640,3072]{1,0:T(8,128)(2,1)} %all-gather.7.cloned.1.call-done, bf16[3072,3072]{1,0:T(8,128)(2,1)} %param.12), kind=kOutput, calls=%fused_computation.27 | convolution fusion | flops 12079595520 | bytes 30670848 | tf_op jit(solution)/shard_map/dot_general | solution.py:55
  225.7 0.6 convert_reduce_fusion
  226.9 52.2 %all-gather.9.cloned.1.call-done = bf16[640,3072]{1,0:T(8,128)(2,1)} async-done(((bf16[80,3072]{1,0:T(8,128)(2,1)}), bf16[640,3072]{1,0:T(8,128)(2,1)}) %all-gather.9.cloned.1.call-update) | async-done | bytes 3932176 | tf_op jit(solution)/shard_map/all_gather | solution.py:28
  279.1 26.3 %multiply_reduce_fusion.1 = (f32[]{:T(128)}, f32[3072,3072]{1,0:T(8,128)}) fusion(bf16[640,3072]{1,0:T(8,128)(2,1)} %all-gather.7.cloned.1.call-done, bf16[640,3072]{1,0:T(8,128)(2,1)} %all-gather.9.cloned.1.call-done), kind=kOutput, calls=%fused_computation.3 | convolution fusion | flops 12098469888 | bytes 45613060 | tf_op jit(solution)/shard_map/dot_general | solution.py:50
  305.5 7.1 %all-gather.11.cloned.1.call-done = bf16[640,3072]{1,0:T(8,128)(2,1)} async-done(((bf16[160,3072]{1,0:T(8,128)(2,1)}), bf16[640,3072]{1,0:T(8,128)(2,1)}) %all-gather.11.cloned.1.call-update) | async-done | bytes 3932176 | tf_op jit(solution)/shard_map/all_gather | solution.py:43
  312.6 26.3 %multiply_reduce_fusion = (f32[]{:T(128)}, f32[3072,3072]{1,0:T(8,128)}) fusion(bf16[640,3072]{1,0:T(8,128)(2,1)} %all-gather.11.cloned.1.call-done, bf16[640,3072]{1,0:T(8,128)(2,1)} %all-gather.5.cloned.1.call-done), kind=kOutput, calls=%fused_computation.2 | convolution fusion | flops 12098469888 | bytes 45613060 | tf_op jit(solution)/shard_map/dot_general | solution.py:47
  340.2 42.6 %all-reduce = (f32[]{:T(128)}, f32[]{:T(128)}, f32[]{:T(128)}) all-reduce(f32[]{:T(128)S(6)} %mul.108, f32[]{:T(128)S(6)} %mul.112, f32[]{:T(128)} %bitcast), channel_id=1, replica_groups=mesh['row'=8,'col'=4] {'row','col'}, use_global_device_ids=true, to_apply=%region_3.0 | all-reduce | flops 3 | bytes 24 | tf_op jit(solution)/shard_map/psum | solution.py:65
  384.8 39.3 %multiply_convert_fusion = (bf16[3072,3072]{1,0:T(8,128)(2,1)}, bf16[3072,3072]{0,1:T(8,128)(2,1)}) fusion(f32[3072,3072]{1,0:T(8,128)} %get-tuple-element.14, f32[]{:T(128)S(6)} %mul.115, f32[]{:T(128)S(6)} %max.6, f32[3072,3072]{1,0:T(8,128)} %get-tuple-element.12), kind=kLoop, calls=%fused_computation | loop fusion | flops 56623104 | bytes 113246216 | tf_op jit(solution)/shard_map/convert_element_type | solution.py:78
  424.0 24.6 %copy.10 = bf16[3072,3072]{1,0:T(8,128)(2,1)} copy(bf16[3072,3072]{0,1:T(8,128)(2,1)} %get-tuple-element.16) | data formatting | bytes 37748736
  448.7 8.9 %reduce-scatter.5.cloned.1.call-done = f32[80,3072]{1,0:T(8,128)} async-done(((f32[640,3072]{1,0:T(8,128)}), f32[80,3072]{1,0:T(8,128)}) %reduce-scatter.5.cloned.1.call-update) | async-done | bytes 983056 | tf_op jit(solution)/shard_map/reduce_scatter | solution.py:54
  457.6 2.0 divide_convert_fusion
  (10 shorter events, 0.1 us)
Async XLA Ops:
  7.2 76.4 %all-gather.5.cloned.1.call-start = ((), (), s32[]{:S(2)}) async-start(), calls=%async_computation.2 | async-start | bytes 4423680 | tf_op jit(solution)/shard_map/all_gather | solution.py:29
  9.8 159.5 %reduce-scatter.3.cloned.1.call-start = ((), (), s32[]{:S(2)}) async-start(), calls=%async_computation.3 | async-start | bytes 9830400 | tf_op jit(solution)/shard_map/reduce_scatter | solution.py:33
  101.8 67.5 %copy-start = (bf16[160,3072]{1,0:T(8,128)(2,1)S(1)}, bf16[160,3072]{1,0:T(8,128)(2,1)}, u32[]{:S(2)}) copy-start(bf16[160,3072]{1,0:T(8,128)(2,1)} %param.8) | copy-start | bytes 2949124
  101.8 104.9 %all-gather.7.cloned.1.call-start = ((), (), s32[]{:S(2)}) async-start(), calls=%async_computation.4 | async-start | bytes 4915200 | tf_op jit(solution)/shard_map/all_gather | solution.py:44
  173.6 105.6 %all-gather.9.cloned.1.call-start = ((), (), s32[]{:S(2)}) async-start(), calls=%async_computation.6 | async-start | bytes 4423680 | tf_op jit(solution)/shard_map/all_gather | solution.py:28
  174.2 138.5 %all-gather.11.cloned.1.call-start = ((), (), s32[]{:S(2)}) async-start(), calls=%async_computation.7 | async-start | bytes 4915200 | tf_op jit(solution)/shard_map/all_gather | solution.py:43
  174.7 282.8 %reduce-scatter.5.cloned.1.call-start = ((), (), s32[]{:S(2)}) async-start(), calls=%async_computation.5 | async-start | bytes 8847360 | tf_op jit(solution)/shard_map/reduce_scatter | solution.py:54
  225.0 0.7 copy-start.1
Sparse Core Ops, SparseCore 0:
  10.8 72.7 all-gather.4
  101.9 67.3 reduce-scatter.2
  173.7 33.0 all-gather.6
  209.0 70.0 all-gather.8
  281.2 31.3 all-gather.10
  316.5 140.9 reduce-scatter.4
where the time goes:
time: 467 us; the launch traced here: 466 us
  waiting for transfers between devices  242 us (52%)
  matrix products  89 us (19%)
  other arithmetic  48.7 us (10%)
  blocking collectives  42.6 us (9%)
  local copies, waits for them, and re-layouts  24.6 us (5%)
  between operations  18.8 us (4%)
    all_gather x1, waiting for transfers between devices, on_device(): lax.all_gather(masked, 'row', axis=0, tiled=True)  73.7 us
    reduce_scatter x1, waiting for transfers between devices, on_device(): lax.psum_scatter(lax.dot_general(block, w_down, contract_last, preferred_...  67.5 us
    all_gather x1, waiting for transfers between devices, on_device(): lax.all_gather(inputs, 'row', axis=0, tiled=True)  52.2 us
    psum x1, blocking collectives, on_device(): lax.psum((count_term, square_term, flag_value), ('row', 'col'))  42.6 us
    convert_element_type x1, other arithmetic, on_device(): (down_sum / token_total * (keep_block * clip_factor)).astype(jnp.bfloat16)  39.3 us
    all_gather x1, waiting for transfers between devices, on_device(): lax.all_gather(hidden_grad, 'col', axis=0, tiled=True)  31.8 us
    dot_general x1, matrix products, on_device(): lax.dot_general(inputs_all, hidden_all, contract_first, preferred_element...  26.3 us
    dot_general x1, matrix products, on_device(): lax.dot_general(act_all, masked_all, contract_first, preferred_element_ty...  26.3 us
  transfers between devices with their start and end apart: 6, of which 6 were waited for; matrix products, arithmetic and copies ran while one was open for 29% of the time, Pallas kernels for 0%

commit v1 on v0

v1 whole, which is shorter than its diff:
```python
import math

import jax
import jax.numpy as jnp
import numpy as np
from jax import lax
from jax.sharding import PartitionSpec as P

F32 = jnp.float32
BF16 = jnp.bfloat16
LAST = (((1,), (1,)), ((), ()))
FIRST = (((0,), (0,)), ((), ()))
FACTOR = math.sqrt(2.0 / math.pi)


def gelu_value(hval):
    inner = FACTOR * (hval + 0.044715 * hval * hval * hval)
    return 0.5 * hval * (1.0 + jnp.tanh(inner))


def gelu_slope(hval):
    tanh_part = jnp.tanh(FACTOR * (hval + 0.044715 * hval * hval * hval))
    return 0.5 * (1.0 + tanh_part) + 0.5 * hval * (1.0 - tanh_part * tanh_part) * FACTOR * (
        1.0 + 3.0 * 0.044715 * hval * hval
    )


def line_plan(length):
    order = []
    for z in range(length):
        prefer = -1 if z % 2 else 1
        others = [s for s in range(length) if s != z]
        others.sort(key=lambda s: (abs(s - z), -prefer * (s - z)))
        order.append([z] + others)
    groups = {}
    for z in range(length):
        for slot in range(1, length):
            shard = order[z][slot]
            near = z - 1 if shard < z else z + 1
            from_slot = order[near].index(shard)
            side = 0
            while True:
                pairs = groups.setdefault((abs(shard - z), slot, from_slot, side), [])
                if all(near != source for source, _ in pairs):
                    pairs.append((near, z))
                    break
                side += 1
    hops = [(key[0], key[1], key[2], groups[key]) for key in sorted(groups)]
    return order, hops


def on_row(pairs):
    return [(2 * a + x, 2 * b + x) for a, b in pairs for x in range(2)]


def swap(value, axis, bit):
    size = lax.axis_size(axis)
    return lax.ppermute(value, axis, [(i, i ^ bit) for i in range(size)])


def member(z, nodes):
    return sum((z == node).astype(jnp.int32) for node in nodes) > 0


def line_gather(own, z, length, hops):
    slots = [own] + [None] * (length - 1)
    arrived = {(0, 0): own}
    for time, slot, from_slot, pairs in hops:
        got = lax.ppermute(arrived[(time - 1, from_slot)], "row", on_row(pairs))
        here = member(z, [b for _, b in pairs])
        for table, key in ((arrived, (time, slot)), (slots, slot)):
            before = table[key] if isinstance(table, list) else table.get(key)
            merged = got if before is None else jnp.where(here, got, before)
            table[key] = merged
    return slots


def line_reduce(parts, hops):
    sums = list(parts)
    for _, slot, from_slot, pairs in reversed(hops):
        got = lax.ppermute(
            sums[slot].astype(BF16), "row", on_row([(b, a) for a, b in pairs])
        )
        sums[from_slot] = sums[from_slot] + got.astype(F32)
    return sums[0]


def after(value, event):
    return lax.optimization_barrier((value, event))[0]


def on_device(inputs, pre_act, out_grad, token_valid, poison, w_up, w_down):
    n_row = lax.axis_size("row")
    n_col = lax.axis_size("col")
    rows = inputs.shape[0]
    length = n_row // 2
    order, hops = line_plan(length)
    row, col = lax.axis_index("row"), lax.axis_index("col")
    z, x, core = row // 2, row % 2, col % 2
    first_core = core == 0

    def split(mine, theirs):
        return jnp.where(first_core, mine, theirs), jnp.where(first_core, theirs, mine)

    def halves(mine, theirs):
        return jnp.concatenate(split(mine, theirs), axis=0)

    masked = out_grad * token_valid.astype(BF16)[:, None]
    masked_mine = line_gather(masked, z, length, hops)
    masked_theirs = [swap(part, "row", 1) for part in masked_mine]
    masked_slots = [halves(a, b) for a, b in zip(masked_mine, masked_theirs)]

    inputs_late = after(inputs, masked_mine[-1])
    inputs_mine = line_gather(inputs_late, z, length, hops)
    inputs_theirs = [swap(part, "row", 1) for part in inputs_mine]
    inputs_all = jnp.concatenate(
        [halves(a, b) for a, b in zip(inputs_mine, inputs_theirs)], axis=0
    )
    masked_all = jnp.concatenate(masked_slots, axis=0)

    bits = []
    bit = n_col // 2
    while bit:
        bits.append(bit)
        bit //= 2
    pieces = [pre_act]
    for bit in bits:
        pieces = pieces + [swap(piece, "col", bit) for piece in pieces]
    gathered = jnp.concatenate(pieces, axis=0)
    per_col = n_row // n_col
    table = jnp.asarray(np.array(order, np.int32))

    def hidden_rows(slot, half):
        which = 2 * table[z, slot] + (x ^ core ^ half)
        apart = (which // per_col) ^ col
        place = sum(((apart // bit) % 2) << i for i, bit in enumerate(bits))
        start = (place * per_col + which % per_col) * rows
        return lax.dynamic_slice_in_dim(gathered, start, rows, axis=0)

    pre_halves = [(hidden_rows(slot, 0), hidden_rows(slot, 1)) for slot in range(length)]
    act_all = gelu_value(
        jnp.concatenate([half for pair in pre_halves for half in pair], axis=0).astype(F32)
    ).astype(BF16)

    hidden_slots = []
    for slot in range(length):
        partial = lax.dot_general(
            masked_slots[slot], w_down, LAST, preferred_element_type=F32
        )
        other = swap(partial[rows:].astype(BF16), "col", 1)
        total = partial[:rows] + other.astype(F32)
        for bit in reversed(bits[:-1]):
            total = total + swap(total.astype(BF16), "col", bit).astype(F32)
        hidden = (total * gelu_slope(pre_halves[slot][0].astype(F32))).astype(BF16)
        hidden_slots.append(jnp.concatenate([hidden, swap(hidden, "col", 1)], axis=0))
    hidden_all = jnp.concatenate(hidden_slots, axis=0)

    sums = [None] * length
    for slot in reversed(range(length)):
        partial = lax.dot_general(
            hidden_slots[slot], w_up, LAST, preferred_element_type=F32
        )
        mine, theirs = split(partial[:rows], partial[rows:])
        sums[slot] = mine + swap(theirs.astype(BF16), "row", 1).astype(F32)
    input_sum = line_reduce(sums, hops)

    def gram(value):
        return lax.dot_general(value, value, LAST, preferred_element_type=F32)

    square_term = jnp.sum(gram(act_all) * gram(masked_all)) + jnp.sum(
        gram(hidden_all) * gram(inputs_all)
    )
    flag_value = poison[0, 0].astype(F32)
    keep_block = 1.0 - flag_value
    count_term = jnp.where(col == 0, jnp.sum(token_valid.astype(F32)), 0.0)
    scalars = jnp.stack([count_term, keep_block * square_term, flag_value])
    for axis, size in (("col", n_col), ("row", n_row)):
        bit = 1
        while bit < size:
            scalars = scalars + swap(scalars, axis, bit)
            bit *= 2
    count_all, square_all, flag_all = scalars[0], jnp.maximum(scalars[1], 0.0), scalars[2]

    token_total = jnp.maximum(count_all, 1.0)
    squares = square_all / (token_total * token_total)
    block_count = float(n_row * n_col)
    estimate = squares * block_count / jnp.maximum(block_count - flag_all, 1.0)
    total_tokens = rows * n_row
    model_width = w_up.shape[0] * n_col
    hidden_width = w_up.shape[1] * n_row
    limit = 0.25 * math.sqrt(hidden_width * model_width / total_tokens)
    clip_factor = jnp.minimum(1.0, limit / jnp.sqrt(estimate + 1e-06))
    scale = keep_block * clip_factor / token_total
    grad_up = lax.dot_general(inputs_all, hidden_all, FIRST, preferred_element_type=F32)
    grad_down = lax.dot_general(act_all, masked_all, FIRST, preferred_element_type=F32)
    return (
        (input_sum / token_total).astype(BF16),
        (grad_up * scale).astype(BF16),
        (grad_down * scale).astype(BF16),
    )


def solution(mesh):
    placed = (
        P("row", "col"),
        P("col", "row"),
        P("row", "col"),
        P("row"),
        P("row", "col"),
        P("col", "row"),
        P("row", "col"),
    )
    return jax.shard_map(
        on_device,
        mesh=mesh,
        in_specs=placed,
        out_specs=(P("row", "col"), P("col", "row"), P("row", "col")),
        check_vma=False,
    )
```

time: 467 us -> 388 us (0.83); the launches traced: 466 us -> 380 us
  waiting for transfers between devices: 242 us -> 62.3 us
  matrix products: 89 us -> 159 us
  starting transfers between devices: 0.42 us -> 57.7 us
  blocking collectives: 42.6 us -> 0 us
  other arithmetic: 48.7 us -> 59.6 us
  between operations: 18.8 us -> 9.12 us
  local copies, waits for them, and re-layouts: 24.6 us -> 33.1 us
    all_gather x4 -> x0, waiting for transfers between devices: 165 us -> none  [the longest x1 73.7 us: on_device(): lax.all_gather(masked, 'row', axis=0, tiled=True)]
    reduce_scatter x2 -> x0, waiting for transfers between devices: 76.4 us -> none  [the longest x1 67.5 us: on_device(): lax.psum_scatter(lax.dot_general(block, w_down, contract_last, preferred_...]
    dot_general x4 -> x14, matrix products: 89 us -> 159 us  [the longest x4 45.6 us: on_device(): lax.dot_general(hidden_slots[slot], w_up, LAST, preferred_element_type=F32)]
    ppermute x0 -> x47, waiting for transfers between devices: none -> 62.3 us  [the longest x32 36.9 us: swap(): return lax.ppermute(value, axis, [(i, i ^ bit) for i in range(size)])]
    ppermute x0 -> x47, starting transfers between devices: none -> 57.7 us  [the longest x32 22 us: swap(): return lax.ppermute(value, axis, [(i, i ^ bit) for i in range(size)])]
    psum x1 -> x0, blocking collectives: 42.6 us -> none  [on_device(): lax.psum((count_term, square_term, flag_value), ('row', 'col'))]
    unnamed x0 -> x18, other arithmetic: none -> 29.9 us
    convert_element_type x4 -> x15, other arithmetic: 46.2 us -> 21.9 us  [the longest x4 8.17 us: on_device(): total = total + swap(total.astype(BF16), 'col', bit).astype(F32)]
  transfers between devices with their start and end apart: 6 -> 47, of which waited for: 6 -> 12; matrix products, arithmetic and copies ran while one was open for 29% -> 63% of each run, Pallas kernels for 0% -> 0%
where the time goes in v1:
time: 388 us; the launch traced here: 380 us
  matrix products  159 us (41%)
  waiting for transfers between devices  62.3 us (16%)
  other arithmetic  59.6 us (15%)
  starting transfers between devices  57.7 us (15%)
  local copies, waits for them, and re-layouts  33.1 us (9%)
  between operations  9.12 us (2%)
    dot_general x4, matrix products, on_device(): lax.dot_general(hidden_slots[slot], w_up, LAST, preferred_element_type=F32)  45.6 us
    dot_general x4, matrix products, on_device(): lax.dot_general(masked_slots[slot], w_down, LAST, preferred_element_type=...  45.2 us
    ppermute x32, waiting for transfers between devices, swap(): return lax.ppermute(value, axis, [(i, i ^ bit) for i in range(size)])  36.9 us
    unnamed x18, other arithmetic  29.9 us
    dot_general x4, matrix products, gram(): return lax.dot_general(value, value, LAST, preferred_element_type=F32)  28.2 us
    ppermute x10, waiting for transfers between devices, line_gather(): got = lax.ppermute(arrived[time - 1, from_slot], 'row', on_row(pairs))  25.4 us
    unnamed x61, local copies, waits for them, and re-layouts  24 us
    ppermute x32, starting transfers between devices, swap(): return lax.ppermute(value, axis, [(i, i ^ bit) for i in range(size)])  22 us
  transfers between devices with their start and end apart: 47, of which 12 were waited for; matrix products, arithmetic and copies ran while one was open for 63% of the time, Pallas kernels for 0%

profile of v1, /device:TPU:0, one launch (start us, length us, event | category | flops | bytes accessed | tf_op | source)
XLA Modules:
  0.0 380.4 jit_solution(7630767206811292222)
XLA Ops:
  23.5 10.2 %fusion.41 = f32[160,3072]{1,0:T(8,128)S(1)} fusion(bf16[3072,3072]{1,0:T(8,128)(2,1)} %param.14, bf16[80,3072]{1,0:T(8,128)(2,1)S(1)} %get-tuple-element.26, bf16[80,3072]{1,0:T(8,128)(2,1)S(1)} %get-tuple-element.28), kind=kOutput, calls=%fused_computation.86 | convolution fusion | flops 3021864960 | bytes 21823488 | tf_op jit(solution)/shard_map/dot_general | solution.py:147
  38.9 11.4 %collective-permute-done.18 = bf16[80,3072]{1,0:T(8,128)(2,1)S(1)} collective-permute-done((bf16[80,3072]{1,0:T(8,128)(2,1)S(1)}, bf16[80,3072]{1,0:T(8,128)(2,1)S(1)}, u32[]{:S(2)}, u32[]{:S(2)}) %collective-permute-start.18) | collective-permute-done | bytes 491552 | tf_op jit(solution)/shard_map/ppermute | solution.py:58
  53.1 10.4 %fusion.57 = f32[160,3072]{1,0:T(8,128)S(1)} fusion(bf16[3072,3072]{1,0:T(8,128)(2,1)} %param.14, bf16[80,3072]{1,0:T(8,128)(2,1)} %get-tuple-element.22, bf16[80,3072]{1,0:T(8,128)(2,1)} %get-tuple-element.24), kind=kOutput, calls=%fused_computation.102 | convolution fusion | flops 3021864960 | bytes 21823488 | tf_op jit(solution)/shard_map/dot_general | solution.py:147
  73.7 13.1 %collective-permute-done.24 = bf16[80,3072]{1,0:T(8,128)(2,1)S(1)} collective-permute-done((bf16[80,3072]{1,0:T(8,128)(2,1)}, bf16[80,3072]{1,0:T(8,128)(2,1)S(1)}, u32[]{:S(2)}, u32[]{:S(2)}) %collective-permute-start.24) | collective-permute-done | bytes 491552 | tf_op jit(solution)/shard_map/ppermute | solution.py:69
  92.5 14.4 %fusion.49 = f32[160,3072]{1,0:T(8,128)} fusion(bf16[3072,3072]{1,0:T(8,128)(2,1)} %param.14, bf16[80,3072]{1,0:T(8,128)(2,1)} %get-tuple-element.18, bf16[80,3072]{1,0:T(8,128)(2,1)} %get-tuple-element.20), kind=kOutput, calls=%fused_computation.94 | convolution fusion | flops 3021864960 | bytes 21823488 | tf_op jit(solution)/shard_map/dot_general | solution.py:147
  111.6 9.6 %collective-permute-done.25 = bf16[80,3072]{1,0:T(8,128)(2,1)S(1)} collective-permute-done((bf16[80,3072]{1,0:T(8,128)(2,1)S(1)}, bf16[80,3072]{1,0:T(8,128)(2,1)S(1)}, u32[]{:S(2)}, u32[]{:S(2)}) %collective-permute-start.25) | collective-permute-done | bytes 491552 | tf_op jit(solution)/shard_map/ppermute | solution.py:58
  123.9 7.8 %fusion.97 = f32[640,640]{1,0:T(8,128)} fusion(bf16[640,3072]{1,0:T(8,128)(2,1)} %get-tuple-element.13), kind=kOutput, calls=%fused_computation.199 | convolution fusion | flops 2516582400 | bytes 5570560 | tf_op jit(solution)/shard_map/dot_general | solution.py:168
  139.0 10.2 %fusion.65 = f32[160,3072]{1,0:T(8,128)S(1)} fusion(bf16[3072,3072]{1,0:T(8,128)(2,1)} %param.14, bf16[80,3072]{1,0:T(8,128)(2,1)S(1)} %get-tuple-element.14, bf16[80,3072]{1,0:T(8,128)(2,1)S(1)} %get-tuple-element.16), kind=kOutput, calls=%fused_computation.110 | convolution fusion | flops 3021864960 | bytes 21823488 | tf_op jit(solution)/shard_map/dot_general | solution.py:147
  155.7 3.5 constant_dynamic-update-slice_fusion.19
  169.8 10.2 %fusion.45 = f32[160,3072]{1,0:T(8,128)S(1)} fusion(bf16[3072,3072]{1,0:T(8,128)(2,1)} %param.13, bf16[80,3072]{1,0:T(8,128)(2,1)S(1)} %collective-permute-done.6, bf16[80,3072]{1,0:T(8,128)(2,1)S(1)} %get-tuple-element.12), kind=kOutput, calls=%fused_computation.90 | convolution fusion | flops 3021864960 | bytes 21823488 | tf_op jit(solution)/shard_map/dot_general | solution.py:160
  200.6 9.5 %collective-permute-done.40 = bf16[80,3072]{1,0:T(8,128)(2,1)S(1)} collective-permute-done((bf16[80,3072]{1,0:T(8,128)(2,1)}, bf16[80,3072]{1,0:T(8,128)(2,1)S(1)}, u32[]{:S(2)}, u32[]{:S(2)}) %collective-permute-start.40) | collective-permute-done | bytes 491552 | tf_op jit(solution)/shard_map/ppermute | solution.py:69
  216.1 10.3 %fusion.61 = f32[160,3072]{1,0:T(8,128)S(1)} fusion(bf16[3072,3072]{1,0:T(8,128)(2,1)} %param.13, bf16[80,3072]{1,0:T(8,128)(2,1)} %copy-done.13, bf16[80,3072]{1,0:T(8,128)(2,1)S(1)} %get-tuple-element.10), kind=kOutput, calls=%fused_computation.106 | convolution fusion | flops 3021864960 | bytes 21823488 | tf_op jit(solution)/shard_map/dot_general | solution.py:160
  232.9 3.3 constant_dynamic-update-slice_fusion.13
  236.5 10.6 %fusion.53 = f32[160,3072]{1,0:T(8,128)S(1)} fusion(bf16[3072,3072]{1,0:T(8,128)(2,1)} %param.13, bf16[80,3072]{1,0:T(8,128)(2,1)} %collective-permute-done.13, bf16[80,3072]{1,0:T(8,128)(2,1)} %get-tuple-element.8), kind=kOutput, calls=%fused_computation.98 | convolution fusion | flops 3021864960 | bytes 21823488 | tf_op jit(solution)/shard_map/dot_general | solution.py:160
  249.0 10.6 %multiply_reduce_fusion.1 = f32[]{:T(128)} fusion(f32[640,640]{1,0:T(8,128)} %fusion.97, bf16[640,3072]{1,0:T(8,128)(2,1)} %get-tuple-element.29), kind=kOutput, calls=%fused_computation.41 | convolution fusion | flops 2537062400 | bytes 5570564 | tf_op jit(solution)/shard_map/dot_general | solution.py:168
  262.8 4.4 %fusion.98 = f32[640,640]{1,0:T(8,128)} fusion(bf16[640,3072]{1,0:T(8,128)(2,1)S(1)} %select_dynamic-update-slice_fusion), kind=kOutput, calls=%fused_computation.200 | convolution fusion | flops 2516582400 | bytes 5570560 | tf_op jit(solution)/shard_map/dot_general | solution.py:168
  267.2 14.6 %fusion.69 = f32[160,3072]{1,0:T(8,128)} fusion(bf16[3072,3072]{1,0:T(8,128)(2,1)} %param.13, bf16[80,3072]{1,0:T(8,128)(2,1)S(1)} %collective-permute-done.28, bf16[80,3072]{1,0:T(8,128)(2,1)} %get-tuple-element.6), kind=kOutput, calls=%fused_computation.114 | convolution fusion | flops 3021864960 | bytes 21823488 | tf_op jit(solution)/shard_map/dot_general | solution.py:160
  286.2 3.4 collective-permute-start.15
  291.6 5.4 %multiply_reduce_fusion = f32[]{:T(128)} fusion(f32[640,640]{1,0:T(8,128)} %fusion.98, bf16[640,3072]{1,0:T(8,128)(2,1)S(1)} %constant_dynamic-update-slice_fusion.12), kind=kOutput, calls=%fused_computation.40 | convolution fusion | flops 2517401600 | bytes 5570564 | tf_op jit(solution)/shard_map/dot_general | solution.py:168
  306.6 3.5 collective-permute-done.45
  310.7 3.9 %collective-permute-done.46 = f32[3]{0:T(128)S(1)} collective-permute-done((f32[3]{0:T(128)S(1)}, f32[3]{0:T(128)S(1)}, u32[]{:S(2)}, u32[]{:S(2)}) %collective-permute-start.46) | collective-permute-done | bytes 44 | tf_op jit(solution)/shard_map/ppermute | solution.py:58
  321.1 21.5 %multiply_convert_fusion = bf16[3072,3072]{1,0:T(8,128)(2,1)} fusion(f32[]{:T(128)S(6)} %div.202, bf16[640,3072]{1,0:T(8,128)(2,1)} %get-tuple-element.13, bf16[640,3072]{1,0:T(8,128)(2,1)} %get-tuple-element.29), kind=kOutput, calls=%fused_computation | convolution fusion | flops 12118130688 | bytes 26738692 | tf_op jit(solution)/shard_map/dot_general | solution.py:195
  347.5 12.4 %collective-permute-start.32 = (bf16[80,3072]{1,0:T(8,128)(2,1)S(1)}, bf16[80,3072]{1,0:T(8,128)(2,1)S(1)}, u32[]{:S(2)}, u32[]{:S(2)}) collective-permute-start(bf16[80,3072]{1,0:T(8,128)(2,1)S(1)} %add_convert_fusion), channel_id=1, source_target_pairs={{0,8},{4,12},{8,0},{12,4},{16,24},{20,28},{24,16},{28,20},{1,9},{5... | collective-permute-start | bytes 1474568 | tf_op jit(solution)/shard_map/ppermute | solution.py:81
  360.0 18.1 %multiply_convert_fusion.1 = bf16[3072,3072]{1,0:T(8,128)(2,1)} fusion(f32[]{:T(128)S(6)} %div.202, bf16[640,3072]{1,0:T(8,128)(2,1)S(1)} %copy-done.24, bf16[640,3072]{1,0:T(8,128)(2,1)S(1)} %copy-done.21), kind=kOutput, calls=%fused_computation.1 | convolution fusion | flops 12098469888 | bytes 26738692 | tf_op jit(solution)/shard_map/dot_general | solution.py:194
  (200 shorter events, 139.0 us)
Async XLA Ops:
  3.3 32.0 %collective-permute-start.17 = (bf16[80,3072]{1,0:T(8,128)(2,1)}, bf16[80,3072]{1,0:T(8,128)(2,1)S(1)}, u32[]{:S(2)}, u32[]{:S(2)}) collective-permute-start(bf16[80,3072]{1,0:T(8,128)(2,1)} %broadcast_multiply_fusion), channel_id=1, source_target_pairs={{8,0},{12,4},{0,8},{4,12},{24,16},{28,20},{16,24},{20,28},{9,1},{1... | collective-permute-start | bytes 1474568 | tf_op jit(solution)/shard_map/ppermute | solution.py:69
  9.3 58.5 %collective-permute-start.3 = (bf16[160,3072]{1,0:T(8,128)(2,1)}, bf16[160,3072]{1,0:T(8,128)(2,1)}, u32[]{:S(2)}, u32[]{:S(2)}) collective-permute-start(bf16[160,3072]{1,0:T(8,128)(2,1)} %param.9), channel_id=1, source_target_pairs={{0,2},{1,3},{2,0},{3,1},{4,6},{5,7},{6,4},{7,5},{8,10},{9,11},{10,... | collective-permute-start | bytes 2949128 | tf_op jit(solution)/shard_map/ppermute | solution.py:58
  10.8 60.4 %collective-permute-start.4 = (bf16[160,3072]{1,0:T(8,128)(2,1)}, bf16[160,3072]{1,0:T(8,128)(2,1)}, u32[]{:S(2)}, u32[]{:S(2)}) collective-permute-start(bf16[160,3072]{1,0:T(8,128)(2,1)} %param.9), channel_id=1, source_target_pairs={{0,1},{1,0},{2,3},{3,2},{4,5},{5,4},{6,7},{7,6},{8,9},{9,8},{10,11... | collective-permute-start | bytes 2949128 | tf_op jit(solution)/shard_map/ppermute | solution.py:58
  35.2 31.4 %collective-permute-start.23 = (bf16[80,3072]{1,0:T(8,128)(2,1)S(1)}, bf16[80,3072]{1,0:T(8,128)(2,1)}, u32[]{:S(2)}, u32[]{:S(2)}) collective-permute-start(bf16[80,3072]{1,0:T(8,128)(2,1)S(1)} %collective-permute-done.17), channel_id=1, source_target_pairs={{16,8},{20,12},{8,16},{12,20},{17,9},{21,13},{9,17},{13,21},{18,10... | collective-permute-start | bytes 1474568 | tf_op jit(solution)/shard_map/ppermute | solution.py:69
  50.4 38.5 %collective-permute-start.10 = (bf16[80,3072]{1,0:T(8,128)(2,1)S(1)}, bf16[80,3072]{1,0:T(8,128)(2,1)S(1)}, u32[]{:S(2)}, u32[]{:S(2)}) collective-permute-start(bf16[80,3072]{1,0:T(8,128)(2,1)S(1)} %broadcast_select_fusion.3), channel_id=1, source_target_pairs={{0,4},{4,0},{8,12},{12,8},{16,20},{20,16},{24,28},{28,24},{1,5},{5... | collective-permute-start | bytes 1474568 | tf_op jit(solution)/shard_map/ppermute | solution.py:58
  64.4 44.6 %collective-permute-start.19 = (bf16[80,3072]{1,0:T(8,128)(2,1)}, bf16[80,3072]{1,0:T(8,128)(2,1)}, u32[]{:S(2)}, u32[]{:S(2)}) collective-permute-start(bf16[80,3072]{1,0:T(8,128)(2,1)} %slice.153), channel_id=1, source_target_pairs={{0,1},{1,0},{2,3},{3,2},{4,5},{5,4},{6,7},{7,6},{8,9},{9,8},{10,11... | collective-permute-start | bytes 1474568 | tf_op jit(solution)/shard_map/ppermute | solution.py:58
  66.6 87.5 %collective-permute-start.2 = (bf16[80,3072]{1,0:T(8,128)(2,1)}, bf16[80,3072]{1,0:T(8,128)(2,1)}, u32[]{:S(2)}, u32[]{:S(2)}) collective-permute-start(bf16[80,3072]{1,0:T(8,128)(2,1)} %fusion.73), channel_id=1, source_target_pairs={{0,2},{1,3},{2,0},{3,1},{4,6},{5,7},{6,4},{7,5},{8,10},{9,11},{10,... | collective-permute-start | bytes 1474568 | tf_op jit(solution)/shard_map/ppermute | solution.py:58
  71.2 60.4 %collective-permute-start.5 = (bf16[160,3072]{1,0:T(8,128)(2,1)}, bf16[160,3072]{1,0:T(8,128)(2,1)}, u32[]{:S(2)}, u32[]{:S(2)}) collective-permute-start(bf16[160,3072]{1,0:T(8,128)(2,1)} %collective-permute-done.3), channel_id=1, source_target_pairs={{0,1},{1,0},{2,3},{3,2},{4,5},{5,4},{6,7},{7,6},{8,9},{9,8},{10,11... | collective-permute-start | bytes 2949128 | tf_op jit(solution)/shard_map/ppermute | solution.py:58
  86.8 79.5 %collective-permute-start.36 = (bf16[80,3072]{1,0:T(8,128)(2,1)}, bf16[80,3072]{1,0:T(8,128)(2,1)}, u32[]{:S(2)}, u32[]{:S(2)}) collective-permute-start(bf16[80,3072]{1,0:T(8,128)(2,1)} %param.8), channel_id=1, source_target_pairs={{16,8},{20,12},{8,16},{12,20},{17,9},{21,13},{9,17},{13,21},{18,10... | collective-permute-start | bytes 1474568 | tf_op jit(solution)/shard_map/ppermute | solution.py:69
  88.8 78.0 %collective-permute-start.34 = (bf16[80,3072]{1,0:T(8,128)(2,1)}, bf16[80,3072]{1,0:T(8,128)(2,1)}, u32[]{:S(2)}, u32[]{:S(2)}) collective-permute-start(bf16[80,3072]{1,0:T(8,128)(2,1)} %param.8), channel_id=1, source_target_pairs={{8,0},{12,4},{0,8},{4,12},{24,16},{28,20},{16,24},{20,28},{9,1},{1... | collective-permute-start | bytes 1474568 | tf_op jit(solution)/shard_map/ppermute | solution.py:69
  121.3 37.9 %collective-permute-start.33 = (bf16[80,3072]{1,0:T(8,128)(2,1)}, bf16[80,3072]{1,0:T(8,128)(2,1)}, u32[]{:S(2)}, u32[]{:S(2)}) collective-permute-start(bf16[80,3072]{1,0:T(8,128)(2,1)} %param.8), channel_id=1, source_target_pairs={{0,4},{4,0},{8,12},{12,8},{16,20},{20,16},{24,28},{28,24},{1,5},{5... | collective-permute-start | bytes 1474568 | tf_op jit(solution)/shard_map/ppermute | solution.py:58
  154.2 34.0 %collective-permute-start.20 = (bf16[80,3072]{1,0:T(8,128)(2,1)}, bf16[80,3072]{1,0:T(8,128)(2,1)}, u32[]{:S(2)}, u32[]{:S(2)}) collective-permute-start(bf16[80,3072]{1,0:T(8,128)(2,1)} %fusion.75), channel_id=1, source_target_pairs={{0,2},{1,3},{2,0},{3,1},{4,6},{5,7},{6,4},{7,5},{8,10},{9,11},{10,... | collective-permute-start | bytes 1474568 | tf_op jit(solution)/shard_map/ppermute | solution.py:58
  166.3 46.8 %collective-permute-start.12 = (bf16[80,3072]{1,0:T(8,128)(2,1)}, bf16[80,3072]{1,0:T(8,128)(2,1)}, u32[]{:S(2)}, u32[]{:S(2)}) collective-permute-start(bf16[80,3072]{1,0:T(8,128)(2,1)} %fusion.74), channel_id=1, source_target_pairs={{0,2},{1,3},{2,0},{3,1},{4,6},{5,7},{6,4},{7,5},{8,10},{9,11},{10,... | collective-permute-start | bytes 1474568 | tf_op jit(solution)/shard_map/ppermute | solution.py:58
  184.5 42.8 %collective-permute-start.38 = (bf16[80,3072]{1,0:T(8,128)(2,1)S(1)}, bf16[80,3072]{1,0:T(8,128)(2,1)}, u32[]{:S(2)}, u32[]{:S(2)}) collective-permute-start(bf16[80,3072]{1,0:T(8,128)(2,1)S(1)} %broadcast_select_fusion.1), channel_id=1, source_target_pairs={{0,4},{4,0},{8,12},{12,8},{16,20},{20,16},{24,28},{28,24},{1,5},{5... | collective-permute-start | bytes 1474568 | tf_op jit(solution)/shard_map/ppermute | solution.py:58
  188.2 44.7 %collective-permute-start.27 = (bf16[80,3072]{1,0:T(8,128)(2,1)}, bf16[80,3072]{1,0:T(8,128)(2,1)}, u32[]{:S(2)}, u32[]{:S(2)}) collective-permute-start(bf16[80,3072]{1,0:T(8,128)(2,1)} %fusion.76), channel_id=1, source_target_pairs={{0,2},{1,3},{2,0},{3,1},{4,6},{5,7},{6,4},{7,5},{8,10},{9,11},{10,... | collective-permute-start | bytes 1474568 | tf_op jit(solution)/shard_map/ppermute | solution.py:58
  210.2 167.9 %collective-permute-start.7 = (bf16[80,3072]{1,0:T(8,128)(2,1)}, bf16[80,3072]{1,0:T(8,128)(2,1)}, u32[]{:S(2)}, u32[]{:S(2)}) collective-permute-start(bf16[80,3072]{1,0:T(8,128)(2,1)} %select_convert_fusion.3), channel_id=1, source_target_pairs={{0,4},{4,0},{8,12},{12,8},{16,20},{20,16},{24,28},{28,24},{1,5},{5... | collective-permute-start | bytes 1474568 | tf_op jit(solution)/shard_map/ppermute | solution.py:58
  211.2 48.4 %collective-permute-start.41 = (bf16[80,3072]{1,0:T(8,128)(2,1)S(1)}, bf16[80,3072]{1,0:T(8,128)(2,1)}, u32[]{:S(2)}, u32[]{:S(2)}) collective-permute-start(bf16[80,3072]{1,0:T(8,128)(2,1)S(1)} %broadcast_select_fusion), channel_id=1, source_target_pairs={{0,4},{4,0},{8,12},{12,8},{16,20},{20,16},{24,28},{28,24},{1,5},{5... | collective-permute-start | bytes 1474568 | tf_op jit(solution)/shard_map/ppermute | solution.py:58
  227.3 119.0 %collective-permute-start.22 = (bf16[80,3072]{1,0:T(8,128)(2,1)}, bf16[80,3072]{1,0:T(8,128)(2,1)}, u32[]{:S(2)}, u32[]{:S(2)}) collective-permute-start(bf16[80,3072]{1,0:T(8,128)(2,1)} %select_convert_fusion.1), channel_id=1, source_target_pairs={{0,4},{4,0},{8,12},{12,8},{16,20},{20,16},{24,28},{28,24},{1,5},{5... | collective-permute-start | bytes 1474568 | tf_op jit(solution)/shard_map/ppermute | solution.py:58
  236.2 31.0 %collective-permute-start.28 = (bf16[80,3072]{1,0:T(8,128)(2,1)}, bf16[80,3072]{1,0:T(8,128)(2,1)S(1)}, u32[]{:S(2)}, u32[]{:S(2)}) collective-permute-start(bf16[80,3072]{1,0:T(8,128)(2,1)} %get-tuple-element.6), channel_id=1, source_target_pairs={{0,1},{1,0},{2,3},{3,2},{4,5},{5,4},{6,7},{7,6},{8,9},{9,8},{10,11... | collective-permute-start | bytes 1474568 | tf_op jit(solution)/shard_map/ppermute | solution.py:58
  248.0 37.3 %collective-permute-start.14 = (bf16[80,3072]{1,0:T(8,128)(2,1)}, bf16[80,3072]{1,0:T(8,128)(2,1)S(1)}, u32[]{:S(2)}, u32[]{:S(2)}) collective-permute-start(bf16[80,3072]{1,0:T(8,128)(2,1)} %select_convert_fusion.2), channel_id=1, source_target_pairs={{0,4},{4,0},{8,12},{12,8},{16,20},{20,16},{24,28},{28,24},{1,5},{5... | collective-permute-start | bytes 1474568 | tf_op jit(solution)/shard_map/ppermute | solution.py:58
  284.3 33.1 %collective-permute-start.29 = (bf16[80,3072]{1,0:T(8,128)(2,1)}, bf16[80,3072]{1,0:T(8,128)(2,1)S(1)}, u32[]{:S(2)}, u32[]{:S(2)}) collective-permute-start(bf16[80,3072]{1,0:T(8,128)(2,1)} %select_convert_fusion), channel_id=1, source_target_pairs={{0,4},{4,0},{8,12},{12,8},{16,20},{20,16},{24,28},{28,24},{1,5},{5... | collective-permute-start | bytes 1474568 | tf_op jit(solution)/shard_map/ppermute | solution.py:58
  286.2 57.5 %collective-permute-start.15 = (bf16[80,3072]{1,0:T(8,128)(2,1)}, bf16[80,3072]{1,0:T(8,128)(2,1)}, u32[]{:S(2)}, u32[]{:S(2)}) collective-permute-start(bf16[80,3072]{1,0:T(8,128)(2,1)} %fusion.77), channel_id=1, source_target_pairs={{0,8},{4,12},{24,16},{28,20},{1,9},{5,13},{25,17},{29,21},{2,10},{... | collective-permute-start | bytes 1474568 | tf_op jit(solution)/shard_map/ppermute | solution.py:81
  345.4 32.6 %collective-permute-start.16 = (bf16[80,3072]{1,0:T(8,128)(2,1)S(1)}, bf16[80,3072]{1,0:T(8,128)(2,1)S(1)}, u32[]{:S(2)}, u32[]{:S(2)}) collective-permute-start(bf16[80,3072]{1,0:T(8,128)(2,1)S(1)} %add_convert_fusion.2), channel_id=1, source_target_pairs={{8,16},{12,20},{16,8},{20,12},{9,17},{13,21},{17,9},{21,13},{10,18... | collective-permute-start | bytes 1474568 | tf_op jit(solution)/shard_map/ppermute | solution.py:81
  347.5 30.5 %collective-permute-start.32 = (bf16[80,3072]{1,0:T(8,128)(2,1)S(1)}, bf16[80,3072]{1,0:T(8,128)(2,1)S(1)}, u32[]{:S(2)}, u32[]{:S(2)}) collective-permute-start(bf16[80,3072]{1,0:T(8,128)(2,1)S(1)} %add_convert_fusion), channel_id=1, source_target_pairs={{0,8},{4,12},{8,0},{12,4},{16,24},{20,28},{24,16},{28,20},{1,9},{5... | collective-permute-start | bytes 1474568 | tf_op jit(solution)/shard_map/ppermute | solution.py:81
  (48 other events, 643.6 us)

commit v2 on v0

v2 whole, which is shorter than its diff:
```python
import functools
import math

import jax
import jax.numpy as jnp
from jax import lax
from jax.experimental import pallas as pl
from jax.experimental.pallas import tpu as pltpu
from jax.sharding import PartitionSpec as P

F32 = jnp.float32
BF16 = jnp.bfloat16
LAST = (((1,), (1,)), ((), ()))
FIRST = (((0,), (0,)), ((), ()))
FACTOR = math.sqrt(2.0 / math.pi)
TILE = 256
VMEM_LIMIT = 56 * 1024 * 1024


def swap(value, axis, bit):
    size = lax.axis_size(axis)
    return lax.ppermute(value, axis, [(i, i ^ bit) for i in range(size)])


def call(kernel, grid, in_specs, out_specs, out_shape, scratch, cost):
    flops, moved, slow = cost
    return pl.pallas_call(
        kernel,
        grid_spec=pltpu.PrefetchScalarGridSpec(
            num_scalar_prefetch=1,
            grid=grid,
            in_specs=in_specs,
            out_specs=out_specs,
            scratch_shapes=scratch,
        ),
        out_shape=out_shape,
        compiler_params=pltpu.CompilerParams(
            dimension_semantics=("arbitrary",), vmem_limit_bytes=VMEM_LIMIT
        ),
        cost_estimate=pl.CostEstimate(
            flops=flops, bytes_accessed=moved, transcendentals=slow
        ),
    )


class Rows:
    def __init__(self, arrays, places, length, rows, by_core=False):
        self.arrays, self.places = arrays, places
        self.length, self.rows, self.by_core = length, rows, by_core

    def specs(self, width, index):
        return [pl.BlockSpec((a.shape[0], width), index) for a in self.arrays]

    def fill(self, target, refs, core):
        for ref, (half, first, count) in zip(refs, self.places):
            base = (half ^ core if self.by_core else half) * (self.length * self.rows)
            for node in range(self.length):
                start = base + node * self.rows + first
                if self.by_core:
                    start = pl.multiple_of(start, 16)
                target[pl.ds(start, count), :] = ref[node * count : (node + 1) * count, :]


def whole_index(i, flags):
    return (0, 0)


def column_index(i, flags):
    return (0, i)


def gelu_all(pieces, offsets, flags, per_col, length, rows):
    width = pieces[0].shape[1]
    tile = 2 * TILE
    tokens = 2 * length * rows

    def kernel(flags_ref, *refs):
        ins, (act_ref, slope_ref) = refs[: len(pieces)], refs[len(pieces) :]
        x, core, col = flags_ref[0], flags_ref[1], flags_ref[2]
        for ref, offset in zip(ins, offsets):
            for part in range(per_col):
                row = (col ^ offset) * per_col + part
                node, half = row // 2, (row % 2) ^ x
                hval = ref[part * rows : (part + 1) * rows, :].astype(F32)
                tanh_part = jnp.tanh(FACTOR * (hval + 0.044715 * hval * hval * hval))
                start = pl.multiple_of((half * length + node) * rows, 16)
                act_ref[pl.ds(start, rows), :] = (0.5 * hval * (1.0 + tanh_part)).astype(BF16)

                @pl.when(half == core)
                def _():
                    slope_ref[pl.ds(pl.multiple_of(node * rows, 16), rows), :] = 0.5 * (
                        1.0 + tanh_part
                    ) + 0.5 * hval * (1.0 - tanh_part * tanh_part) * FACTOR * (
                        1.0 + 3.0 * 0.044715 * hval * hval
                    )

    return call(
        kernel,
        (width // tile,),
        [pl.BlockSpec((p.shape[0], tile), column_index) for p in pieces],
        [
            pl.BlockSpec((tokens, tile), column_index),
            pl.BlockSpec((tokens // 2, tile), column_index),
        ],
        [
            jax.ShapeDtypeStruct((tokens, width), BF16),
            jax.ShapeDtypeStruct((tokens // 2, width), F32),
        ],
        [],
        (30 * tokens * width, 6 * tokens * width, tokens * width),
    )(flags, *pieces)


def act_grad_part(mine, theirs, w_down, flags):
    count, depth = mine.shape
    width = w_down.shape[0]

    def kernel(flags_ref, mine_ref, theirs_ref, w_ref, keep_ref, send_ref, both):
        @pl.when(pl.program_id(0) == 0)
        def _():
            core = flags_ref[1]
            both[pl.ds(pl.multiple_of(core * count, 16), count), :] = mine_ref[...]
            both[pl.ds(pl.multiple_of((1 - core) * count, 16), count), :] = theirs_ref[...]

        product = lax.dot_general(both[...], w_ref[...], LAST, preferred_element_type=F32)
        keep_ref[...] = product[:count]
        send_ref[...] = product[count:].astype(BF16)

    return call(
        kernel,
        (width // TILE,),
        [
            pl.BlockSpec((count, depth), whole_index),
            pl.BlockSpec((count, depth), whole_index),
            pl.BlockSpec((TILE, depth), lambda i, flags: (i, 0)),
        ],
        [pl.BlockSpec((count, TILE), column_index)] * 2,
        [
            jax.ShapeDtypeStruct((count, width), F32),
            jax.ShapeDtypeStruct((count, width), BF16),
        ],
        [pltpu.VMEM((2 * count, depth), BF16)],
        (4 * count * depth * width, 2 * depth * width + 10 * count * width, 0),
    )(flags, mine, theirs, w_down)


def input_part(hidden, w_up, first, width, flags):
    depth = w_up.shape[1]
    half = hidden.length * hidden.rows
    n = len(hidden.arrays)

    def kernel(flags_ref, *refs):
        w_ref, mine_ref, theirs_ref, both = refs[n:]

        @pl.when(pl.program_id(0) == 0)
        def _():
            hidden.fill(both, refs[:n], flags_ref[1])

        product = lax.dot_general(both[...], w_ref[...], LAST, preferred_element_type=F32)
        mine_ref[...] = product[:half]
        theirs_ref[...] = product[half:].astype(BF16)

    return call(
        kernel,
        (width // TILE,),
        hidden.specs(depth, whole_index)
        + [pl.BlockSpec((TILE, depth), lambda i, flags: (first // TILE + i, 0))],
        [pl.BlockSpec((half, TILE), column_index)] * 2,
        [
            jax.ShapeDtypeStruct((half, width), F32),
            jax.ShapeDtypeStruct((half, width), BF16),
        ],
        [pltpu.VMEM((2 * half, depth), BF16)],
        (4 * half * depth * width, 2 * depth * width + 4 * half * (depth + 2 * width), 0),
    )(flags, *hidden.arrays, w_up)


def gram_inner(left, right, flags):
    width = left.arrays[0].shape[1]
    tile = 2 * TILE if width % (2 * TILE) == 0 else TILE
    tokens = 2 * left.length * left.rows
    n, m = len(left.arrays), len(right.arrays)
    steps = width // tile

    def kernel(flags_ref, *refs):
        out_ref, left_all, right_all, left_gram, right_gram = refs[n + m :]
        step, core = pl.program_id(0), flags_ref[1]
        left.fill(left_all, refs[:n], core)
        right.fill(right_all, refs[n : n + m], core)

        @pl.when(step == 0)
        def _():
            left_gram[...] = jnp.zeros_like(left_gram)
            right_gram[...] = jnp.zeros_like(right_gram)

        for rows, total in ((left_all, left_gram), (right_all, right_gram)):
            total[...] += lax.dot_general(
                rows[...], rows[...], LAST, preferred_element_type=F32
            )

        @pl.when(step == steps - 1)
        def _():
            out_ref[...] = jnp.sum(left_gram[...] * right_gram[...], axis=0, keepdims=True)

    gram = pltpu.VMEM((tokens, tokens), F32)
    out = call(
        kernel,
        (steps,),
        left.specs(tile, column_index) + right.specs(tile, column_index),
        pl.BlockSpec((1, tokens), whole_index),
        jax.ShapeDtypeStruct((1, tokens), F32),
        [pltpu.VMEM((tokens, tile), BF16)] * 2 + [gram] * 2,
        (4 * tokens * tokens * width, 4 * tokens * width, 0),
    )(flags, *left.arrays, *right.arrays)
    return jnp.sum(out)


def gradient(left, right, scale, flags):
    width, right_width = left.arrays[0].shape[1], right.arrays[0].shape[1]
    tokens = 2 * left.length * left.rows
    n, m = len(left.arrays), len(right.arrays)

    def kernel(flags_ref, scale_ref, *refs):
        out_ref, left_all, right_all = refs[n + m :]
        core = flags_ref[1]

        @pl.when(pl.program_id(0) == 0)
        def _():
            right.fill(right_all, refs[n : n + m], core)

        left.fill(left_all, refs[:n], core)
        product = lax.dot_general(
            left_all[...], right_all[...], FIRST, preferred_element_type=F32
        )
        out_ref[...] = (product * scale_ref[0, 0]).astype(BF16)

    return call(
        kernel,
        (width // TILE,),
        [pl.BlockSpec(memory_space=pltpu.SMEM)]
        + left.specs(TILE, column_index)
        + right.specs(right_width, whole_index),
        pl.BlockSpec((TILE, right_width), lambda i, flags: (i, 0)),
        jax.ShapeDtypeStruct((width, right_width), BF16),
        [pltpu.VMEM((tokens, TILE), BF16), pltpu.VMEM((tokens, right_width), BF16)],
        (
            2 * tokens * width * right_width,
            2 * width * right_width + 2 * tokens * (width + right_width),
            0,
        ),
    )(flags, scale.reshape(1, 1), *left.arrays, *right.arrays)


def row_chunks(rows):
    units, left = rows // 16, rows % 16
    if left or units < 3:
        return [(0, rows)]
    sizes = [units // 3, (units - units // 3) // 2]
    sizes.append(units - sum(sizes))
    firsts = [0, sizes[0], sizes[0] + sizes[1]]
    return [(16 * first, 16 * size) for first, size in zip(firsts, sizes)]


def on_device(inputs, pre_act, out_grad, token_valid, poison, w_up, w_down):
    n_row = lax.axis_size("row")
    n_col = lax.axis_size("col")
    rows = inputs.shape[0]
    length = n_row // 2
    row, col = lax.axis_index("row"), lax.axis_index("col")
    x, core = row % 2, col % 2
    flags = jnp.stack([x, core, col]).astype(jnp.int32)
    lines = [[2 * node + side for node in range(length)] for side in range(2)]
    bits = []
    bit = n_col // 2
    while bit:
        bits.append(bit)
        bit //= 2

    def along_line(value):
        return lax.all_gather(value, "row", axis=0, tiled=True, axis_index_groups=lines)

    masked = out_grad * token_valid.astype(BF16)[:, None]
    chunks = row_chunks(rows)
    masked_mine = [along_line(masked[a : a + n]) for a, n in chunks]
    masked_theirs = [swap(part, "row", 1) for part in masked_mine]

    pieces, offsets = [pre_act], [0]
    for bit in bits:
        pieces = pieces + [swap(piece, "col", bit) for piece in pieces]
        offsets = offsets + [offset ^ bit for offset in offsets]
    act, slope = gelu_all(pieces, offsets, flags, n_row // n_col, length, rows)
    slope = slope.reshape(length, rows, -1)

    kept, sent = [], []
    for (first, count), mine, theirs in zip(chunks, masked_mine, masked_theirs):
        keep, send = act_grad_part(mine, theirs, w_down, flags)
        total = keep + swap(send, "col", 1).astype(F32)
        for bit in reversed(bits[:-1]):
            total = total + swap(total.astype(BF16), "col", bit).astype(F32)
        slope_part = slope[:, first : first + count].reshape(total.shape)
        hidden = (total * slope_part).astype(BF16)
        kept.append(hidden)
        sent.append(swap(hidden, "col", 1))

    width = inputs.shape[1] // 2
    inputs_mine = [along_line(inputs[:, i * width : (i + 1) * width]) for i in range(2)]
    inputs_theirs = [swap(part, "row", 1) for part in inputs_mine]

    places = [(half, first, count) for half in range(2) for first, count in chunks]
    full = [(0, 0, rows), (1, 0, rows)]
    hidden_all = Rows(kept + sent, places, length, rows, by_core=True)
    masked_all = Rows(masked_mine + masked_theirs, places, length, rows)
    act_all = Rows([act[: length * rows], act[length * rows :]], full, length, rows)
    inputs_all = [
        Rows(list(pair), full, length, rows) for pair in zip(inputs_mine, inputs_theirs)
    ]
    inputs_whole = Rows(
        [jnp.concatenate(inputs_mine, axis=1), jnp.concatenate(inputs_theirs, axis=1)],
        full,
        length,
        rows,
    )
    del inputs_all

    model = w_up.shape[0]
    parts = 3 if model % (3 * TILE) == 0 else 1
    step = model // parts
    input_sums = []
    for part in range(parts):
        mine, theirs = input_part(hidden_all, w_up, part * step, step, flags)
        pair = (mine + swap(theirs, "row", 1).astype(F32)).astype(BF16)
        input_sums.append(
            lax.psum_scatter(
                pair, "row", scatter_dimension=0, axis_index_groups=lines, tiled=True
            )
        )

    square_term = gram_inner(act_all, masked_all, flags) + gram_inner(
        inputs_whole, hidden_all, flags
    )
    flag_value = poison[0, 0].astype(F32)
    keep_block = 1.0 - flag_value
    count_term = jnp.where(col == 0, jnp.sum(token_valid.astype(F32)), 0.0)
    scalars = jnp.stack([count_term, keep_block * square_term, flag_value])
    for axis, size in (("col", n_col), ("row", n_row)):
        bit = 1
        while bit < size:
            scalars = scalars + swap(scalars, axis, bit)
            bit *= 2
    count_all, square_all, flag_all = scalars[0], jnp.maximum(scalars[1], 0.0), scalars[2]

    token_total = jnp.maximum(count_all, 1.0)
    squares = square_all / (token_total * token_total)
    block_count = float(n_row * n_col)
    estimate = squares * block_count / jnp.maximum(block_count - flag_all, 1.0)
    total_tokens = rows * n_row
    model_width = w_up.shape[0] * n_col
    hidden_width = w_up.shape[1] * n_row
    limit = 0.25 * math.sqrt(hidden_width * model_width / total_tokens)
    clip_factor = jnp.minimum(1.0, limit / jnp.sqrt(estimate + 1e-06))
    scale = keep_block * clip_factor / token_total
    grad_down = gradient(act_all, masked_all, scale, flags)
    grad_up = gradient(inputs_whole, hidden_all, scale, flags)
    input_sum = jnp.concatenate(input_sums, axis=1).astype(F32)
    return (input_sum / token_total).astype(BF16), grad_up, grad_down


def solution(mesh):
    placed = (
        P("row", "col"),
        P("col", "row"),
        P("row", "col"),
        P("row"),
        P("row", "col"),
        P("col", "row"),
        P("row", "col"),
    )
    return jax.shard_map(
        on_device,
        mesh=mesh,
        in_specs=placed,
        out_specs=(P("row", "col"), P("col", "row"), P("row", "col")),
        check_vma=False,
    )
```

time: 467 us -> 376 us (0.81)
  waiting for transfers between devices: 242 us -> 58.1 us
  Pallas kernels: 0 us -> 150 us
  matrix products: 89 us -> 0 us
  blocking collectives: 42.6 us -> 90.6 us
  other arithmetic: 48.7 us -> 16 us
  starting transfers between devices: 0.42 us -> 21.4 us
  local copies, waits for them, and re-layouts: 24.6 us -> 18.7 us
    all_gather x4 -> x0, waiting for transfers between devices: 165 us -> none  [the longest x1 73.7 us: on_device(): lax.all_gather(masked, 'row', axis=0, tiled=True)]
    pallas_call x0 -> x11, Pallas kernels: none -> 150 us  [the longest x3 46.1 us: act_grad_part(): call(kernel, (width // TILE,), [pl.BlockSpec((count, depth), whole_index)...]
    all_gather x0 -> x5, blocking collectives: none -> 90.6 us  [along_line(): lax.all_gather(value, 'row', axis=0, tiled=True, axis_index_groups=lines)]
    dot_general x4 -> x0, matrix products: 89 us -> none  [the longest x1 26.3 us: on_device(): lax.dot_general(inputs_all, hidden_all, contract_first, preferred_element...]
    reduce_scatter x2 -> x3, waiting for transfers between devices: 76.4 us -> 0.03 us  [on_device(): lax.psum_scatter(pair, 'row', scatter_dimension=0, axis_index_groups=line...]
    ppermute x0 -> x25, waiting for transfers between devices: none -> 58 us  [swap(): return lax.ppermute(value, axis, [(i, i ^ bit) for i in range(size)])]
    psum x1 -> x0, blocking collectives: 42.6 us -> none  [on_device(): lax.psum((count_term, square_term, flag_value), ('row', 'col'))]
    convert_element_type x4 -> x11, other arithmetic: 46.2 us -> 10.7 us  [the longest x3 4.51 us: on_device(): pair = (mine + swap(theirs, 'row', 1).astype(F32)).astype(BF16)]
  transfers between devices with their start and end apart: 6 -> 28, of which waited for: 6 -> 9; matrix products, arithmetic and copies ran while one was open for 29% -> 7% of each run, Pallas kernels for 0% -> 37%
where the time goes in v2:
time: 376 us; the launch traced here: 374 us
  Pallas kernels  150 us (40%)
  blocking collectives  90.6 us (24%)
  waiting for transfers between devices  58.1 us (15%)
  starting transfers between devices  21.4 us (6%)
  between operations  18.9 us (5%)
  local copies, waits for them, and re-layouts  18.7 us (5%)
  other arithmetic  16 us (4%)
    all_gather x5, blocking collectives, along_line(): lax.all_gather(value, 'row', axis=0, tiled=True, axis_index_groups=lines)  90.6 us
    ppermute x25, waiting for transfers between devices, swap(): return lax.ppermute(value, axis, [(i, i ^ bit) for i in range(size)])  58 us
    pallas_call x3, Pallas kernels, act_grad_part(): call(kernel, (width // TILE,), [pl.BlockSpec((count, depth), whole_index)...  46.1 us
    pallas_call x2, Pallas kernels, gradient(): call(kernel, (width // TILE,), [pl.BlockSpec(memory_space=pltpu.SMEM)] +...  43.3 us
    pallas_call x3, Pallas kernels, input_part(): call(kernel, (width // TILE,), hidden.specs(depth, whole_index) + [pl.Blo...  29.1 us
    pallas_call x2, Pallas kernels, gram_inner(): call(kernel, (steps,), left.specs(tile, column_index) + right.specs(tile,...  22.1 us
    ppermute x25, starting transfers between devices, swap(): return lax.ppermute(value, axis, [(i, i ^ bit) for i in range(size)])  21.1 us
    pallas_call x1, Pallas kernels, gelu_all(): call(kernel, (width // tile,), [pl.BlockSpec((p.shape[0], tile), column_i...  9.28 us
  transfers between devices with their start and end apart: 28, of which 9 were waited for; matrix products, arithmetic and copies ran while one was open for 7% of the time, Pallas kernels for 37%

profile of v2, /device:TPU:0, one launch (start us, length us, event | category | flops | bytes accessed | tf_op | source)
XLA Modules:
  0.0 373.5 jit_solution(18134481943236475422)
XLA Ops:
  7.2 3.0 collective-permute-start.3
  12.1 19.9 %all_gather.17.mine_ref.refs_4_ = bf16[128,3072]{1,0:T(8,128)(2,1)S(1)} all-gather(bf16[32,3072]{1,0:T(8,128)(2,1)S(1)} %get-tuple-element.37), channel_id=1, replica_groups={{0,8,16,24},{4,12,20,28},{1,9,17,25},{5,13,21,29},{2,10,18,26},{6,14,22..., dimensions={0}, use_global_device_ids=true | all-gather | bytes 983040 | tf_op jit(solution)/shard_map/all_gather | solution.py:280
  33.5 18.1 %all_gather.16.mine_ref.refs_3_ = bf16[128,3072]{1,0:T(8,128)(2,1)S(1)} all-gather(bf16[32,3072]{1,0:T(8,128)(2,1)S(1)} %get-tuple-element.38), channel_id=1, replica_groups={{0,8,16,24},{4,12,20,28},{1,9,17,25},{5,13,21,29},{2,10,18,26},{6,14,22..., dimensions={0}, use_global_device_ids=true | all-gather | bytes 983040 | tf_op jit(solution)/shard_map/all_gather | solution.py:280
  52.2 15.3 %all_gather.15.mine_ref.refs_2_ = bf16[64,3072]{1,0:T(8,128)(2,1)S(1)} all-gather(bf16[16,3072]{1,0:T(8,128)(2,1)S(1)} %slice.52), channel_id=1, replica_groups={{0,8,16,24},{4,12,20,28},{1,9,17,25},{5,13,21,29},{2,10,18,26},{6,14,22..., dimensions={0}, use_global_device_ids=true | all-gather | bytes 491520 | tf_op jit(solution)/shard_map/all_gather | solution.py:280
  69.0 20.0 %all_gather.18 = bf16[320,1536]{1,0:T(8,128)(2,1)} all-gather(bf16[80,1536]{1,0:T(8,128)(2,1)S(1)} %get-tuple-element.36), channel_id=1, replica_groups={{0,8,16,24},{4,12,20,28},{1,9,17,25},{5,13,21,29},{2,10,18,26},{6,14,22..., dimensions={0}, use_global_device_ids=true | all-gather | bytes 1228800 | tf_op jit(solution)/shard_map/all_gather | solution.py:280
  89.0 17.2 %all_gather.19 = bf16[320,1536]{1,0:T(8,128)(2,1)} all-gather(bf16[80,1536]{1,0:T(8,128)(2,1)S(1)} %get-tuple-element.35), channel_id=1, replica_groups={{0,8,16,24},{4,12,20,28},{1,9,17,25},{5,13,21,29},{2,10,18,26},{6,14,22..., dimensions={0}, use_global_device_ids=true | all-gather | bytes 1228800 | tf_op jit(solution)/shard_map/all_gather | solution.py:280
  113.9 15.2 %shard_map.94 = (f32[64,3072]{1,0:T(8,128)}, bf16[64,3072]{1,0:T(8,128)(2,1)}) custom-call(s32[3]{0:T(128)} %pad_add_fusion.flags_ref, bf16[64,3072]{1,0:T(8,128)(2,1)} %copy-done.15, bf16[64,3072]{1,0:T(8,128)(2,1)} %collective-permute-done.theirs_ref.refs_5_, bf16[3072,3072]{1,0:T(8,128)(2,1)} %w_ref.5), custom_call_target="tpu_custom_call" | custom-call | flops 2415919104 | bytes 20840448 | tf_op jit(solution)/shard_map/pallas_call | solution.py:129
  130.0 15.4 %shard_map.97 = (f32[128,3072]{1,0:T(8,128)}, bf16[128,3072]{1,0:T(8,128)(2,1)}) custom-call(s32[3]{0:T(128)} %pad_add_fusion.flags_ref, bf16[128,3072]{1,0:T(8,128)(2,1)} %copy-done.9, bf16[128,3072]{1,0:T(8,128)(2,1)} %copy-done.19, bf16[3072,3072]{1,0:T(8,128)(2,1)} %w_ref.5), custom_call_target="tpu_custom_call" | custom-call | flops 4831838208 | bytes 22806528 | tf_op jit(solution)/shard_map/pallas_call | solution.py:129
  146.3 15.4 %shard_map.96 = (f32[128,3072]{1,0:T(8,128)}, bf16[128,3072]{1,0:T(8,128)(2,1)}) custom-call(s32[3]{0:T(128)} %pad_add_fusion.flags_ref, bf16[128,3072]{1,0:T(8,128)(2,1)} %copy-done.10, bf16[128,3072]{1,0:T(8,128)(2,1)} %copy-done.20, bf16[3072,3072]{1,0:T(8,128)(2,1)} %w_ref.5), custom_call_target="tpu_custom_call" | custom-call | flops 4831838208 | bytes 22806528 | tf_op jit(solution)/shard_map/pallas_call | solution.py:129
  168.5 9.3 %shard_map.95 = (bf16[640,3072]{1,0:T(8,128)(2,1)}, f32[320,3072]{1,0:T(8,128)}) custom-call(s32[3]{0:T(128)} %pad_add_fusion.flags_ref, bf16[160,3072]{1,0:T(8,128)(2,1)} %refs_0_.1, bf16[160,3072]{1,0:T(8,128)(2,1)} %collective-permute-done.3.refs_1_, bf16[160,3072]{1,0:T(8,128)(2,1)} %collective-permute-done.4.refs_2_, bf16[160,3072]{1,0:T(8,128)(2,1)} %copy-done.18), custom_call_target="tpu_custom_call" | custom-call | flops 58982400 | bytes 11796480 | tf_op jit(solution)/shard_map/pallas_call | solution.py:97
  181.1 12.0 %collective-permute-done.11 = bf16[128,3072]{1,0:T(8,128)(2,1)S(1)} collective-permute-done((bf16[128,3072]{1,0:T(8,128)(2,1)S(1)}, bf16[128,3072]{1,0:T(8,128)(2,1)S(1)}, u32[]{:S(2)}, u32[]{:S(2)}) %collective-permute-start.11) | collective-permute-done | bytes 786464 | tf_op jit(solution)/shard_map/ppermute | solution.py:22
  193.6 15.7 %collective-permute-done.8 = bf16[128,3072]{1,0:T(8,128)(2,1)} collective-permute-done((bf16[128,3072]{1,0:T(8,128)(2,1)}, bf16[128,3072]{1,0:T(8,128)(2,1)}, u32[]{:S(2)}, u32[]{:S(2)}) %collective-permute-start.8) | collective-permute-done | bytes 786464 | tf_op jit(solution)/shard_map/ppermute | solution.py:22
  217.6 10.0 %shard_map.98 = (f32[320,1024]{1,0:T(8,128)}, bf16[320,1024]{1,0:T(8,128)(2,1)}) custom-call(s32[3]{0:T(128)} %pad_add_fusion.flags_ref, bf16[64,3072]{1,0:T(8,128)(2,1)} %copy-done.6, bf16[128,3072]{1,0:T(8,128)(2,1)} %copy-done.1, bf16[128,3072]{1,0:T(8,128)(2,1)} %copy-done, bf16[64,3072]{1,0:T(8,128)(2,1)} %copy-done.8, bf16[128,3072]{1,0:T(8,128)(2,1)} %copy-done.3, ...), custom_call_target="tpu_custom_call" | custom-call | flops 4026531840 | bytes 12845056 | tf_op jit(solution)/shard_map/pallas_call | solution.py:163
  231.4 13.2 %collective-permute-done.15 = bf16[320,1024]{1,0:T(8,128)(2,1)S(1)} collective-permute-done((bf16[320,1024]{1,0:T(8,128)(2,1)}, bf16[320,1024]{1,0:T(8,128)(2,1)S(1)}, u32[]{:S(2)}, u32[]{:S(2)}) %collective-permute-start.15) | collective-permute-done | bytes 655392 | tf_op jit(solution)/shard_map/ppermute | solution.py:22
  245.9 9.6 %shard_map.99 = (f32[320,1024]{1,0:T(8,128)}, bf16[320,1024]{1,0:T(8,128)(2,1)}) custom-call(s32[3]{0:T(128)} %pad_add_fusion.flags_ref, bf16[64,3072]{1,0:T(8,128)(2,1)} %copy-done.6, bf16[128,3072]{1,0:T(8,128)(2,1)} %copy-done.1, bf16[128,3072]{1,0:T(8,128)(2,1)} %copy-done, bf16[64,3072]{1,0:T(8,128)(2,1)} %copy-done.8, bf16[128,3072]{1,0:T(8,128)(2,1)} %copy-done.3, ...), custom_call_target="tpu_custom_call" | custom-call | flops 4026531840 | bytes 12845056 | tf_op jit(solution)/shard_map/pallas_call | solution.py:163
  257.0 10.9 %shard_map.101 = f32[1,640]{1,0:T(1,128)} custom-call(s32[3]{0:T(128)} %pad_add_fusion.flags_ref, bf16[320,3072]{1,0:T(8,128)(2,1)} %get-tuple-element.32.refs_0_, bf16[320,3072]{1,0:T(8,128)(2,1)} %get-tuple-element.31.refs_1_, bf16[64,3072]{1,0:T(8,128)(2,1)} %copy-done.15, bf16[128,3072]{1,0:T(8,128)(2,1)} %copy-done.10, bf16[128,3072]{1,0:T(8,128)(2,1)} %copy-done.9, ...), custom_call_target="tpu_custom_call" | custom-call | flops 5033164800 | bytes 7864320 | tf_op jit(solution)/shard_map/pallas_call | solution.py:206
  269.3 11.2 %shard_map.102 = f32[1,640]{1,0:T(1,128)} custom-call(s32[3]{0:T(128)} %pad_add_fusion.flags_ref, bf16[320,3072]{1,0:T(8,128)(2,1)} %constant_dynamic-update-slice_fusion.refs_0_, bf16[320,3072]{1,0:T(8,128)(2,1)} %copy-done.21, bf16[64,3072]{1,0:T(8,128)(2,1)} %copy-done.6, bf16[128,3072]{1,0:T(8,128)(2,1)} %copy-done.1, bf16[128,3072]{1,0:T(8,128)(2,1)} %copy-done, ...), custom_call_target="tpu_custom_call" | custom-call | flops 5033164800 | bytes 7864320 | tf_op jit(solution)/shard_map/pallas_call | solution.py:206
  282.9 9.5 %shard_map.100 = (f32[320,1024]{1,0:T(8,128)}, bf16[320,1024]{1,0:T(8,128)(2,1)}) custom-call(s32[3]{0:T(128)} %pad_add_fusion.flags_ref, bf16[64,3072]{1,0:T(8,128)(2,1)} %copy-done.6, bf16[128,3072]{1,0:T(8,128)(2,1)} %copy-done.1, bf16[128,3072]{1,0:T(8,128)(2,1)} %copy-done, bf16[64,3072]{1,0:T(8,128)(2,1)} %copy-done.8, bf16[128,3072]{1,0:T(8,128)(2,1)} %copy-done.3, ...), custom_call_target="tpu_custom_call" | custom-call | flops 4026531840 | bytes 12845056 | tf_op jit(solution)/shard_map/pallas_call | solution.py:163
  296.0 3.1 collective-permute-done.21
  300.7 7.7 %collective-permute-done.22 = f32[3]{0:T(128)S(1)} collective-permute-done((f32[3]{0:T(128)S(1)}, f32[3]{0:T(128)S(1)}, u32[]{:S(2)}, u32[]{:S(2)}) %collective-permute-start.22) | collective-permute-done | bytes 44 | tf_op jit(solution)/shard_map/ppermute | solution.py:22
  313.9 2.5 collective-permute-done.24
  319.2 2.4 add_convert_fusion
  321.7 21.7 %shard_map.104 = bf16[3072,3072]{1,0:T(8,128)(2,1)} custom-call(s32[3]{0:T(128)} %pad_add_fusion.flags_ref, f32[1,1]{1,0:T(1,128)} %bitcast.14.scale_ref, bf16[320,3072]{1,0:T(8,128)(2,1)} %get-tuple-element.32.refs_0_, bf16[320,3072]{1,0:T(8,128)(2,1)} %get-tuple-element.31.refs_1_, bf16[64,3072]{1,0:T(8,128)(2,1)} %copy-done.15, ...), custom_call_target="tpu_custom_call" | custom-call | flops 12079595520 | bytes 26738688 | tf_op jit(solution)/shard_map/pallas_call | solution.py:237
  343.3 21.7 %shard_map.103 = bf16[3072,3072]{1,0:T(8,128)(2,1)} custom-call(s32[3]{0:T(128)} %pad_add_fusion.flags_ref, f32[1,1]{1,0:T(1,128)} %bitcast.14.scale_ref, bf16[320,3072]{1,0:T(8,128)(2,1)} %constant_dynamic-update-slice_fusion.refs_0_, bf16[320,3072]{1,0:T(8,128)(2,1)} %copy-done.21, bf16[64,3072]{1,0:T(8,128)(2,1)} %copy-done.6, ...), custom_call_target="tpu_custom_call" | custom-call | flops 12079595520 | bytes 26738688 | tf_op jit(solution)/shard_map/pallas_call | solution.py:237
  (132 shorter events, 54.6 us)
Async XLA Ops:
  7.2 357.8 %reduce-scatter.4.cloned.1.call-start = ((), (), s32[]{:S(2)}) async-start(), calls=%async_computation.3 | async-start | bytes 819200 | tf_op jit(solution)/shard_map/reduce_scatter | solution.py:333
  7.2 154.7 %collective-permute-start.3 = (bf16[160,3072]{1,0:T(8,128)(2,1)}, bf16[160,3072]{1,0:T(8,128)(2,1)}, u32[]{:S(2)}, u32[]{:S(2)}) collective-permute-start(bf16[160,3072]{1,0:T(8,128)(2,1)} %refs_0_.1), channel_id=1, source_target_pairs={{0,2},{1,3},{2,0},{3,1},{4,6},{5,7},{6,4},{7,5},{8,10},{9,11},{10,... | collective-permute-start | bytes 2949128 | tf_op jit(solution)/shard_map/ppermute | solution.py:22
  10.2 156.1 %collective-permute-start.4 = (bf16[160,3072]{1,0:T(8,128)(2,1)}, bf16[160,3072]{1,0:T(8,128)(2,1)}, u32[]{:S(2)}, u32[]{:S(2)}) collective-permute-start(bf16[160,3072]{1,0:T(8,128)(2,1)} %refs_0_.1), channel_id=1, source_target_pairs={{0,1},{1,0},{2,3},{3,2},{4,5},{5,4},{6,7},{7,6},{8,9},{9,8},{10,11... | collective-permute-start | bytes 2949128 | tf_op jit(solution)/shard_map/ppermute | solution.py:22
  32.0 97.1 %collective-permute-start.9 = (bf16[128,3072]{1,0:T(8,128)(2,1)S(1)}, bf16[128,3072]{1,0:T(8,128)(2,1)S(1)}, u32[]{:S(2)}, u32[]{:S(2)}) collective-permute-start(bf16[128,3072]{1,0:T(8,128)(2,1)S(1)} %all_gather.17.mine_ref.refs_4_), channel_id=1, source_target_pairs={{0,4},{4,0},{8,12},{12,8},{16,20},{20,16},{24,28},{28,24},{1,5},{5... | collective-permute-start | bytes 2359304 | tf_op jit(solution)/shard_map/ppermute | solution.py:22
  51.6 93.8 %collective-permute-start.6 = (bf16[128,3072]{1,0:T(8,128)(2,1)S(1)}, bf16[128,3072]{1,0:T(8,128)(2,1)S(1)}, u32[]{:S(2)}, u32[]{:S(2)}) collective-permute-start(bf16[128,3072]{1,0:T(8,128)(2,1)S(1)} %all_gather.16.mine_ref.refs_3_), channel_id=1, source_target_pairs={{0,4},{4,0},{8,12},{12,8},{16,20},{20,16},{24,28},{28,24},{1,5},{5... | collective-permute-start | bytes 2359304 | tf_op jit(solution)/shard_map/ppermute | solution.py:22
  67.5 46.0 %collective-permute-start = (bf16[64,3072]{1,0:T(8,128)(2,1)S(1)}, bf16[64,3072]{1,0:T(8,128)(2,1)}, u32[]{:S(2)}, u32[]{:S(2)}) collective-permute-start(bf16[64,3072]{1,0:T(8,128)(2,1)S(1)} %all_gather.15.mine_ref.refs_2_), channel_id=1, source_target_pairs={{0,4},{4,0},{8,12},{12,8},{16,20},{20,16},{24,28},{28,24},{1,5},{5... | collective-permute-start | bytes 1179656 | tf_op jit(solution)/shard_map/ppermute | solution.py:22
  113.4 98.4 %collective-permute-start.18 = (bf16[320,1536]{1,0:T(8,128)(2,1)}, bf16[320,1536]{1,0:T(8,128)(2,1)}, u32[]{:S(2)}, u32[]{:S(2)}) collective-permute-start(bf16[320,1536]{1,0:T(8,128)(2,1)} %all_gather.18), channel_id=1, source_target_pairs={{0,4},{4,0},{8,12},{12,8},{16,20},{20,16},{24,28},{28,24},{1,5},{5... | collective-permute-start | bytes 2949128 | tf_op jit(solution)/shard_map/ppermute | solution.py:22
  129.1 32.6 %collective-permute-start.1 = (bf16[64,3072]{1,0:T(8,128)(2,1)}, bf16[64,3072]{1,0:T(8,128)(2,1)S(1)}, u32[]{:S(2)}, u32[]{:S(2)}) collective-permute-start(bf16[64,3072]{1,0:T(8,128)(2,1)} %get-tuple-element.18), channel_id=1, source_target_pairs={{0,1},{1,0},{2,3},{3,2},{4,5},{5,4},{6,7},{7,6},{8,9},{9,8},{10,11... | collective-permute-start | bytes 1179656 | tf_op jit(solution)/shard_map/ppermute | solution.py:22
  145.4 18.1 %collective-permute-start.10 = (bf16[128,3072]{1,0:T(8,128)(2,1)}, bf16[128,3072]{1,0:T(8,128)(2,1)S(1)}, u32[]{:S(2)}, u32[]{:S(2)}) collective-permute-start(bf16[128,3072]{1,0:T(8,128)(2,1)} %get-tuple-element.23), channel_id=1, source_target_pairs={{0,1},{1,0},{2,3},{3,2},{4,5},{5,4},{6,7},{7,6},{8,9},{9,8},{10,11... | collective-permute-start | bytes 2359304 | tf_op jit(solution)/shard_map/ppermute | solution.py:22
  161.9 51.2 %collective-permute-start.19 = (bf16[320,1536]{1,0:T(8,128)(2,1)}, bf16[320,1536]{1,0:T(8,128)(2,1)}, u32[]{:S(2)}, u32[]{:S(2)}) collective-permute-start(bf16[320,1536]{1,0:T(8,128)(2,1)} %all_gather.19), channel_id=1, source_target_pairs={{0,4},{4,0},{8,12},{12,8},{16,20},{20,16},{24,28},{28,24},{1,5},{5... | collective-permute-start | bytes 2949128 | tf_op jit(solution)/shard_map/ppermute | solution.py:22
  163.6 3.9 %collective-permute-start.5 = (bf16[160,3072]{1,0:T(8,128)(2,1)}, bf16[160,3072]{1,0:T(8,128)(2,1)S(1)}, u32[]{:S(2)}, u32[]{:S(2)}) collective-permute-start(bf16[160,3072]{1,0:T(8,128)(2,1)} %collective-permute-done.3.refs_1_), channel_id=1, source_target_pairs={{0,1},{1,0},{2,3},{3,2},{4,5},{5,4},{6,7},{7,6},{8,9},{9,8},{10,11... | collective-permute-start | bytes 2949128 | tf_op jit(solution)/shard_map/ppermute | solution.py:22
  164.3 46.7 %collective-permute-start.2 = (bf16[64,3072]{1,0:T(8,128)(2,1)S(1)}, bf16[64,3072]{1,0:T(8,128)(2,1)S(1)}, u32[]{:S(2)}, u32[]{:S(2)}) collective-permute-start(bf16[64,3072]{1,0:T(8,128)(2,1)S(1)} %fusion.5), channel_id=1, source_target_pairs={{0,2},{1,3},{2,0},{3,1},{4,6},{5,7},{6,4},{7,5},{8,10},{9,11},{10,... | collective-permute-start | bytes 1179656 | tf_op jit(solution)/shard_map/ppermute | solution.py:22
  166.3 26.8 %collective-permute-start.11 = (bf16[128,3072]{1,0:T(8,128)(2,1)S(1)}, bf16[128,3072]{1,0:T(8,128)(2,1)S(1)}, u32[]{:S(2)}, u32[]{:S(2)}) collective-permute-start(bf16[128,3072]{1,0:T(8,128)(2,1)S(1)} %fusion.3), channel_id=1, source_target_pairs={{0,2},{1,3},{2,0},{3,1},{4,6},{5,7},{6,4},{7,5},{8,10},{9,11},{10,... | collective-permute-start | bytes 2359304 | tf_op jit(solution)/shard_map/ppermute | solution.py:22
  167.5 41.8 %collective-permute-start.8 = (bf16[128,3072]{1,0:T(8,128)(2,1)}, bf16[128,3072]{1,0:T(8,128)(2,1)}, u32[]{:S(2)}, u32[]{:S(2)}) collective-permute-start(bf16[128,3072]{1,0:T(8,128)(2,1)} %fusion.2), channel_id=1, source_target_pairs={{0,2},{1,3},{2,0},{3,1},{4,6},{5,7},{6,4},{7,5},{8,10},{9,11},{10,... | collective-permute-start | bytes 2359304 | tf_op jit(solution)/shard_map/ppermute | solution.py:22
  193.5 21.0 %collective-permute-start.14 = (bf16[128,3072]{1,0:T(8,128)(2,1)S(1)}, bf16[128,3072]{1,0:T(8,128)(2,1)S(1)}, u32[]{:S(2)}, u32[]{:S(2)}) collective-permute-start(bf16[128,3072]{1,0:T(8,128)(2,1)S(1)} %fusion.refs_2_.refs_4_), channel_id=1, source_target_pairs={{0,1},{1,0},{2,3},{3,2},{4,5},{5,4},{6,7},{7,6},{8,9},{9,8},{10,11... | collective-permute-start | bytes 2359304 | tf_op jit(solution)/shard_map/ppermute | solution.py:22
  211.0 4.9 %collective-permute-start.13 = (bf16[128,3072]{1,0:T(8,128)(2,1)S(1)}, bf16[128,3072]{1,0:T(8,128)(2,1)S(1)}, u32[]{:S(2)}, u32[]{:S(2)}) collective-permute-start(bf16[128,3072]{1,0:T(8,128)(2,1)S(1)} %fusion.1.refs_1_.refs_3_), channel_id=1, source_target_pairs={{0,1},{1,0},{2,3},{3,2},{4,5},{5,4},{6,7},{7,6},{8,9},{9,8},{10,11... | collective-permute-start | bytes 2359304 | tf_op jit(solution)/shard_map/ppermute | solution.py:22
  227.7 16.9 %collective-permute-start.15 = (bf16[320,1024]{1,0:T(8,128)(2,1)}, bf16[320,1024]{1,0:T(8,128)(2,1)S(1)}, u32[]{:S(2)}, u32[]{:S(2)}) collective-permute-start(bf16[320,1024]{1,0:T(8,128)(2,1)} %get-tuple-element.25), channel_id=1, source_target_pairs={{0,4},{4,0},{8,12},{12,8},{16,20},{20,16},{24,28},{28,24},{1,5},{5... | collective-permute-start | bytes 1966088 | tf_op jit(solution)/shard_map/ppermute | solution.py:22
  245.7 119.3 %reduce-scatter.6.cloned.1.call-start = ((), (), s32[]{:S(2)}) async-start(), calls=%async_computation.4 | async-start | bytes 819200 | tf_op jit(solution)/shard_map/reduce_scatter | solution.py:333
  255.5 26.3 %collective-permute-start.16 = (bf16[320,1024]{1,0:T(8,128)(2,1)}, bf16[320,1024]{1,0:T(8,128)(2,1)S(1)}, u32[]{:S(2)}, u32[]{:S(2)}) collective-permute-start(bf16[320,1024]{1,0:T(8,128)(2,1)} %get-tuple-element.27), channel_id=1, source_target_pairs={{0,4},{4,0},{8,12},{12,8},{16,20},{20,16},{24,28},{28,24},{1,5},{5... | collective-permute-start | bytes 1966088 | tf_op jit(solution)/shard_map/ppermute | solution.py:22
  282.9 82.1 %reduce-scatter.8.cloned.1.call-start = ((), (), s32[]{:S(2)}) async-start(), calls=%async_computation.5 | async-start | bytes 819200 | tf_op jit(solution)/shard_map/reduce_scatter | solution.py:333
  292.5 26.8 %collective-permute-start.17 = (bf16[320,1024]{1,0:T(8,128)(2,1)}, bf16[320,1024]{1,0:T(8,128)(2,1)S(1)}, u32[]{:S(2)}, u32[]{:S(2)}) collective-permute-start(bf16[320,1024]{1,0:T(8,128)(2,1)} %get-tuple-element.29), channel_id=1, source_target_pairs={{0,4},{4,0},{8,12},{12,8},{16,20},{20,16},{24,28},{28,24},{1,5},{5... | collective-permute-start | bytes 1966088 | tf_op jit(solution)/shard_map/ppermute | solution.py:22
  295.6 3.5 collective-permute-start.21
  299.2 9.2 %collective-permute-start.22 = (f32[3]{0:T(128)S(1)}, f32[3]{0:T(128)S(1)}, u32[]{:S(2)}, u32[]{:S(2)}) collective-permute-start(f32[3]{0:T(128)S(1)} %fusion.12), channel_id=1, source_target_pairs={{0,4},{4,0},{8,12},{12,8},{16,20},{20,16},{24,28},{28,24},{1,5},{5... | collective-permute-start | bytes 44 | tf_op jit(solution)/shard_map/ppermute | solution.py:22
  312.0 4.4 %collective-permute-start.24 = (f32[3]{0:T(128)S(1)}, f32[3]{0:T(128)S(1)}, u32[]{:S(2)}, u32[]{:S(2)}) collective-permute-start(f32[3]{0:T(128)S(1)} %add.76), channel_id=1, source_target_pairs={{0,16},{4,20},{8,24},{12,28},{16,0},{20,4},{24,8},{28,12},{1,17},{... | collective-permute-start | bytes 44 | tf_op jit(solution)/shard_map/ppermute | solution.py:22
  (28 other events, 332.4 us)
Sparse Core Ops, SparseCore 0:
  245.8 22.3 reduce-scatter.3
  283.0 21.5 reduce-scatter.5
  321.8 21.5 reduce-scatter.7

commit v3 on v0

v3 whole, which is shorter than its diff:
```python
import math

import jax
import jax.numpy as jnp
from jax import lax
from jax.experimental import pallas as pl
from jax.experimental.pallas import tpu as pltpu
from jax.sharding import PartitionSpec as P

F32 = jnp.float32
BF16 = jnp.bfloat16
LAST = (((1,), (1,)), ((), ()))
PLAIN = (((1,), (0,)), ((), ()))
FACTOR = math.sqrt(2.0 / math.pi)
TILE = 256
VMEM_LIMIT = 56 * 1024 * 1024


def swap(value, axis, bit):
    size = lax.axis_size(axis)
    return lax.ppermute(value, axis, [(i, i ^ bit) for i in range(size)])


def bits_of(size):
    return [1 << i for i in range(size.bit_length() - 1)]


def turned(index, size):
    return sum(((index // bit) % 2) * (size // 2 // bit) for bit in bits_of(size))


def call(kernel, grid, in_specs, out_specs, out_shape, scratch, cost):
    flops, moved, slow = cost
    return pl.pallas_call(
        kernel,
        grid_spec=pltpu.PrefetchScalarGridSpec(
            num_scalar_prefetch=1,
            grid=grid,
            in_specs=in_specs,
            out_specs=out_specs,
            scratch_shapes=scratch,
        ),
        out_shape=out_shape,
        compiler_params=pltpu.CompilerParams(
            dimension_semantics=("arbitrary",), vmem_limit_bytes=VMEM_LIMIT
        ),
        cost_estimate=pl.CostEstimate(
            flops=flops, bytes_accessed=moved, transcendentals=slow
        ),
    )


def whole_index(i, flags):
    return (0, 0)


def column_index(i, flags):
    return (0, i)


def row_index(i, flags):
    return (i, 0)


def aligned(start):
    return pl.multiple_of(start, 16)


def gelu_all(pre_all, flags, n_row, rows):
    tokens, width = pre_all.shape

    def kernel(flags_ref, pre_ref, act_ref, turn_ref, slope_ref):
        row, core = flags_ref[0], flags_ref[1]
        for source in range(n_row):
            index = row ^ source
            hval = pre_ref[source * rows : (source + 1) * rows, :].astype(F32)
            tanh_part = jnp.tanh(FACTOR * (hval + 0.044715 * hval * hval * hval))
            act_ref[pl.ds(aligned(turned(index, n_row) * rows), rows), :] = (
                0.5 * hval * (1.0 + tanh_part)
            ).astype(BF16)

            @pl.when(index % 2 == core)
            def _():
                slope_ref[pl.ds(aligned((index // 2) * rows), rows), :] = 0.5 * (
                    1.0 + tanh_part
                ) + 0.5 * hval * (1.0 - tanh_part * tanh_part) * FACTOR * (
                    1.0 + 3.0 * 0.044715 * hval * hval
                )

        turn_ref[...] = act_ref[...].T

    return call(
        kernel,
        (width // TILE,),
        [pl.BlockSpec((tokens, TILE), column_index)],
        [
            pl.BlockSpec((tokens, TILE), column_index),
            pl.BlockSpec((TILE, tokens), row_index),
            pl.BlockSpec((tokens // 2, TILE), column_index),
        ],
        [
            jax.ShapeDtypeStruct((tokens, width), BF16),
            jax.ShapeDtypeStruct((width, tokens), BF16),
            jax.ShapeDtypeStruct((tokens // 2, width), F32),
        ],
        [],
        (30 * tokens * width, 8 * tokens * width, tokens * width),
    )(flags, pre_all)


def act_grad_part(mine, theirs, w_down, flags):
    rows, depth = mine[0].shape
    n = len(mine)
    count = n * rows
    padded = -(-2 * count // 128) * 128
    width = w_down.shape[0]

    def kernel(flags_ref, *refs):
        w_ref, keep_ref, send_ref, both, both_turned = refs[2 * n :]

        @pl.when(pl.program_id(0) == 0)
        def _():
            core = flags_ref[1]
            if padded > 2 * count:
                both[2 * count :, :] = jnp.zeros((padded - 2 * count, depth), BF16)
            for i, ref in enumerate(refs[: 2 * n]):
                place = (core if i < n else 1 - core) * count + (i % n) * rows
                both[pl.ds(aligned(place), rows), :] = ref[...]
            both_turned[...] = both[...].T

        product = lax.dot_general(
            w_ref[...], both_turned[...], PLAIN, preferred_element_type=F32
        ).T
        keep_ref[...] = product[:count]
        send_ref[...] = product[count : 2 * count].astype(BF16)

    return call(
        kernel,
        (width // TILE,),
        [pl.BlockSpec((rows, depth), whole_index)] * (2 * n)
        + [pl.BlockSpec((TILE, depth), row_index)],
        [pl.BlockSpec((count, TILE), column_index)] * 2,
        [
            jax.ShapeDtypeStruct((count, width), F32),
            jax.ShapeDtypeStruct((count, width), BF16),
        ],
        [pltpu.VMEM((padded, depth), BF16), pltpu.VMEM((depth, padded), BF16)],
        (4 * count * depth * width, 2 * depth * width + 10 * count * width, 0),
    )(flags, *mine, *theirs, w_down)


def arrange(pieces, places, tokens, rows, flags):
    width = pieces[0].shape[1]
    tile = 2 * TILE if width % (2 * TILE) == 0 else TILE
    n = len(pieces)

    def kernel(flags_ref, *refs):
        out_ref, turn_ref = refs[n:]
        row, core = flags_ref[0], flags_ref[1]
        for ref, blocks in zip(refs[:n], places):
            for k, place in enumerate(blocks):
                out_ref[pl.ds(aligned(place(row, core) * rows), rows), :] = ref[
                    k * rows : (k + 1) * rows, :
                ]
        turn_ref[...] = out_ref[...].T

    return call(
        kernel,
        (width // tile,),
        [pl.BlockSpec((p.shape[0], tile), column_index) for p in pieces],
        [
            pl.BlockSpec((tokens, tile), column_index),
            pl.BlockSpec((tile, tokens), row_index),
        ],
        [
            jax.ShapeDtypeStruct((tokens, width), BF16),
            jax.ShapeDtypeStruct((width, tokens), BF16),
        ],
        [],
        (0, 6 * tokens * width, 0),
    )(flags, *pieces)


def input_part(hidden_turned, w_up, first, width, flags):
    depth, tokens = hidden_turned.shape
    half = tokens // 2

    def kernel(flags_ref, turned_ref, w_ref, mine_ref, theirs_ref):
        product = lax.dot_general(
            w_ref[...], turned_ref[...], PLAIN, preferred_element_type=F32
        ).T
        mine_ref[...] = product[:half]
        theirs_ref[...] = product[half:].astype(BF16)

    return call(
        kernel,
        (width // TILE,),
        [
            pl.BlockSpec((depth, tokens), whole_index),
            pl.BlockSpec((TILE, depth), lambda i, flags: (first // TILE + i, 0)),
        ],
        [pl.BlockSpec((half, TILE), column_index)] * 2,
        [
            jax.ShapeDtypeStruct((half, width), F32),
            jax.ShapeDtypeStruct((half, width), BF16),
        ],
        [],
        (2 * tokens * depth * width, 2 * depth * width + 2 * tokens * depth, 0),
    )(flags, hidden_turned, w_up)


def gram_inner(left, left_turned, right, right_turned, rows, flags):
    pieces = left if left_turned is None else [left, left_turned]
    n = len(pieces)
    tokens, width = right.shape
    tile = 2 * TILE if width % (2 * TILE) == 0 else TILE
    steps = width // tile

    def kernel(flags_ref, *refs):
        right_ref, right_turn_ref, out_ref, left_gram, right_gram = refs[n : n + 5]
        step = pl.program_id(0)

        @pl.when(step == 0)
        def _():
            left_gram[...] = jnp.zeros_like(left_gram)
            right_gram[...] = jnp.zeros_like(right_gram)

        if left_turned is None:
            left_all = refs[n + 5]
            for i, ref in enumerate(refs[:n]):
                left_all[i * rows : (i + 1) * rows, :] = ref[...]
            left_gram[...] += lax.dot_general(
                left_all[...], left_all[...], LAST, preferred_element_type=F32
            )
        else:
            left_gram[...] += lax.dot_general(
                refs[0][...], refs[1][...], PLAIN, preferred_element_type=F32
            )
        right_gram[...] += lax.dot_general(
            right_ref[...], right_turn_ref[...], PLAIN, preferred_element_type=F32
        )

        @pl.when(step == steps - 1)
        def _():
            out_ref[...] = jnp.sum(left_gram[...] * right_gram[...], axis=0, keepdims=True)

    plain = [pl.BlockSpec((tokens, tile), column_index), pl.BlockSpec((tile, tokens), row_index)]
    gram = pltpu.VMEM((tokens, tokens), F32)
    if left_turned is None:
        left_specs = [pl.BlockSpec((rows, tile), column_index)] * n
        extra = [pltpu.VMEM((tokens, tile), BF16)]
    else:
        left_specs, extra = plain, []
    out = call(
        kernel,
        (steps,),
        left_specs + plain,
        pl.BlockSpec((1, tokens), whole_index),
        jax.ShapeDtypeStruct((1, tokens), F32),
        [gram] * 2 + extra,
        (4 * tokens * tokens * width, 8 * tokens * width, 0),
    )(flags, *pieces, right, right_turned)
    return jnp.sum(out)


def gradient(left_turned, right, rows, scale, flags):
    height, tokens = left_turned.shape
    width = right[0].shape[1]
    n = len(right)

    def kernel(flags_ref, scale_ref, left_ref, *refs):
        out_ref = refs[n]
        if n == 1:
            right_all = refs[0][...]
        else:
            for i, ref in enumerate(refs[:n]):
                refs[n + 1][i * rows : (i + 1) * rows, :] = ref[...]
            right_all = refs[n + 1][...]
        product = lax.dot_general(
            left_ref[...], right_all, PLAIN, preferred_element_type=F32
        )
        out_ref[...] = (product * scale_ref[0, 0]).astype(BF16)

    return call(
        kernel,
        (width // TILE,),
        [
            pl.BlockSpec(memory_space=pltpu.SMEM),
            pl.BlockSpec((height, tokens), whole_index),
        ]
        + [pl.BlockSpec((piece.shape[0], TILE), column_index) for piece in right],
        pl.BlockSpec((height, TILE), column_index),
        jax.ShapeDtypeStruct((height, width), BF16),
        [pltpu.VMEM((tokens, TILE), BF16)] if n > 1 else [],
        (2 * tokens * width * height, 2 * width * height + 2 * tokens * (width + height), 0),
    )(flags, scale.reshape(1, 1), left_turned, *right)


def after(value, event):
    return lax.optimization_barrier((value, event))[0]


def on_device(inputs, pre_act, out_grad, token_valid, poison, w_up, w_down):
    n_row = lax.axis_size("row")
    n_col = lax.axis_size("col")
    rows = inputs.shape[0]
    tokens = rows * n_row
    slots = n_row // 2
    row, col = lax.axis_index("row"), lax.axis_index("col")
    core = col % 2
    flags = jnp.stack([row, core]).astype(jnp.int32)
    row_bits, col_bits = bits_of(n_row), bits_of(n_col)

    masked = {0: out_grad * token_valid.astype(BF16)[:, None]}
    for bit in reversed(row_bits):
        for index in sorted(masked):
            masked[index | bit] = swap(masked[index], "row", bit)

    pre_all = lax.all_gather(pre_act, "col", axis=0, tiled=True)
    inputs_all = lax.all_gather(after(inputs, pre_all), "row", axis=0, tiled=True)
    act, act_turned, slope = gelu_all(pre_all, flags, n_row, rows)

    groups = 2 if slots % 2 == 0 else 1
    per_group = slots // groups
    kept, sent = [], []
    for group in range(groups):
        chosen = range(group * per_group, (group + 1) * per_group)
        keep, send = act_grad_part(
            [masked[2 * slot] for slot in chosen],
            [masked[2 * slot + 1] for slot in chosen],
            w_down,
            flags,
        )
        total = keep + swap(send, "col", 1).astype(F32)
        for bit in col_bits[1:]:
            total = total + swap(total.astype(BF16), "col", bit).astype(F32)
        first = group * per_group * rows
        hidden = (total * slope[first : first + per_group * rows]).astype(BF16)
        kept.append(hidden)
        sent.append(swap(hidden, "col", 1))

    def hidden_place(half, slot):
        return lambda row, core: turned(2 * slot + (half ^ core), n_row)

    hidden_places = [
        [hidden_place(half, group * per_group + k) for k in range(per_group)]
        for half in range(2)
        for group in range(groups)
    ]
    hidden_all, hidden_turned = arrange(kept + sent, hidden_places, tokens, rows, flags)

    def inputs_place(source):
        return lambda row, core: turned(row ^ source, n_row)

    inputs_all, inputs_turned = arrange(
        [inputs_all], [[inputs_place(source) for source in range(n_row)]], tokens, rows, flags
    )
    masked_blocks = [masked[turned(place, n_row)] for place in range(n_row)]

    model = w_up.shape[0]
    parts = 3 if model % (3 * TILE) == 0 else 1
    step = model // parts
    input_sums = []
    for part in range(parts):
        total, theirs = input_part(hidden_turned, w_up, part * step, step, flags)
        total = total + swap(theirs, "row", 1).astype(F32)
        for bit in row_bits[1:]:
            half = total.shape[0] // 2
            total = total[:half] + swap(total[half:].astype(BF16), "row", bit).astype(F32)
        input_sums.append(total)

    square_term = gram_inner(
        masked_blocks, None, act, act_turned, rows, flags
    ) + gram_inner(inputs_all, inputs_turned, hidden_all, hidden_turned, rows, flags)
    flag_value = poison[0, 0].astype(F32)
    keep_block = 1.0 - flag_value
    count_term = jnp.where(col == 0, jnp.sum(token_valid.astype(F32)), 0.0)
    scalars = jnp.stack([count_term, keep_block * square_term, flag_value])
    for axis, bits in (("col", col_bits), ("row", row_bits)):
        for bit in bits:
            scalars = scalars + swap(scalars, axis, bit)
    count_all, square_all, flag_all = scalars[0], jnp.maximum(scalars[1], 0.0), scalars[2]

    token_total = jnp.maximum(count_all, 1.0)
    squares = square_all / (token_total * token_total)
    block_count = float(n_row * n_col)
    estimate = squares * block_count / jnp.maximum(block_count - flag_all, 1.0)
    model_width = w_up.shape[0] * n_col
    hidden_width = w_up.shape[1] * n_row
    limit = 0.25 * math.sqrt(hidden_width * model_width / tokens)
    clip_factor = jnp.minimum(1.0, limit / jnp.sqrt(estimate + 1e-06))
    scale = keep_block * clip_factor / token_total
    grad_down = gradient(act_turned, masked_blocks, rows, scale, flags)
    grad_up = gradient(inputs_turned, [hidden_all], rows, scale, flags)
    input_sum = jnp.concatenate(input_sums, axis=1)
    return (input_sum / token_total).astype(BF16), grad_up, grad_down


def solution(mesh):
    placed = (
        P("row", "col"),
        P("col", "row"),
        P("row", "col"),
        P("row"),
        P("row", "col"),
        P("col", "row"),
        P("row", "col"),
    )
    return jax.shard_map(
        on_device,
        mesh=mesh,
        in_specs=placed,
        out_specs=(P("row", "col"), P("col", "row"), P("row", "col")),
        check_vma=False,
    )
```

time: 467 us -> 349 us (0.75)
  Pallas kernels: 0 us -> 163 us
  waiting for transfers between devices: 242 us -> 115 us
  matrix products: 89 us -> 0 us
  blocking collectives: 42.6 us -> 0 us
  other arithmetic: 48.7 us -> 15.4 us
  starting transfers between devices: 0.42 us -> 29.9 us
  local copies, waits for them, and re-layouts: 24.6 us -> 4.13 us
    all_gather x4 -> x2, waiting for transfers between devices: 165 us -> 0.02 us  [the longest x1 0.02 us: on_device(): lax.all_gather(after(inputs, pre_all), 'row', axis=0, tiled=True)]
    pallas_call x0 -> x12, Pallas kernels: none -> 163 us  [the longest x2 42.5 us: gradient(): call(kernel, (width // TILE,), [pl.BlockSpec(memory_space=pltpu.SMEM), pl...]
    ppermute x0 -> x27, waiting for transfers between devices: none -> 115 us  [swap(): return lax.ppermute(value, axis, [(i, i ^ bit) for i in range(size)])]
    dot_general x4 -> x0, matrix products: 89 us -> none  [the longest x1 26.3 us: on_device(): lax.dot_general(inputs_all, hidden_all, contract_first, preferred_element...]
    reduce_scatter x2 -> x0, waiting for transfers between devices: 76.4 us -> none  [the longest x1 67.5 us: on_device(): lax.psum_scatter(lax.dot_general(block, w_down, contract_last, preferred_...]
    psum x1 -> x0, blocking collectives: 42.6 us -> none  [on_device(): lax.psum((count_term, square_term, flag_value), ('row', 'col'))]
    convert_element_type x4 -> x5, other arithmetic: 46.2 us -> 9.17 us  [the longest x1 5.22 us: on_device(): hidden = (total * slope[first:first + per_group * rows]).astype(BF16)]
    ppermute x0 -> x27, starting transfers between devices: none -> 29.8 us  [swap(): return lax.ppermute(value, axis, [(i, i ^ bit) for i in range(size)])]
  transfers between devices with their start and end apart: 6 -> 29, of which waited for: 6 -> 17; matrix products, arithmetic and copies ran while one was open for 29% -> 4% of each run, Pallas kernels for 0% -> 29%
where the time goes in v3:
time: 349 us; the launch traced here: 347 us
  Pallas kernels  163 us (47%)
  waiting for transfers between devices  115 us (33%)
  starting transfers between devices  29.9 us (9%)
  between operations  19.1 us (5%)
  other arithmetic  15.4 us (4%)
  local copies, waits for them, and re-layouts  4.13 us (1%)
    ppermute x27, waiting for transfers between devices, swap(): return lax.ppermute(value, axis, [(i, i ^ bit) for i in range(size)])  115 us
    pallas_call x2, Pallas kernels, gradient(): call(kernel, (width // TILE,), [pl.BlockSpec(memory_space=pltpu.SMEM), pl...  42.5 us
    pallas_call x2, Pallas kernels, act_grad_part(): call(kernel, (width // TILE,), [pl.BlockSpec((rows, depth), whole_index)]...  39 us
    pallas_call x3, Pallas kernels, input_part(): call(kernel, (width // TILE,), [pl.BlockSpec((depth, tokens), whole_index...  29.9 us
    ppermute x27, starting transfers between devices, swap(): return lax.ppermute(value, axis, [(i, i ^ bit) for i in range(size)])  29.8 us
    pallas_call x2, Pallas kernels, gram_inner(): call(kernel, (steps,), left_specs + plain, pl.BlockSpec((1, tokens), whol...  23.2 us
    pallas_call x2, Pallas kernels, arrange(): call(kernel, (width // tile,), [pl.BlockSpec((p.shape[0], tile), column_i...  15.3 us
    pallas_call x1, Pallas kernels, gelu_all(): call(kernel, (width // TILE,), [pl.BlockSpec((tokens, TILE), column_index...  12.8 us
  transfers between devices with their start and end apart: 29, of which 17 were waited for; matrix products, arithmetic and copies ran while one was open for 4% of the time, Pallas kernels for 29%

profile of v3, /device:TPU:0, one launch (start us, length us, event | category | flops | bytes accessed | tf_op | source)
XLA Modules:
  0.0 346.6 jit_solution(9193934767608154446)
XLA Ops:
  9.8 4.1 %collective-permute-start.5 = (bf16[80,3072]{1,0:T(8,128)(2,1)S(1)}, bf16[80,3072]{1,0:T(8,128)(2,1)S(1)}, u32[]{:S(2)}, u32[]{:S(2)}) collective-permute-start(bf16[80,3072]{1,0:T(8,128)(2,1)S(1)} %broadcast_multiply_fusion.refs_0_), channel_id=1, source_target_pairs={{0,16},{4,20},{8,24},{12,28},{16,0},{20,4},{24,8},{28,12},{1,17},{... | collective-permute-start | bytes 1474568 | tf_op jit(solution)/shard_map/ppermute | solution.py:21
  15.4 20.3 %collective-permute-done.5.refs_0_.refs_1_ = bf16[80,3072]{1,0:T(8,128)(2,1)S(1)} collective-permute-done((bf16[80,3072]{1,0:T(8,128)(2,1)S(1)}, bf16[80,3072]{1,0:T(8,128)(2,1)S(1)}, u32[]{:S(2)}, u32[]{:S(2)}) %collective-permute-start.5) | collective-permute-done | bytes 491552 | tf_op jit(solution)/shard_map/ppermute | solution.py:21
  40.5 7.6 %collective-permute-done.6.refs_1_.refs_3_ = bf16[80,3072]{1,0:T(8,128)(2,1)} collective-permute-done((bf16[80,3072]{1,0:T(8,128)(2,1)S(1)}, bf16[80,3072]{1,0:T(8,128)(2,1)}, u32[]{:S(2)}, u32[]{:S(2)}) %collective-permute-start.6) | collective-permute-done | bytes 491552 | tf_op jit(solution)/shard_map/ppermute | solution.py:21
  50.5 10.5 %collective-permute-done.2.refs_3_.refs_6_ = bf16[80,3072]{1,0:T(8,128)(2,1)S(1)} collective-permute-done((bf16[80,3072]{1,0:T(8,128)(2,1)S(1)}, bf16[80,3072]{1,0:T(8,128)(2,1)S(1)}, u32[]{:S(2)}, u32[]{:S(2)}) %collective-permute-start.2) | collective-permute-done | bytes 491552 | tf_op jit(solution)/shard_map/ppermute | solution.py:21
  61.8 19.5 %shard_map.94 = (f32[160,3072]{1,0:T(8,128)}, bf16[160,3072]{1,0:T(8,128)(2,1)}) custom-call(s32[2]{0:T(128)} %pad_add_fusion.flags_ref, bf16[80,3072]{1,0:T(8,128)(2,1)} %copy-done.10, bf16[80,3072]{1,0:T(8,128)(2,1)} %copy-done.12, bf16[80,3072]{1,0:T(8,128)(2,1)} %copy-done.13, bf16[80,3072]{1,0:T(8,128)(2,1)} %copy-done.14, bf16[3072,3072]{1,0:T(8,128)(2,1)} %refs_4_.3), custom_call_target="tpu_custom_call" | custom-call | flops 6039797760 | bytes 23789568 | tf_op jit(solution)/shard_map/pallas_call | solution.py:137
  83.0 19.5 %shard_map.96 = (f32[160,3072]{1,0:T(8,128)}, bf16[160,3072]{1,0:T(8,128)(2,1)}) custom-call(s32[2]{0:T(128)} %pad_add_fusion.flags_ref, bf16[80,3072]{1,0:T(8,128)(2,1)} %copy-done.11, bf16[80,3072]{1,0:T(8,128)(2,1)} %collective-permute-done.6.refs_1_.refs_3_, bf16[80,3072]{1,0:T(8,128)(2,1)} %copy-done.15, bf16[80,3072]{1,0:T(8,128)(2,1)} %copy-done.16, ...), custom_call_target="tpu_custom_call" | custom-call | flops 6039797760 | bytes 23789568 | tf_op jit(solution)/shard_map/pallas_call | solution.py:137
  108.3 12.8 %shard_map.95 = (bf16[640,3072]{1,0:T(8,128)(2,1)}, bf16[3072,640]{1,0:T(8,128)(2,1)}, f32[320,3072]{1,0:T(8,128)}) custom-call(s32[2]{0:T(128)} %pad_add_fusion.flags_ref, bf16[640,3072]{1,0:T(8,128)(2,1)} %all-gather.3.cloned.1.call-done.pre_ref), custom_call_target="tpu_custom_call" | custom-call | flops 58982400 | bytes 15728640 | tf_op jit(solution)/shard_map/pallas_call | solution.py:92
  121.1 8.0 %collective-permute-done.4 = bf16[160,3072]{1,0:T(8,128)(2,1)} collective-permute-done((bf16[160,3072]{1,0:T(8,128)(2,1)}, bf16[160,3072]{1,0:T(8,128)(2,1)}, u32[]{:S(2)}, u32[]{:S(2)}) %collective-permute-start.4) | collective-permute-done | bytes 983072 | tf_op jit(solution)/shard_map/ppermute | solution.py:21
  129.1 20.1 %collective-permute-done.10 = bf16[160,3072]{1,0:T(8,128)(2,1)} collective-permute-done((bf16[160,3072]{1,0:T(8,128)(2,1)}, bf16[160,3072]{1,0:T(8,128)(2,1)}, u32[]{:S(2)}, u32[]{:S(2)}) %collective-permute-start.10) | collective-permute-done | bytes 983072 | tf_op jit(solution)/shard_map/ppermute | solution.py:21
  149.3 5.2 %multiply_convert_fusion = (bf16[160,3072]{1,0:T(8,128)(2,1)}, bf16[160,3072]{1,0:T(8,128)(2,1)}) fusion(f32[320,3072]{1,0:T(8,128)} %get-tuple-element.23, bf16[160,3072]{1,0:T(8,128)(2,1)} %collective-permute-done.10, f32[160,3072]{1,0:T(8,128)S(1)} %copy-done.2, bf16[160,3072]{1,0:T(8,128)(2,1)S(1)} %copy-done.4, ...), kind=kLoop, calls=%fused_computation | loop fusion | flops 5898240 | bytes 13762560 | tf_op jit(solution)/shard_map/convert_element_type | solution.py:338
  159.6 7.9 %shard_map.97 = (bf16[640,3072]{1,0:T(8,128)(2,1)}, bf16[3072,640]{1,0:T(8,128)(2,1)}) custom-call(s32[2]{0:T(128)} %pad_add_fusion.flags_ref, bf16[160,3072]{1,0:T(8,128)(2,1)} %get-tuple-element.40.refs_0_, bf16[160,3072]{1,0:T(8,128)(2,1)} %get-tuple-element.39.refs_1_, bf16[160,3072]{1,0:T(8,128)(2,1)} %copy-done.9, bf16[160,3072]{1,0:T(8,128)(2,1)} %copy-done.8), custom_call_target="tpu_custom_call" | custom-call | bytes 11796480 | tf_op jit(solution)/shard_map/pallas_call | solution.py:167
  167.6 10.0 %shard_map.100 = (f32[320,1024]{1,0:T(8,128)}, bf16[320,1024]{1,0:T(8,128)(2,1)}) custom-call(s32[2]{0:T(128)} %pad_add_fusion.flags_ref, bf16[3072,640]{1,0:T(8,128)(2,1)} %get-tuple-element.26.turned_ref.refs_3_, bf16[3072,3072]{1,0:T(8,128)(2,1)} %w_ref.5), custom_call_target="tpu_custom_call" | custom-call | flops 4026531840 | bytes 10223616 | tf_op jit(solution)/shard_map/pallas_call | solution.py:195
  179.1 9.9 %shard_map.99 = (f32[320,1024]{1,0:T(8,128)}, bf16[320,1024]{1,0:T(8,128)(2,1)}) custom-call(s32[2]{0:T(128)} %pad_add_fusion.flags_ref, bf16[3072,640]{1,0:T(8,128)(2,1)} %get-tuple-element.26.turned_ref.refs_3_, bf16[3072,3072]{1,0:T(8,128)(2,1)} %w_ref.5), custom_call_target="tpu_custom_call" | custom-call | flops 4026531840 | bytes 10223616 | tf_op jit(solution)/shard_map/pallas_call | solution.py:195
  189.0 10.0 %shard_map.98 = (f32[320,1024]{1,0:T(8,128)}, bf16[320,1024]{1,0:T(8,128)(2,1)}) custom-call(s32[2]{0:T(128)} %pad_add_fusion.flags_ref, bf16[3072,640]{1,0:T(8,128)(2,1)} %get-tuple-element.26.turned_ref.refs_3_, bf16[3072,3072]{1,0:T(8,128)(2,1)} %w_ref.5), custom_call_target="tpu_custom_call" | custom-call | flops 4026531840 | bytes 10223616 | tf_op jit(solution)/shard_map/pallas_call | solution.py:195
  201.0 11.5 %shard_map.101 = f32[1,640]{1,0:T(1,128)} custom-call(s32[2]{0:T(128)} %pad_add_fusion.flags_ref, bf16[80,3072]{1,0:T(8,128)(2,1)} %copy-done.10, bf16[80,3072]{1,0:T(8,128)(2,1)} %copy-done.11, bf16[80,3072]{1,0:T(8,128)(2,1)} %copy-done.12, bf16[80,3072]{1,0:T(8,128)(2,1)} %collective-permute-done.6.refs_1_.refs_3_, bf16[80,3072]{1,0:T(8,128)(2,1)} %copy-done.13, ...), custom_call_target="tpu_custom_call" | custom-call | flops 5033164800 | bytes 15728640 | tf_op jit(solution)/shard_map/pallas_call | solution.py:254
  218.6 11.1 %collective-permute-done.13 = bf16[320,1024]{1,0:T(8,128)(2,1)S(1)} collective-permute-done((bf16[320,1024]{1,0:T(8,128)(2,1)}, bf16[320,1024]{1,0:T(8,128)(2,1)S(1)}, u32[]{:S(2)}, u32[]{:S(2)}) %collective-permute-start.13) | collective-permute-done | bytes 655392 | tf_op jit(solution)/shard_map/ppermute | solution.py:21
  234.9 10.8 %collective-permute-done.14 = bf16[160,1024]{1,0:T(8,128)(2,1)S(1)} collective-permute-done((bf16[160,1024]{1,0:T(8,128)(2,1)S(1)}, bf16[160,1024]{1,0:T(8,128)(2,1)S(1)}, u32[]{:S(2)}, u32[]{:S(2)}) %collective-permute-start.14) | collective-permute-done | bytes 327712 | tf_op jit(solution)/shard_map/ppermute | solution.py:21
  246.0 9.4 %collective-permute-done.15 = bf16[80,1024]{1,0:T(8,128)(2,1)S(1)} collective-permute-done((bf16[80,1024]{1,0:T(8,128)(2,1)S(1)}, bf16[80,1024]{1,0:T(8,128)(2,1)S(1)}, u32[]{:S(2)}, u32[]{:S(2)}) %collective-permute-start.15) | collective-permute-done | bytes 163872 | tf_op jit(solution)/shard_map/ppermute | solution.py:21
  255.5 7.3 %shard_map.102 = (bf16[640,3072]{1,0:T(8,128)(2,1)}, bf16[3072,640]{1,0:T(8,128)(2,1)}) custom-call(s32[2]{0:T(128)} %pad_add_fusion.flags_ref, bf16[640,3072]{1,0:T(8,128)(2,1)} %all-gather.5.cloned.1.call-done.refs_0_), custom_call_target="tpu_custom_call" | custom-call | bytes 11796480 | tf_op jit(solution)/shard_map/pallas_call | solution.py:167
  262.9 11.7 %shard_map.103 = f32[1,640]{1,0:T(1,128)} custom-call(s32[2]{0:T(128)} %pad_add_fusion.flags_ref, bf16[640,3072]{1,0:T(8,128)(2,1)} %get-tuple-element.36.refs_0_, bf16[3072,640]{1,0:T(8,128)(2,1)} %get-tuple-element.37.refs_1_.left_ref, bf16[640,3072]{1,0:T(8,128)(2,1)} %get-tuple-element.38.refs_2_.refs_0_, ...), custom_call_target="tpu_custom_call" | custom-call | flops 5033164800 | bytes 15728640 | tf_op jit(solution)/shard_map/pallas_call | solution.py:254
  285.7 3.5 %collective-permute-done.25 = f32[3]{0:T(128)S(1)} collective-permute-done((f32[3]{0:T(128)S(1)}, f32[3]{0:T(128)S(1)}, u32[]{:S(2)}, u32[]{:S(2)}) %collective-permute-start.25) | collective-permute-done | bytes 44 | tf_op jit(solution)/shard_map/ppermute | solution.py:21
  290.6 3.0 collective-permute-done.26
  296.4 21.0 %shard_map.104 = bf16[3072,3072]{1,0:T(8,128)(2,1)} custom-call(s32[2]{0:T(128)} %pad_add_fusion.flags_ref, f32[1,1]{1,0:T(1,128)} %bitcast.9.scale_ref, bf16[3072,640]{1,0:T(8,128)(2,1)} %get-tuple-element.37.refs_1_.left_ref, bf16[640,3072]{1,0:T(8,128)(2,1)} %get-tuple-element.38.refs_2_.refs_0_), custom_call_target="tpu_custom_call" | custom-call | flops 12079595520 | bytes 26738688 | tf_op jit(solution)/shard_map/pallas_call | solution.py:284
  318.2 21.5 %shard_map.105 = bf16[3072,3072]{1,0:T(8,128)(2,1)} custom-call(s32[2]{0:T(128)} %pad_add_fusion.flags_ref, f32[1,1]{1,0:T(1,128)} %bitcast.9.scale_ref, bf16[3072,640]{1,0:T(8,128)(2,1)} %get-tuple-element.34.refs_9_.left_ref, bf16[80,3072]{1,0:T(8,128)(2,1)} %copy-done.10, bf16[80,3072]{1,0:T(8,128)(2,1)} %copy-done.11, bf16[80,3072]{1,0:T(8,128)(2,1)} %copy-done.12, ...), custom_call_target="tpu_custom_call" | custom-call | flops 12079595520 | bytes 26738688 | tf_op jit(solution)/shard_map/pallas_call | solution.py:284
  (116 shorter events, 50.9 us)
Async XLA Ops:
  7.2 101.1 %all-gather.3.cloned.1.call-start = ((), (), s32[]{:S(2)}) async-start(), calls=%async_computation | async-start | bytes 4915200 | tf_op jit(solution)/shard_map/all_gather | solution.py:319
  7.9 247.6 %all-gather.5.cloned.1.call-start = ((), (), s32[]{:S(2)}) async-start(), calls=%async_computation.1 | async-start | bytes 4423680 | tf_op jit(solution)/shard_map/all_gather | solution.py:320
  9.8 26.0 %collective-permute-start.5 = (bf16[80,3072]{1,0:T(8,128)(2,1)S(1)}, bf16[80,3072]{1,0:T(8,128)(2,1)S(1)}, u32[]{:S(2)}, u32[]{:S(2)}) collective-permute-start(bf16[80,3072]{1,0:T(8,128)(2,1)S(1)} %broadcast_multiply_fusion.refs_0_), channel_id=1, source_target_pairs={{0,16},{4,20},{8,24},{12,28},{16,0},{20,4},{24,8},{28,12},{1,17},{... | collective-permute-start | bytes 1474568 | tf_op jit(solution)/shard_map/ppermute | solution.py:21
  13.9 24.0 %collective-permute-start = (bf16[80,3072]{1,0:T(8,128)(2,1)S(1)}, bf16[80,3072]{1,0:T(8,128)(2,1)S(1)}, u32[]{:S(2)}, u32[]{:S(2)}) collective-permute-start(bf16[80,3072]{1,0:T(8,128)(2,1)S(1)} %broadcast_multiply_fusion.refs_0_), channel_id=1, source_target_pairs={{0,8},{4,12},{8,0},{12,4},{16,24},{20,28},{24,16},{28,20},{1,9},{5... | collective-permute-start | bytes 1474568 | tf_op jit(solution)/shard_map/ppermute | solution.py:21
  35.7 12.5 %collective-permute-start.6 = (bf16[80,3072]{1,0:T(8,128)(2,1)S(1)}, bf16[80,3072]{1,0:T(8,128)(2,1)}, u32[]{:S(2)}, u32[]{:S(2)}) collective-permute-start(bf16[80,3072]{1,0:T(8,128)(2,1)S(1)} %collective-permute-done.5.refs_0_.refs_1_), channel_id=1, source_target_pairs={{0,8},{4,12},{8,0},{12,4},{16,24},{20,28},{24,16},{28,20},{1,9},{5... | collective-permute-start | bytes 1474568 | tf_op jit(solution)/shard_map/ppermute | solution.py:21
  36.3 14.1 %collective-permute-start.1 = (bf16[80,3072]{1,0:T(8,128)(2,1)S(1)}, bf16[80,3072]{1,0:T(8,128)(2,1)S(1)}, u32[]{:S(2)}, u32[]{:S(2)}) collective-permute-start(bf16[80,3072]{1,0:T(8,128)(2,1)S(1)} %broadcast_multiply_fusion.refs_0_), channel_id=1, source_target_pairs={{0,4},{4,0},{8,12},{12,8},{16,20},{20,16},{24,28},{28,24},{1,5},{5... | collective-permute-start | bytes 1474568 | tf_op jit(solution)/shard_map/ppermute | solution.py:21
  37.8 23.2 %collective-permute-start.2 = (bf16[80,3072]{1,0:T(8,128)(2,1)S(1)}, bf16[80,3072]{1,0:T(8,128)(2,1)S(1)}, u32[]{:S(2)}, u32[]{:S(2)}) collective-permute-start(bf16[80,3072]{1,0:T(8,128)(2,1)S(1)} %collective-permute-done.refs_1_.refs_2_), channel_id=1, source_target_pairs={{0,4},{4,0},{8,12},{12,8},{16,20},{20,16},{24,28},{28,24},{1,5},{5... | collective-permute-start | bytes 1474568 | tf_op jit(solution)/shard_map/ppermute | solution.py:21
  39.0 42.4 %collective-permute-start.7 = (bf16[80,3072]{1,0:T(8,128)(2,1)S(1)}, bf16[80,3072]{1,0:T(8,128)(2,1)S(1)}, u32[]{:S(2)}, u32[]{:S(2)}) collective-permute-start(bf16[80,3072]{1,0:T(8,128)(2,1)S(1)} %collective-permute-done.5.refs_0_.refs_1_), channel_id=1, source_target_pairs={{0,4},{4,0},{8,12},{12,8},{16,20},{20,16},{24,28},{28,24},{1,5},{5... | collective-permute-start | bytes 1474568 | tf_op jit(solution)/shard_map/ppermute | solution.py:21
  48.2 33.3 %collective-permute-start.8 = (bf16[80,3072]{1,0:T(8,128)(2,1)}, bf16[80,3072]{1,0:T(8,128)(2,1)S(1)}, u32[]{:S(2)}, u32[]{:S(2)}) collective-permute-start(bf16[80,3072]{1,0:T(8,128)(2,1)} %collective-permute-done.6.refs_1_.refs_3_), channel_id=1, source_target_pairs={{0,4},{4,0},{8,12},{12,8},{16,20},{20,16},{24,28},{28,24},{1,5},{5... | collective-permute-start | bytes 1474568 | tf_op jit(solution)/shard_map/ppermute | solution.py:21
  81.3 21.7 %collective-permute-start.3 = (bf16[160,3072]{1,0:T(8,128)(2,1)}, bf16[160,3072]{1,0:T(8,128)(2,1)S(1)}, u32[]{:S(2)}, u32[]{:S(2)}) collective-permute-start(bf16[160,3072]{1,0:T(8,128)(2,1)} %get-tuple-element.22), channel_id=1, source_target_pairs={{0,1},{1,0},{2,3},{3,2},{4,5},{5,4},{6,7},{7,6},{8,9},{9,8},{10,11... | collective-permute-start | bytes 2949128 | tf_op jit(solution)/shard_map/ppermute | solution.py:21
  104.2 24.9 %collective-permute-start.4 = (bf16[160,3072]{1,0:T(8,128)(2,1)}, bf16[160,3072]{1,0:T(8,128)(2,1)}, u32[]{:S(2)}, u32[]{:S(2)}) collective-permute-start(bf16[160,3072]{1,0:T(8,128)(2,1)} %fusion), channel_id=1, source_target_pairs={{0,2},{1,3},{2,0},{3,1},{4,6},{5,7},{6,4},{7,5},{8,10},{9,11},{10,... | collective-permute-start | bytes 2949128 | tf_op jit(solution)/shard_map/ppermute | solution.py:21
  107.0 42.3 %collective-permute-start.10 = (bf16[160,3072]{1,0:T(8,128)(2,1)}, bf16[160,3072]{1,0:T(8,128)(2,1)}, u32[]{:S(2)}, u32[]{:S(2)}) collective-permute-start(bf16[160,3072]{1,0:T(8,128)(2,1)} %fusion.1), channel_id=1, source_target_pairs={{0,2},{1,3},{2,0},{3,1},{4,6},{5,7},{6,4},{7,5},{8,10},{9,11},{10,... | collective-permute-start | bytes 2949128 | tf_op jit(solution)/shard_map/ppermute | solution.py:21
  154.5 4.2 %collective-permute-start.11 = (bf16[160,3072]{1,0:T(8,128)(2,1)}, bf16[160,3072]{1,0:T(8,128)(2,1)S(1)}, u32[]{:S(2)}, u32[]{:S(2)}) collective-permute-start(bf16[160,3072]{1,0:T(8,128)(2,1)} %get-tuple-element.40.refs_0_), channel_id=1, source_target_pairs={{0,1},{1,0},{2,3},{3,2},{4,5},{5,4},{6,7},{7,6},{8,9},{9,8},{10,11... | collective-permute-start | bytes 2949128 | tf_op jit(solution)/shard_map/ppermute | solution.py:21
  177.6 36.3 %collective-permute-start.19 = (bf16[320,1024]{1,0:T(8,128)(2,1)}, bf16[320,1024]{1,0:T(8,128)(2,1)S(1)}, u32[]{:S(2)}, u32[]{:S(2)}) collective-permute-start(bf16[320,1024]{1,0:T(8,128)(2,1)} %get-tuple-element.32), channel_id=1, source_target_pairs={{0,4},{4,0},{8,12},{12,8},{16,20},{20,16},{24,28},{28,24},{1,5},{5... | collective-permute-start | bytes 1966088 | tf_op jit(solution)/shard_map/ppermute | solution.py:21
  199.0 17.8 %collective-permute-start.16 = (bf16[320,1024]{1,0:T(8,128)(2,1)}, bf16[320,1024]{1,0:T(8,128)(2,1)S(1)}, u32[]{:S(2)}, u32[]{:S(2)}) collective-permute-start(bf16[320,1024]{1,0:T(8,128)(2,1)} %get-tuple-element.30), channel_id=1, source_target_pairs={{0,4},{4,0},{8,12},{12,8},{16,20},{20,16},{24,28},{28,24},{1,5},{5... | collective-permute-start | bytes 1966088 | tf_op jit(solution)/shard_map/ppermute | solution.py:21
  199.5 30.2 %collective-permute-start.13 = (bf16[320,1024]{1,0:T(8,128)(2,1)}, bf16[320,1024]{1,0:T(8,128)(2,1)S(1)}, u32[]{:S(2)}, u32[]{:S(2)}) collective-permute-start(bf16[320,1024]{1,0:T(8,128)(2,1)} %get-tuple-element.28), channel_id=1, source_target_pairs={{0,4},{4,0},{8,12},{12,8},{16,20},{20,16},{24,28},{28,24},{1,5},{5... | collective-permute-start | bytes 1966088 | tf_op jit(solution)/shard_map/ppermute | solution.py:21
  214.1 17.4 %collective-permute-start.20 = (bf16[160,1024]{1,0:T(8,128)(2,1)S(1)}, bf16[160,1024]{1,0:T(8,128)(2,1)S(1)}, u32[]{:S(2)}, u32[]{:S(2)}) collective-permute-start(bf16[160,1024]{1,0:T(8,128)(2,1)S(1)} %slice.100), channel_id=1, source_target_pairs={{0,8},{4,12},{8,0},{12,4},{16,24},{20,28},{24,16},{28,20},{1,9},{5... | collective-permute-start | bytes 983048 | tf_op jit(solution)/shard_map/ppermute | solution.py:21
  217.1 16.5 %collective-permute-start.17 = (bf16[160,1024]{1,0:T(8,128)(2,1)S(1)}, bf16[160,1024]{1,0:T(8,128)(2,1)S(1)}, u32[]{:S(2)}, u32[]{:S(2)}) collective-permute-start(bf16[160,1024]{1,0:T(8,128)(2,1)S(1)} %slice.101), channel_id=1, source_target_pairs={{0,8},{4,12},{8,0},{12,4},{16,24},{20,28},{24,16},{28,20},{1,9},{5... | collective-permute-start | bytes 983048 | tf_op jit(solution)/shard_map/ppermute | solution.py:21
  230.0 15.7 %collective-permute-start.14 = (bf16[160,1024]{1,0:T(8,128)(2,1)S(1)}, bf16[160,1024]{1,0:T(8,128)(2,1)S(1)}, u32[]{:S(2)}, u32[]{:S(2)}) collective-permute-start(bf16[160,1024]{1,0:T(8,128)(2,1)S(1)} %slice.102), channel_id=1, source_target_pairs={{0,8},{4,12},{8,0},{12,4},{16,24},{20,28},{24,16},{28,20},{1,9},{5... | collective-permute-start | bytes 983048 | tf_op jit(solution)/shard_map/ppermute | solution.py:21
  231.7 14.2 %collective-permute-start.21 = (bf16[80,1024]{1,0:T(8,128)(2,1)S(1)}, bf16[80,1024]{1,0:T(8,128)(2,1)S(1)}, u32[]{:S(2)}, u32[]{:S(2)}) collective-permute-start(bf16[80,1024]{1,0:T(8,128)(2,1)S(1)} %slice.103), channel_id=1, source_target_pairs={{0,16},{4,20},{8,24},{12,28},{16,0},{20,4},{24,8},{28,12},{1,17},{... | collective-permute-start | bytes 491528 | tf_op jit(solution)/shard_map/ppermute | solution.py:21
  233.7 12.2 %collective-permute-start.18 = (bf16[80,1024]{1,0:T(8,128)(2,1)S(1)}, bf16[80,1024]{1,0:T(8,128)(2,1)S(1)}, u32[]{:S(2)}, u32[]{:S(2)}) collective-permute-start(bf16[80,1024]{1,0:T(8,128)(2,1)S(1)} %slice.104), channel_id=1, source_target_pairs={{0,16},{4,20},{8,24},{12,28},{16,0},{20,4},{24,8},{28,12},{1,17},{... | collective-permute-start | bytes 491528 | tf_op jit(solution)/shard_map/ppermute | solution.py:21
  245.8 9.6 %collective-permute-start.15 = (bf16[80,1024]{1,0:T(8,128)(2,1)S(1)}, bf16[80,1024]{1,0:T(8,128)(2,1)S(1)}, u32[]{:S(2)}, u32[]{:S(2)}) collective-permute-start(bf16[80,1024]{1,0:T(8,128)(2,1)S(1)} %slice.105), channel_id=1, source_target_pairs={{0,16},{4,20},{8,24},{12,28},{16,0},{20,4},{24,8},{28,12},{1,17},{... | collective-permute-start | bytes 491528 | tf_op jit(solution)/shard_map/ppermute | solution.py:21
  278.5 3.5 %collective-permute-start.23 = (f32[3]{0:T(128)S(1)}, f32[3]{0:T(128)S(1)}, u32[]{:S(2)}, u32[]{:S(2)}) collective-permute-start(f32[3]{0:T(128)S(1)} %fusion.4), channel_id=1, source_target_pairs={{0,2},{1,3},{2,0},{3,1},{4,6},{5,7},{6,4},{7,5},{8,10},{9,11},{10,... | collective-permute-start | bytes 44 | tf_op jit(solution)/shard_map/ppermute | solution.py:21
  289.2 4.4 %collective-permute-start.26 = (f32[3]{0:T(128)S(1)}, f32[3]{0:T(128)S(1)}, u32[]{:S(2)}, u32[]{:S(2)}) collective-permute-start(f32[3]{0:T(128)S(1)} %add.82), channel_id=1, source_target_pairs={{0,16},{4,20},{8,24},{12,28},{16,0},{20,4},{24,8},{28,12},{1,17},{... | collective-permute-start | bytes 44 | tf_op jit(solution)/shard_map/ppermute | solution.py:21
  (23 other events, 292.3 us)
Sparse Core Ops, SparseCore 0:
  9.6 35.6 all-gather.2
  108.4 70.3 all-gather.4

commit v4 on v0

v4 whole, which is shorter than its diff:
```python
import math

import jax
import jax.numpy as jnp
from jax import lax
from jax.experimental import pallas as pl
from jax.experimental.pallas import tpu as pltpu
from jax.sharding import PartitionSpec as P

F32 = jnp.float32
BF16 = jnp.bfloat16
LAST = (((1,), (1,)), ((), ()))
PLAIN = (((1,), (0,)), ((), ()))
FACTOR = math.sqrt(2.0 / math.pi)
TILE = 256
VMEM_LIMIT = 56 * 1024 * 1024


def swap(value, axis, bit):
    size = lax.axis_size(axis)
    return lax.ppermute(value, axis, [(i, i ^ bit) for i in range(size)])


def bits_of(size):
    return [1 << i for i in range(size.bit_length() - 1)]


def turned(index, size):
    return sum(((index // bit) % 2) * (size // 2 // bit) for bit in bits_of(size))


def call(kernel, grid, in_specs, out_specs, out_shape, scratch, cost, aliases=None):
    flops, moved, slow = cost
    return pl.pallas_call(
        kernel,
        grid_spec=pltpu.PrefetchScalarGridSpec(
            num_scalar_prefetch=1,
            grid=grid,
            in_specs=in_specs,
            out_specs=out_specs,
            scratch_shapes=scratch,
        ),
        out_shape=out_shape,
        input_output_aliases=aliases or {},
        compiler_params=pltpu.CompilerParams(
            dimension_semantics=("arbitrary",), vmem_limit_bytes=VMEM_LIMIT
        ),
        cost_estimate=pl.CostEstimate(
            flops=flops, bytes_accessed=moved, transcendentals=slow
        ),
    )


def whole_index(i, flags):
    return (0, 0)


def column_index(i, flags):
    return (0, i)


def aligned(start):
    return pl.multiple_of(start, 16)


def gelu_all(pre_all, flags, n_row, rows):
    tokens, width = pre_all.shape

    def kernel(flags_ref, pre_ref, act_ref, slope_ref):
        row, core = flags_ref[0], flags_ref[1]
        for source in range(n_row):
            index = row ^ source
            hval = pre_ref[source * rows : (source + 1) * rows, :].astype(F32)
            tanh_part = jnp.tanh(FACTOR * (hval + 0.044715 * hval * hval * hval))
            act_ref[pl.ds(aligned(turned(index, n_row) * rows), rows), :] = (
                0.5 * hval * (1.0 + tanh_part)
            ).astype(BF16)

            @pl.when(index % 2 == core)
            def _():
                slope_ref[pl.ds(aligned((index // 2) * rows), rows), :] = 0.5 * (
                    1.0 + tanh_part
                ) + 0.5 * hval * (1.0 - tanh_part * tanh_part) * FACTOR * (
                    1.0 + 3.0 * 0.044715 * hval * hval
                )

    return call(
        kernel,
        (width // TILE,),
        [pl.BlockSpec((tokens, TILE), column_index)],
        [
            pl.BlockSpec((tokens, TILE), column_index),
            pl.BlockSpec((tokens // 2, TILE), column_index),
        ],
        [
            jax.ShapeDtypeStruct((tokens, width), BF16),
            jax.ShapeDtypeStruct((tokens // 2, width), F32),
        ],
        [],
        (30 * tokens * width, 6 * tokens * width, tokens * width),
    )(flags, pre_all)


def arrange(chunks, places, rows, flags):
    width = chunks[0][0].shape[1]
    tokens = sum(piece.shape[0] for piece in chunks[0])
    tile = 2 * TILE if width % (2 * TILE) == 0 else TILE
    tiles = width // tile
    n = len(places)

    def kernel(flags_ref, *refs):
        row, core = flags_ref[0], flags_ref[1]

        def fill(pieces):
            for ref, blocks in zip(pieces, places):
                for k, place in enumerate(blocks):
                    refs[-1][pl.ds(aligned(place(row, core) * rows), rows), :] = ref[
                        k * rows : (k + 1) * rows, :
                    ]

        for c in range(len(chunks)):
            pl.when(pl.program_id(0) // tiles == c)(lambda c=c: fill(refs[c * n : c * n + n]))

    def of_chunk(c):
        return lambda i, flags: (0, jnp.clip(i - c * tiles, 0, tiles - 1))

    return call(
        kernel,
        (tiles * len(chunks),),
        [
            pl.BlockSpec((piece.shape[0], tile), of_chunk(c))
            for c, pieces in enumerate(chunks)
            for piece in pieces
        ],
        pl.BlockSpec((tokens, tile), column_index),
        jax.ShapeDtypeStruct((tokens, width * len(chunks)), BF16),
        [],
        (0, 4 * tokens * width * len(chunks), 0),
    )(flags, *[piece for pieces in chunks for piece in pieces])


def stack(target, refs):
    if len(refs) == 1:
        return refs[0]
    start = 0
    for ref in refs:
        target[start : start + ref.shape[0], :] = ref[...]
        start += ref.shape[0]
    return target


def gram_inner(left, right, flags):
    n, m = len(left), len(right)
    tokens = sum(piece.shape[0] for piece in left)
    width = left[0].shape[1]
    tile = 2 * TILE if width % (2 * TILE) == 0 else TILE
    steps = width // tile

    def kernel(flags_ref, *refs):
        out_ref, left_all, right_all, left_gram, right_gram = refs[n + m :]
        step = pl.program_id(0)
        left_rows = stack(left_all, refs[:n])
        right_rows = stack(right_all, refs[n : n + m])

        @pl.when(step == 0)
        def _():
            left_gram[...] = jnp.zeros_like(left_gram)
            right_gram[...] = jnp.zeros_like(right_gram)

        for rows, total in ((left_rows, left_gram), (right_rows, right_gram)):
            total[...] += lax.dot_general(
                rows[...], rows[...], LAST, preferred_element_type=F32
            )

        @pl.when(step == steps - 1)
        def _():
            out_ref[...] = jnp.sum(left_gram[...] * right_gram[...], axis=0, keepdims=True)

    gram = pltpu.VMEM((tokens, tokens), F32)
    out = call(
        kernel,
        (steps,),
        [pl.BlockSpec((piece.shape[0], tile), column_index) for piece in left + right],
        pl.BlockSpec((1, tokens), whole_index),
        jax.ShapeDtypeStruct((1, tokens), F32),
        [pltpu.VMEM((tokens, tile), BF16)] * 2 + [gram] * 2,
        (4 * tokens * tokens * width, 4 * tokens * width, 0),
    )(flags, *left, *right)
    return jnp.sum(out)


def gradient(left, right, scale, flags, part, parts, before):
    height, width = left[0].shape[1], right[0].shape[1]
    tokens = sum(piece.shape[0] for piece in left)
    tile = 2 * TILE if height % (2 * TILE * parts) == 0 else TILE
    steps = height // tile // parts
    across = next(n for n in (768, 512, 256, width) if width % n == 0)
    n, m = len(left), len(right)

    def kernel(flags_ref, scale_ref, *refs):
        out_ref, left_all, right_all = refs[-3:]

        @pl.when(pl.program_id(0) == 0)
        def _():
            stack(right_all, refs[n : n + m])

        right_rows = refs[n] if m == 1 else right_all
        left_turned = stack(left_all, refs[:n])[...].T
        for start in range(0, width, across):
            product = lax.dot_general(
                left_turned,
                right_rows[:, start : start + across],
                PLAIN,
                preferred_element_type=F32,
            )
            out_ref[:, start : start + across] = (product * scale_ref[0, 0]).astype(BF16)

    def rows_of_part(i, flags):
        return (part * steps + i, 0)

    operands = [flags, scale.reshape(1, 1), *left, *right]
    in_specs = (
        [pl.BlockSpec(memory_space=pltpu.SMEM)]
        + [
            pl.BlockSpec((piece.shape[0], tile), lambda i, flags: (0, part * steps + i))
            for piece in left
        ]
        + [pl.BlockSpec((piece.shape[0], width), whole_index) for piece in right]
    )
    aliases = {}
    if before is not None:
        aliases = {len(operands): 0}
        operands.append(before)
        in_specs.append(pl.BlockSpec(memory_space=pl.ANY))
    return call(
        kernel,
        (steps,),
        in_specs,
        pl.BlockSpec((tile, width), rows_of_part),
        jax.ShapeDtypeStruct((height, width), BF16),
        [
            pltpu.VMEM((tokens, tile) if n > 1 else (16, 128), BF16),
            pltpu.VMEM((tokens, width) if m > 1 else (16, 128), BF16),
        ],
        (
            2 * tokens * width * height // parts,
            2 * width * height // parts + 2 * tokens * (width + height),
            0,
        ),
        aliases,
    )(*operands)


def after(value, *events):
    return lax.optimization_barrier((value, *events))[0]


def on_device(inputs, pre_act, out_grad, token_valid, poison, w_up, w_down):
    n_row = lax.axis_size("row")
    n_col = lax.axis_size("col")
    rows = inputs.shape[0]
    tokens = rows * n_row
    slots = n_row // 2
    row, col = lax.axis_index("row"), lax.axis_index("col")
    core = col % 2
    flags = jnp.stack([row, core]).astype(jnp.int32)
    row_bits, col_bits = bits_of(n_row), bits_of(n_col)

    def exchange(own, first_hop):
        blocks = {0: own}
        for bit in reversed(row_bits[1:]):
            for index in sorted(blocks):
                if index % 2 == 0:
                    source = blocks[index] if index == 0 else after(blocks[index], blocks[1])
                    blocks[index | bit] = swap(source, "row", bit)
                    if 1 not in blocks:
                        blocks[1] = swap(first_hop(own), "row", 1)
        for index in sorted(blocks):
            if index % 2 == 0 and index > 0:
                blocks[index | 1] = swap(blocks[index], "row", 1)
        return [blocks[index] for index in range(n_row)]

    pre_all = lax.all_gather(pre_act, "col", axis=0, tiled=True)
    masked = exchange(out_grad * token_valid.astype(BF16)[:, None], lambda own: own)
    inputs_all = exchange(after(inputs, masked[-2]), lambda own: after(own, masked[-1]))

    def group_place(index):
        return lambda row, core: ((index % 2) ^ core) * slots + index // 2

    block = arrange(
        [masked], [[group_place(index)] for index in range(n_row)], rows, flags
    )
    block = after(block, pre_all)
    half = tokens // 2
    hidden_width = w_down.shape[0]
    parts = 3 if hidden_width % (3 * TILE) == 0 else 1
    step = hidden_width // parts
    totals = []
    for part in range(parts):
        if part == parts - 1:
            block = after(block, inputs_all[2], *totals[:-1])
        partial = lax.dot_general(
            block, w_down[part * step : (part + 1) * step], LAST, preferred_element_type=F32
        )
        other = swap(partial[half:].astype(BF16), "col", 1)
        totals.append(partial[:half] + other.astype(F32))
    act, slope = gelu_all(
        after(pre_all, inputs_all[1], inputs_all[n_row // 2]), flags, n_row, rows
    )
    masked_blocks = [masked[turned(place, n_row)] for place in range(n_row)]
    square_down = gram_inner(
        masked_blocks, [after(act, inputs_all[3], inputs_all[-2])], flags
    )
    hidden_pieces = []
    for part, total in enumerate(totals):
        for bit in col_bits[1:]:
            total = total + swap(total.astype(BF16), "col", bit).astype(F32)
        hidden = (total * slope[:, part * step : (part + 1) * step]).astype(BF16)
        hidden_pieces.append([hidden, swap(hidden, "col", 1)])

    def hidden_place(side, slot):
        return lambda row, core: turned(2 * slot + (side ^ core), n_row)

    hidden_places = [[hidden_place(side, slot) for slot in range(slots)] for side in range(2)]
    hidden_pieces[0][0] = after(hidden_pieces[0][0], square_down, *inputs_all)
    hidden_all = arrange(hidden_pieces, hidden_places, rows, flags)
    inputs_blocks = [inputs_all[turned(place, n_row)] for place in range(n_row)]

    model = w_up.shape[0]
    parts = 3 if model % (3 * TILE) == 0 else 1
    step = model // parts
    flag_value = poison[0, 0].astype(F32)
    keep_block = 1.0 - flag_value
    count_term = jnp.where(col == 0, jnp.sum(token_valid.astype(F32)), 0.0)
    stages, partials = [], []
    operand = hidden_all
    for part in range(parts):
        partial = lax.dot_general(
            operand, w_up[part * step : (part + 1) * step], LAST, preferred_element_type=F32
        )
        partials.append(partial)
        theirs = partial[half:].astype(BF16)
        total = partial[:half] + swap(theirs, "row", 1).astype(F32)
        stages.append([total])
        for bit in row_bits[1:]:
            split = total.shape[0] // 2
            total = total[:split] + swap(total[split:].astype(BF16), "row", bit).astype(F32)
            stages[-1].append(total)
        if part == 0:
            square_up = gram_inner(inputs_blocks, [after(hidden_all, theirs)], flags)
            scalars = jnp.stack(
                [count_term, keep_block * (square_down + square_up), flag_value]
            )
            for bit in col_bits:
                scalars = scalars + swap(scalars, "col", bit)
            operand = after(hidden_all, scalars, stages[0][0])
        else:
            operand = after(operand, stages[0][1])
    for hop, bit in enumerate(row_bits):
        if 0 < hop < parts:
            scalars = after(scalars, partials[hop])
        scalars = scalars + swap(scalars, "row", bit)
    count_all, square_all, flag_all = scalars[0], jnp.maximum(scalars[1], 0.0), scalars[2]

    token_total = jnp.maximum(count_all, 1.0)
    squares = square_all / (token_total * token_total)
    block_count = float(n_row * n_col)
    estimate = squares * block_count / jnp.maximum(block_count - flag_all, 1.0)
    limit = 0.25 * math.sqrt(
        (w_up.shape[1] * n_row) * (w_up.shape[0] * n_col) / tokens
    )
    clip_factor = jnp.minimum(1.0, limit / jnp.sqrt(estimate + 1e-06))
    scale = keep_block * clip_factor / token_total

    grads = []
    call_index = 0
    for left, right in (([act], masked_blocks), (inputs_blocks, [hidden_all])):
        out = None
        for part in range(2):
            events = [
                stage[call_index - i + 1]
                for i, stage in enumerate(stages)
                if 0 <= call_index - i + 1 < len(stage)
            ]
            out = gradient(left, right, after(scale, *events), flags, part, 2, out)
            call_index += 1
        grads.append(out)
    input_sum = jnp.concatenate([stage[-1] for stage in stages], axis=1)
    return (input_sum / token_total).astype(BF16), grads[1], grads[0]


def solution(mesh):
    placed = (
        P("row", "col"),
        P("col", "row"),
        P("row", "col"),
        P("row"),
        P("row", "col"),
        P("col", "row"),
        P("row", "col"),
    )
    return jax.shard_map(
        on_device,
        mesh=mesh,
        in_specs=placed,
        out_specs=(P("row", "col"), P("col", "row"), P("row", "col")),
        check_vma=False,
    )
```

time: 467 us -> 323 us (0.69)
  waiting for transfers between devices: 242 us -> 89.9 us
  Pallas kernels: 0 us -> 99.1 us
  matrix products: 89 us -> 42 us
  blocking collectives: 42.6 us -> 0 us
  starting transfers between devices: 0.42 us -> 41.8 us
  other arithmetic: 48.7 us -> 20.6 us
  local copies, waits for them, and re-layouts: 24.6 us -> 8.93 us
    all_gather x4 -> x1, waiting for transfers between devices: 165 us -> 0.01 us  [on_device(): pre_all = lax.all_gather(pre_act, 'col', axis=0, tiled=True)]
    pallas_call x0 -> x9, Pallas kernels: none -> 99.1 us  [the longest x4 52 us: gradient(): call(kernel, (steps,), in_specs, pl.BlockSpec((tile, width), rows_of_part...]
    ppermute x0 -> x37, waiting for transfers between devices: none -> 89.2 us  [swap(): return lax.ppermute(value, axis, [(i, i ^ bit) for i in range(size)])]
    reduce_scatter x2 -> x0, waiting for transfers between devices: 76.4 us -> none  [the longest x1 67.5 us: on_device(): lax.psum_scatter(lax.dot_general(block, w_down, contract_last, preferred_...]
    dot_general x4 -> x6, matrix products: 89 us -> 42 us  [the longest x3 21 us: on_device(): lax.dot_general(operand, w_up[part * step:(part + 1) * step], LAST, prefe...]
    psum x1 -> x0, blocking collectives: 42.6 us -> none  [on_device(): lax.psum((count_term, square_term, flag_value), ('row', 'col'))]
    ppermute x0 -> x37, starting transfers between devices: none -> 41.7 us  [swap(): return lax.ppermute(value, axis, [(i, i ^ bit) for i in range(size)])]
    convert_element_type x4 -> x6, other arithmetic: 46.2 us -> 9.66 us  [the longest x1 4.97 us: on_device(): hidden = (total * slope[:, part * step:(part + 1) * step]).astype(BF16)]
  transfers between devices with their start and end apart: 6 -> 38, of which waited for: 6 -> 12; matrix products, arithmetic and copies ran while one was open for 29% -> 17% of each run, Pallas kernels for 0% -> 25%
where the time goes in v4:
time: 323 us; the launch traced here: 321 us
  Pallas kernels  99.1 us (31%)
  waiting for transfers between devices  89.9 us (28%)
  matrix products  42 us (13%)
  starting transfers between devices  41.8 us (13%)
  other arithmetic  20.6 us (6%)
  between operations  19 us (6%)
  local copies, waits for them, and re-layouts  8.93 us (3%)
    ppermute x37, waiting for transfers between devices, swap(): return lax.ppermute(value, axis, [(i, i ^ bit) for i in range(size)])  89.2 us
    pallas_call x4, Pallas kernels, gradient(): call(kernel, (steps,), in_specs, pl.BlockSpec((tile, width), rows_of_part...  52 us
    ppermute x37, starting transfers between devices, swap(): return lax.ppermute(value, axis, [(i, i ^ bit) for i in range(size)])  41.7 us
    pallas_call x2, Pallas kernels, gram_inner(): call(kernel, (steps,), [pl.BlockSpec((piece.shape[0], tile), column_index...  21.9 us
    dot_general x3, matrix products, on_device(): lax.dot_general(operand, w_up[part * step:(part + 1) * step], LAST, prefe...  21 us
    dot_general x3, matrix products, on_device(): lax.dot_general(block, w_down[part * step:(part + 1) * step], LAST, prefe...  21 us
    pallas_call x2, Pallas kernels, arrange(): call(kernel, (tiles * len(chunks),), [pl.BlockSpec((piece.shape[0], tile)...  13.4 us
    pallas_call x1, Pallas kernels, gelu_all(): call(kernel, (width // TILE,), [pl.BlockSpec((tokens, TILE), column_index...  11.7 us
  transfers between devices with their start and end apart: 38, of which 12 were waited for; matrix products, arithmetic and copies ran while one was open for 17% of the time, Pallas kernels for 25%

profile of v4, /device:TPU:0, one launch (start us, length us, event | category | flops | bytes accessed | tf_op | source)
XLA Modules:
  0.0 321.2 jit_solution(4576309519649486516)
XLA Ops:
  9.7 4.1 %collective-permute-start.3 = (bf16[80,3072]{1,0:T(8,128)(2,1)S(1)}, bf16[80,3072]{1,0:T(8,128)(2,1)S(1)}, u32[]{:S(2)}, u32[]{:S(2)}) collective-permute-start(bf16[80,3072]{1,0:T(8,128)(2,1)S(1)} %broadcast_multiply_fusion.refs_0_.refs_1_), channel_id=1, source_target_pairs={{0,16},{4,20},{8,24},{12,28},{16,0},{20,4},{24,8},{28,12},{1,17},{... | collective-permute-start | bytes 1474568 | tf_op jit(solution)/shard_map/ppermute | solution.py:21
  16.9 18.8 %collective-permute-done.3.refs_4_.refs_1_.refs_2_ = bf16[80,3072]{1,0:T(8,128)(2,1)S(1)} collective-permute-done((bf16[80,3072]{1,0:T(8,128)(2,1)S(1)}, bf16[80,3072]{1,0:T(8,128)(2,1)S(1)}, u32[]{:S(2)}, u32[]{:S(2)}) %collective-permute-start.3) | collective-permute-done | bytes 491552 | tf_op jit(solution)/shard_map/ppermute | solution.py:21
  38.4 9.7 %collective-permute-done.5.refs_6_.refs_3_.refs_4_ = bf16[80,3072]{1,0:T(8,128)(2,1)S(1)} collective-permute-done((bf16[80,3072]{1,0:T(8,128)(2,1)S(1)}, bf16[80,3072]{1,0:T(8,128)(2,1)S(1)}, u32[]{:S(2)}, u32[]{:S(2)}) %collective-permute-start.5) | collective-permute-done | bytes 491552 | tf_op jit(solution)/shard_map/ppermute | solution.py:21
  51.5 9.5 %collective-permute-done.2.refs_3_.refs_6_.refs_7_ = bf16[80,3072]{1,0:T(8,128)(2,1)S(1)} collective-permute-done((bf16[80,3072]{1,0:T(8,128)(2,1)S(1)}, bf16[80,3072]{1,0:T(8,128)(2,1)S(1)}, u32[]{:S(2)}, u32[]{:S(2)}) %collective-permute-start.2) | collective-permute-done | bytes 491552 | tf_op jit(solution)/shard_map/ppermute | solution.py:21
  61.0 9.4 %collective-permute-done.6.refs_7_.refs_8_ = bf16[80,3072]{1,0:T(8,128)(2,1)} collective-permute-done((bf16[80,3072]{1,0:T(8,128)(2,1)S(1)}, bf16[80,3072]{1,0:T(8,128)(2,1)}, u32[]{:S(2)}, u32[]{:S(2)}) %collective-permute-start.6) | collective-permute-done | bytes 491552 | tf_op jit(solution)/shard_map/ppermute | solution.py:21
  70.4 6.4 %shard_map.94 = bf16[640,3072]{1,0:T(8,128)(2,1)} custom-call(s32[2]{0:T(128)} %pad_add_fusion.flags_ref, bf16[80,3072]{1,0:T(8,128)(2,1)} %copy-done.1, bf16[80,3072]{1,0:T(8,128)(2,1)} %copy-done.3, bf16[80,3072]{1,0:T(8,128)(2,1)} %copy-done.4, bf16[80,3072]{1,0:T(8,128)(2,1)} %copy-done.7, bf16[80,3072]{1,0:T(8,128)(2,1)} %copy-done.2, ...), custom_call_target="tpu_custom_call" | custom-call | bytes 7864320 | tf_op jit(solution)/shard_map/pallas_call | solution.py:127
  76.8 7.7 %fusion.10 = f32[640,1024]{1,0:T(8,128)S(1)} fusion(bf16[640,3072]{1,0:T(8,128)(2,1)} %shard_map.94, bf16[3072,3072]{1,0:T(8,128)(2,1)} %param.13), kind=kOutput, calls=%fused_computation.10 | convolution fusion | flops 4026531840 | bytes 12845056 | tf_op jit(solution)/shard_map/dot_general | solution.py:302
  84.7 6.6 %fusion.8 = f32[640,1024]{1,0:T(8,128)S(1)} fusion(bf16[640,3072]{1,0:T(8,128)(2,1)S(1)} %copy-done.8, bf16[3072,3072]{1,0:T(8,128)(2,1)} %param.13), kind=kOutput, calls=%fused_computation.8 | convolution fusion | flops 4026531840 | bytes 12845056 | tf_op jit(solution)/shard_map/dot_general | solution.py:302
  93.1 6.6 %fusion.6 = f32[640,1024]{1,0:T(8,128)S(1)} fusion(bf16[640,3072]{1,0:T(8,128)(2,1)S(1)} %copy-done.8, bf16[3072,3072]{1,0:T(8,128)(2,1)} %param.13), kind=kOutput, calls=%fused_computation.6 | convolution fusion | flops 4026531840 | bytes 12845056 | tf_op jit(solution)/shard_map/dot_general | solution.py:302
  110.5 20.0 %collective-permute-done.10.refs_1_ = bf16[80,3072]{1,0:T(8,128)(2,1)} collective-permute-done((bf16[80,3072]{1,0:T(8,128)(2,1)S(1)}, bf16[80,3072]{1,0:T(8,128)(2,1)}, u32[]{:S(2)}, u32[]{:S(2)}) %collective-permute-start.10) | collective-permute-done | bytes 491552 | tf_op jit(solution)/shard_map/ppermute | solution.py:21
  132.7 11.7 %shard_map.95 = (bf16[640,3072]{1,0:T(8,128)(2,1)}, f32[320,3072]{1,0:T(8,128)}) custom-call(s32[2]{0:T(128)} %pad_add_fusion.flags_ref, bf16[640,3072]{1,0:T(8,128)(2,1)} %all-gather.2.cloned.1.call-done.pre_ref), custom_call_target="tpu_custom_call" | custom-call | flops 58982400 | bytes 11796480 | tf_op jit(solution)/shard_map/pallas_call | solution.py:87
  146.5 5.0 %multiply_convert_fusion = (bf16[320,1024]{1,0:T(8,128)(2,1)}, bf16[320,1024]{1,0:T(8,128)(2,1)}, bf16[320,1024]{1,0:T(8,128)(2,1)}) fusion(f32[320,3072]{1,0:T(8,128)} %get-tuple-element.28, bf16[320,1024]{1,0:T(8,128)(2,1)} %collective-permute-done.21, bf16[320,1024]{1,0:T(8,128)(2,1)S(1)} %collective-permute-done.20, f32[640,1024]{1,0:T(8,128)S(1)} %fusion.6, ...), kind=kLoop, calls=%fused_computation.24 | loop fusion | flops 5242880 | bytes 13107200 | tf_op jit(solution)/shard_map/convert_element_type | solution.py:318
  155.9 11.0 %shard_map.96 = f32[1,640]{1,0:T(1,128)} custom-call(s32[2]{0:T(128)} %pad_add_fusion.flags_ref, bf16[80,3072]{1,0:T(8,128)(2,1)} %copy-done.1, bf16[80,3072]{1,0:T(8,128)(2,1)} %copy-done.2, bf16[80,3072]{1,0:T(8,128)(2,1)} %copy-done.4, bf16[80,3072]{1,0:T(8,128)(2,1)} %copy-done.5, bf16[80,3072]{1,0:T(8,128)(2,1)} %copy-done.3, ...), custom_call_target="tpu_custom_call" | custom-call | flops 5033164800 | bytes 7864320 | tf_op jit(solution)/shard_map/pallas_call | solution.py:180
  168.2 8.2 %collective-permute-done.15.refs_7_ = bf16[80,3072]{1,0:T(8,128)(2,1)S(1)} collective-permute-done((bf16[80,3072]{1,0:T(8,128)(2,1)}, bf16[80,3072]{1,0:T(8,128)(2,1)S(1)}, u32[]{:S(2)}, u32[]{:S(2)}) %collective-permute-start.15) | collective-permute-done | bytes 491552 | tf_op jit(solution)/shard_map/ppermute | solution.py:21
  178.4 7.0 %shard_map.97.refs_8_ = bf16[640,3072]{1,0:T(8,128)(2,1)} custom-call(s32[2]{0:T(128)} %pad_add_fusion.flags_ref, bf16[320,1024]{1,0:T(8,128)(2,1)} %get-tuple-element.32.refs_0_, bf16[320,1024]{1,0:T(8,128)(2,1)} %copy-done.20, bf16[320,1024]{1,0:T(8,128)(2,1)} %get-tuple-element.46.refs_2_, bf16[320,1024]{1,0:T(8,128)(2,1)} %copy-done.19, ...), custom_call_target="tpu_custom_call" | custom-call | bytes 7864320 | tf_op jit(solution)/shard_map/pallas_call | solution.py:127
  185.4 7.8 %fusion.4 = f32[640,1024]{1,0:T(8,128)S(1)} fusion(bf16[640,3072]{1,0:T(8,128)(2,1)} %shard_map.97.refs_8_, bf16[3072,3072]{1,0:T(8,128)(2,1)} %param.12), kind=kOutput, calls=%fused_computation.4 | convolution fusion | flops 4026531840 | bytes 12845056 | tf_op jit(solution)/shard_map/dot_general | solution.py:338
  196.3 10.9 %shard_map.98 = f32[1,640]{1,0:T(1,128)} custom-call(s32[2]{0:T(128)} %pad_add_fusion.flags_ref, bf16[80,3072]{1,0:T(8,128)(2,1)} %refs_0_.2, bf16[80,3072]{1,0:T(8,128)(2,1)} %collective-permute-done.10.refs_1_, bf16[80,3072]{1,0:T(8,128)(2,1)} %collective-permute-done.11.refs_2_, bf16[80,3072]{1,0:T(8,128)(2,1)} %collective-permute-done.13.refs_3_, ...), custom_call_target="tpu_custom_call" | custom-call | flops 5033164800 | bytes 7864320 | tf_op jit(solution)/shard_map/pallas_call | solution.py:180
  220.0 6.6 %fusion.2 = f32[640,1024]{1,0:T(8,128)S(1)} fusion(bf16[640,3072]{1,0:T(8,128)(2,1)S(1)} %copy-done, bf16[3072,3072]{1,0:T(8,128)(2,1)} %param.12), kind=kOutput, calls=%fused_computation.2 | convolution fusion | flops 4026531840 | bytes 12845056 | tf_op jit(solution)/shard_map/dot_general | solution.py:338
  234.6 6.6 %fusion = f32[640,1024]{1,0:T(8,128)S(1)} fusion(bf16[640,3072]{1,0:T(8,128)(2,1)S(1)} %copy-done, bf16[3072,3072]{1,0:T(8,128)(2,1)} %param.12), kind=kOutput, calls=%fused_computation | convolution fusion | flops 4026531840 | bytes 12845056 | tf_op jit(solution)/shard_map/dot_general | solution.py:338
  244.5 4.4 %collective-permute-done.36 = f32[3]{0:T(128)S(1)} collective-permute-done((f32[3]{0:T(128)S(1)}, f32[3]{0:T(128)S(1)}, u32[]{:S(2)}, u32[]{:S(2)}) %collective-permute-start.36) | collective-permute-done | bytes 44 | tf_op jit(solution)/shard_map/ppermute | solution.py:21
  256.3 13.0 %shard_map.101.refs_9_ = bf16[3072,3072]{1,0:T(8,128)(2,1)} custom-call(s32[2]{0:T(128)} %pad_add_fusion.flags_ref, f32[1,1]{1,0:T(1,128)} %bitcast.12.scale_ref, bf16[640,3072]{1,0:T(8,128)(2,1)} %get-tuple-element.31.refs_8_.refs_0_, bf16[80,3072]{1,0:T(8,128)(2,1)} %copy-done.1, bf16[80,3072]{1,0:T(8,128)(2,1)} %copy-done.2, bf16[80,3072]{1,0:T(8,128)(2,1)} %copy-done.4, ...), custom_call_target="tpu_custom_call" | custom-call | flops 6039797760 | bytes 17301504 | tf_op jit(solution)/shard_map/pallas_call | solution.py:235
  271.3 13.1 %shard_map.102 = bf16[3072,3072]{1,0:T(8,128)(2,1)} custom-call(s32[2]{0:T(128)} %pad_add_fusion.flags_ref, f32[1,1]{1,0:T(1,128)} %bitcast.11.scale_ref, bf16[640,3072]{1,0:T(8,128)(2,1)} %get-tuple-element.31.refs_8_.refs_0_, bf16[80,3072]{1,0:T(8,128)(2,1)} %copy-done.1, bf16[80,3072]{1,0:T(8,128)(2,1)} %copy-done.2, ...), custom_call_target="tpu_custom_call", output_to_operand_aliasing={{}: (11, {})} | custom-call | flops 6039797760 | bytes 17301504 | tf_op jit(solution)/shard_map/pallas_call | solution.py:235
  287.5 13.0 %shard_map.99.refs_9_ = bf16[3072,3072]{1,0:T(8,128)(2,1)} custom-call(s32[2]{0:T(128)} %pad_add_fusion.flags_ref, f32[1,1]{1,0:T(1,128)} %bitcast.10.scale_ref, bf16[80,3072]{1,0:T(8,128)(2,1)} %refs_0_.2, bf16[80,3072]{1,0:T(8,128)(2,1)} %collective-permute-done.10.refs_1_, bf16[80,3072]{1,0:T(8,128)(2,1)} %collective-permute-done.11.refs_2_, ...), custom_call_target="tpu_custom_call" | custom-call | flops 6039797760 | bytes 17301504 | tf_op jit(solution)/shard_map/pallas_call | solution.py:235
  301.5 12.9 %shard_map.100 = bf16[3072,3072]{1,0:T(8,128)(2,1)} custom-call(s32[2]{0:T(128)} %pad_add_fusion.flags_ref, f32[1,1]{1,0:T(1,128)} %bitcast.9.scale_ref, bf16[80,3072]{1,0:T(8,128)(2,1)} %refs_0_.2, bf16[80,3072]{1,0:T(8,128)(2,1)} %collective-permute-done.10.refs_1_, ...), custom_call_target="tpu_custom_call", output_to_operand_aliasing={{}: (11, {})} | custom-call | flops 6039797760 | bytes 17301504 | tf_op jit(solution)/shard_map/pallas_call | solution.py:235
  (151 shorter events, 72.2 us)
Async XLA Ops:
  7.2 69.6 %all-gather.2.cloned.1.call-start = ((), (), s32[]{:S(2)}) async-start(), calls=%async_computation | async-start | bytes 4915200 | tf_op jit(solution)/shard_map/all_gather | solution.py:283
  9.7 26.0 %collective-permute-start.3 = (bf16[80,3072]{1,0:T(8,128)(2,1)S(1)}, bf16[80,3072]{1,0:T(8,128)(2,1)S(1)}, u32[]{:S(2)}, u32[]{:S(2)}) collective-permute-start(bf16[80,3072]{1,0:T(8,128)(2,1)S(1)} %broadcast_multiply_fusion.refs_0_.refs_1_), channel_id=1, source_target_pairs={{0,16},{4,20},{8,24},{12,28},{16,0},{20,4},{24,8},{28,12},{1,17},{... | collective-permute-start | bytes 1474568 | tf_op jit(solution)/shard_map/ppermute | solution.py:21
  13.8 21.9 %collective-permute-start = (bf16[80,3072]{1,0:T(8,128)(2,1)S(1)}, bf16[80,3072]{1,0:T(8,128)(2,1)S(1)}, u32[]{:S(2)}, u32[]{:S(2)}) collective-permute-start(bf16[80,3072]{1,0:T(8,128)(2,1)S(1)} %broadcast_multiply_fusion.refs_0_.refs_1_), channel_id=1, source_target_pairs={{0,4},{4,0},{8,12},{12,8},{16,20},{20,16},{24,28},{28,24},{1,5},{5... | collective-permute-start | bytes 1474568 | tf_op jit(solution)/shard_map/ppermute | solution.py:21
  15.3 22.5 %collective-permute-start.1 = (bf16[80,3072]{1,0:T(8,128)(2,1)S(1)}, bf16[80,3072]{1,0:T(8,128)(2,1)S(1)}, u32[]{:S(2)}, u32[]{:S(2)}) collective-permute-start(bf16[80,3072]{1,0:T(8,128)(2,1)S(1)} %broadcast_multiply_fusion.refs_0_.refs_1_), channel_id=1, source_target_pairs={{0,8},{4,12},{8,0},{12,4},{16,24},{20,28},{24,16},{28,20},{1,9},{5... | collective-permute-start | bytes 1474568 | tf_op jit(solution)/shard_map/ppermute | solution.py:21
  37.8 23.2 %collective-permute-start.2 = (bf16[80,3072]{1,0:T(8,128)(2,1)S(1)}, bf16[80,3072]{1,0:T(8,128)(2,1)S(1)}, u32[]{:S(2)}, u32[]{:S(2)}) collective-permute-start(bf16[80,3072]{1,0:T(8,128)(2,1)S(1)} %collective-permute-done.1.refs_2_.refs_3_), channel_id=1, source_target_pairs={{0,4},{4,0},{8,12},{12,8},{16,20},{20,16},{24,28},{28,24},{1,5},{5... | collective-permute-start | bytes 1474568 | tf_op jit(solution)/shard_map/ppermute | solution.py:21
  48.1 22.3 %collective-permute-start.6 = (bf16[80,3072]{1,0:T(8,128)(2,1)S(1)}, bf16[80,3072]{1,0:T(8,128)(2,1)}, u32[]{:S(2)}, u32[]{:S(2)}) collective-permute-start(bf16[80,3072]{1,0:T(8,128)(2,1)S(1)} %collective-permute-done.5.refs_6_.refs_3_.refs_4_), channel_id=1, source_target_pairs={{0,4},{4,0},{8,12},{12,8},{16,20},{20,16},{24,28},{28,24},{1,5},{5... | collective-permute-start | bytes 1474568 | tf_op jit(solution)/shard_map/ppermute | solution.py:21
  49.9 43.2 %collective-permute-start.11 = (bf16[80,3072]{1,0:T(8,128)(2,1)}, bf16[80,3072]{1,0:T(8,128)(2,1)}, u32[]{:S(2)}, u32[]{:S(2)}) collective-permute-start(bf16[80,3072]{1,0:T(8,128)(2,1)} %refs_0_.2), channel_id=1, source_target_pairs={{0,8},{4,12},{8,0},{12,4},{16,24},{20,28},{24,16},{28,20},{1,9},{5... | collective-permute-start | bytes 1474568 | tf_op jit(solution)/shard_map/ppermute | solution.py:21
  101.0 43.5 %collective-permute-start.18 = (bf16[320,1024]{1,0:T(8,128)(2,1)}, bf16[320,1024]{1,0:T(8,128)(2,1)}, u32[]{:S(2)}, u32[]{:S(2)}) collective-permute-start(bf16[320,1024]{1,0:T(8,128)(2,1)} %fusion.13), channel_id=1, source_target_pairs={{0,2},{1,3},{2,0},{3,1},{4,6},{5,7},{6,4},{7,5},{8,10},{9,11},{10,... | collective-permute-start | bytes 1966088 | tf_op jit(solution)/shard_map/ppermute | solution.py:21
  102.5 42.0 %collective-permute-start.8 = (bf16[320,1024]{1,0:T(8,128)(2,1)}, bf16[320,1024]{1,0:T(8,128)(2,1)}, u32[]{:S(2)}, u32[]{:S(2)}) collective-permute-start(bf16[320,1024]{1,0:T(8,128)(2,1)} %get-tuple-element.43), channel_id=1, source_target_pairs={{0,2},{1,3},{2,0},{3,1},{4,6},{5,7},{6,4},{7,5},{8,10},{9,11},{10,... | collective-permute-start | bytes 1966088 | tf_op jit(solution)/shard_map/ppermute | solution.py:21
  104.1 42.4 %collective-permute-start.21 = (bf16[320,1024]{1,0:T(8,128)(2,1)}, bf16[320,1024]{1,0:T(8,128)(2,1)}, u32[]{:S(2)}, u32[]{:S(2)}) collective-permute-start(bf16[320,1024]{1,0:T(8,128)(2,1)} %fusion.14), channel_id=1, source_target_pairs={{0,2},{1,3},{2,0},{3,1},{4,6},{5,7},{6,4},{7,5},{8,10},{9,11},{10,... | collective-permute-start | bytes 1966088 | tf_op jit(solution)/shard_map/ppermute | solution.py:21
  105.6 24.9 %collective-permute-start.10 = (bf16[80,3072]{1,0:T(8,128)(2,1)S(1)}, bf16[80,3072]{1,0:T(8,128)(2,1)}, u32[]{:S(2)}, u32[]{:S(2)}) collective-permute-start(bf16[80,3072]{1,0:T(8,128)(2,1)S(1)} %copy-done.9), channel_id=1, source_target_pairs={{0,16},{4,20},{8,24},{12,28},{16,0},{20,4},{24,8},{28,12},{1,17},{... | collective-permute-start | bytes 1474568 | tf_op jit(solution)/shard_map/ppermute | solution.py:21
  109.0 22.9 %collective-permute-start.9 = (bf16[80,3072]{1,0:T(8,128)(2,1)S(1)}, bf16[80,3072]{1,0:T(8,128)(2,1)S(1)}, u32[]{:S(2)}, u32[]{:S(2)}) collective-permute-start(bf16[80,3072]{1,0:T(8,128)(2,1)S(1)} %copy-done.9), channel_id=1, source_target_pairs={{0,4},{4,0},{8,12},{12,8},{16,20},{20,16},{24,28},{28,24},{1,5},{5... | collective-permute-start | bytes 1474568 | tf_op jit(solution)/shard_map/ppermute | solution.py:21
  130.5 21.5 %collective-permute-start.12 = (bf16[80,3072]{1,0:T(8,128)(2,1)}, bf16[80,3072]{1,0:T(8,128)(2,1)}, u32[]{:S(2)}, u32[]{:S(2)}) collective-permute-start(bf16[80,3072]{1,0:T(8,128)(2,1)} %collective-permute-done.11.refs_2_), channel_id=1, source_target_pairs={{0,4},{4,0},{8,12},{12,8},{16,20},{20,16},{24,28},{28,24},{1,5},{5... | collective-permute-start | bytes 1474568 | tf_op jit(solution)/shard_map/ppermute | solution.py:21
  132.7 20.7 %collective-permute-start.13 = (bf16[80,3072]{1,0:T(8,128)(2,1)}, bf16[80,3072]{1,0:T(8,128)(2,1)}, u32[]{:S(2)}, u32[]{:S(2)}) collective-permute-start(bf16[80,3072]{1,0:T(8,128)(2,1)} %collective-permute-done.10.refs_1_), channel_id=1, source_target_pairs={{0,8},{4,12},{8,0},{12,4},{16,24},{20,28},{24,16},{28,20},{1,9},{5... | collective-permute-start | bytes 1474568 | tf_op jit(solution)/shard_map/ppermute | solution.py:21
  151.5 24.9 %collective-permute-start.22 = (bf16[320,1024]{1,0:T(8,128)(2,1)}, bf16[320,1024]{1,0:T(8,128)(2,1)S(1)}, u32[]{:S(2)}, u32[]{:S(2)}) collective-permute-start(bf16[320,1024]{1,0:T(8,128)(2,1)} %get-tuple-element.45.refs_4_), channel_id=1, source_target_pairs={{0,1},{1,0},{2,3},{3,2},{4,5},{5,4},{6,7},{7,6},{8,9},{9,8},{10,11... | collective-permute-start | bytes 1966088 | tf_op jit(solution)/shard_map/ppermute | solution.py:21
  151.5 24.9 %collective-permute-start.19 = (bf16[320,1024]{1,0:T(8,128)(2,1)}, bf16[320,1024]{1,0:T(8,128)(2,1)S(1)}, u32[]{:S(2)}, u32[]{:S(2)}) collective-permute-start(bf16[320,1024]{1,0:T(8,128)(2,1)} %get-tuple-element.46.refs_2_), channel_id=1, source_target_pairs={{0,1},{1,0},{2,3},{3,2},{4,5},{5,4},{6,7},{7,6},{8,9},{9,8},{10,11... | collective-permute-start | bytes 1966088 | tf_op jit(solution)/shard_map/ppermute | solution.py:21
  152.0 24.4 %collective-permute-start.16 = (bf16[320,1024]{1,0:T(8,128)(2,1)}, bf16[320,1024]{1,0:T(8,128)(2,1)S(1)}, u32[]{:S(2)}, u32[]{:S(2)}) collective-permute-start(bf16[320,1024]{1,0:T(8,128)(2,1)} %get-tuple-element.32.refs_0_), channel_id=1, source_target_pairs={{0,1},{1,0},{2,3},{3,2},{4,5},{5,4},{6,7},{7,6},{8,9},{9,8},{10,11... | collective-permute-start | bytes 1966088 | tf_op jit(solution)/shard_map/ppermute | solution.py:21
  152.0 16.2 %collective-permute-start.14 = (bf16[80,3072]{1,0:T(8,128)(2,1)}, bf16[80,3072]{1,0:T(8,128)(2,1)S(1)}, u32[]{:S(2)}, u32[]{:S(2)}) collective-permute-start(bf16[80,3072]{1,0:T(8,128)(2,1)} %collective-permute-done.10.refs_1_), channel_id=1, source_target_pairs={{0,4},{4,0},{8,12},{12,8},{16,20},{20,16},{24,28},{28,24},{1,5},{5... | collective-permute-start | bytes 1474568 | tf_op jit(solution)/shard_map/ppermute | solution.py:21
  153.4 22.9 %collective-permute-start.15 = (bf16[80,3072]{1,0:T(8,128)(2,1)}, bf16[80,3072]{1,0:T(8,128)(2,1)S(1)}, u32[]{:S(2)}, u32[]{:S(2)}) collective-permute-start(bf16[80,3072]{1,0:T(8,128)(2,1)} %collective-permute-done.13.refs_3_), channel_id=1, source_target_pairs={{0,4},{4,0},{8,12},{12,8},{16,20},{20,16},{24,28},{28,24},{1,5},{5... | collective-permute-start | bytes 1474568 | tf_op jit(solution)/shard_map/ppermute | solution.py:21
  194.8 23.4 %collective-permute-start.23 = (bf16[320,1024]{1,0:T(8,128)(2,1)S(1)}, bf16[320,1024]{1,0:T(8,128)(2,1)}, u32[]{:S(2)}, u32[]{:S(2)}) collective-permute-start(bf16[320,1024]{1,0:T(8,128)(2,1)S(1)} %slice.229), channel_id=1, source_target_pairs={{0,4},{4,0},{8,12},{12,8},{16,20},{20,16},{24,28},{28,24},{1,5},{5... | collective-permute-start | bytes 1966088 | tf_op jit(solution)/shard_map/ppermute | solution.py:21
  229.1 24.1 %collective-permute-start.28 = (bf16[320,1024]{1,0:T(8,128)(2,1)}, bf16[320,1024]{1,0:T(8,128)(2,1)}, u32[]{:S(2)}, u32[]{:S(2)}) collective-permute-start(bf16[320,1024]{1,0:T(8,128)(2,1)} %slice.228), channel_id=1, source_target_pairs={{0,4},{4,0},{8,12},{12,8},{16,20},{20,16},{24,28},{28,24},{1,5},{5... | collective-permute-start | bytes 1966088 | tf_op jit(solution)/shard_map/ppermute | solution.py:21
  231.2 20.4 %collective-permute-start.25 = (bf16[80,1024]{1,0:T(8,128)(2,1)S(1)}, bf16[80,1024]{1,0:T(8,128)(2,1)}, u32[]{:S(2)}, u32[]{:S(2)}) collective-permute-start(bf16[80,1024]{1,0:T(8,128)(2,1)S(1)} %slice.238), channel_id=1, source_target_pairs={{0,16},{4,20},{8,24},{12,28},{16,0},{20,4},{24,8},{28,12},{1,17},{... | collective-permute-start | bytes 491528 | tf_op jit(solution)/shard_map/ppermute | solution.py:21
  243.8 25.5 %collective-permute-start.31 = (bf16[320,1024]{1,0:T(8,128)(2,1)}, bf16[320,1024]{1,0:T(8,128)(2,1)}, u32[]{:S(2)}, u32[]{:S(2)}) collective-permute-start(bf16[320,1024]{1,0:T(8,128)(2,1)} %slice.227), channel_id=1, source_target_pairs={{0,4},{4,0},{8,12},{12,8},{16,20},{20,16},{24,28},{28,24},{1,5},{5... | collective-permute-start | bytes 1966088 | tf_op jit(solution)/shard_map/ppermute | solution.py:21
  254.6 16.5 %collective-permute-start.29 = (bf16[160,1024]{1,0:T(8,128)(2,1)S(1)}, bf16[160,1024]{1,0:T(8,128)(2,1)S(1)}, u32[]{:S(2)}, u32[]{:S(2)}) collective-permute-start(bf16[160,1024]{1,0:T(8,128)(2,1)S(1)} %slice.234), channel_id=1, source_target_pairs={{0,8},{4,12},{8,0},{12,4},{16,24},{20,28},{24,16},{28,20},{1,9},{5... | collective-permute-start | bytes 983048 | tf_op jit(solution)/shard_map/ppermute | solution.py:21
  (36 other events, 444.5 us)
Sparse Core Ops, SparseCore 0:
  9.6 35.6 all-gather.1

commit v5 on v4

v5 whole, which is shorter than its diff:
```python
import math

import jax
import jax.numpy as jnp
from jax import lax
from jax.experimental import pallas as pl
from jax.experimental.pallas import tpu as pltpu
from jax.sharding import PartitionSpec as P

F32 = jnp.float32
BF16 = jnp.bfloat16
LAST = (((1,), (1,)), ((), ()))
FIRST = (((0,), (0,)), ((), ()))
FACTOR = math.sqrt(2.0 / math.pi)
TILE = 256
VMEM_LIMIT = 56 * 1024 * 1024


def swap(value, axis, bit):
    size = lax.axis_size(axis)
    return lax.ppermute(value, axis, [(i, i ^ bit) for i in range(size)])


def bits_of(size):
    return [1 << i for i in range(size.bit_length() - 1)]


def turned(index, size):
    return sum(((index // bit) % 2) * (size // 2 // bit) for bit in bits_of(size))


def call(kernel, grid, in_specs, out_specs, out_shape, scratch, cost, aliases=None):
    flops, moved, slow = cost
    return pl.pallas_call(
        kernel,
        grid_spec=pltpu.PrefetchScalarGridSpec(
            num_scalar_prefetch=1,
            grid=grid,
            in_specs=in_specs,
            out_specs=out_specs,
            scratch_shapes=scratch,
        ),
        out_shape=out_shape,
        input_output_aliases=aliases or {},
        compiler_params=pltpu.CompilerParams(
            dimension_semantics=("arbitrary",), vmem_limit_bytes=VMEM_LIMIT
        ),
        cost_estimate=pl.CostEstimate(
            flops=flops, bytes_accessed=moved, transcendentals=slow
        ),
    )


def whole_index(i, flags):
    return (0, 0)


def column_index(i, flags):
    return (0, i)


def aligned(start):
    return pl.multiple_of(start, 16)


def token_place(side, order, core, per_group):
    group, k = order // per_group, order % per_group
    return (2 * group + (side ^ core)) * per_group + k


def gelu_all(pre_all, flags, n_row, per_group, rows):
    tokens, width = pre_all.shape
    slots = n_row // 2

    def kernel(flags_ref, pre_ref, act_ref, slope_ref):
        row, core = flags_ref[0], flags_ref[1]
        for source in range(n_row):
            index = row ^ source
            hval = pre_ref[source * rows : (source + 1) * rows, :].astype(F32)
            tanh_part = jnp.tanh(FACTOR * (hval + 0.044715 * hval * hval * hval))
            order = turned(index // 2, slots)
            place = token_place(index % 2, order, core, per_group)
            act_ref[pl.ds(aligned(place * rows), rows), :] = (
                0.5 * hval * (1.0 + tanh_part)
            ).astype(BF16)

            @pl.when(index % 2 == core)
            def _():
                slope_ref[pl.ds(aligned(order * rows), rows), :] = 0.5 * (
                    1.0 + tanh_part
                ) + 0.5 * hval * (1.0 - tanh_part * tanh_part) * FACTOR * (
                    1.0 + 3.0 * 0.044715 * hval * hval
                )

    return call(
        kernel,
        (width // TILE,),
        [pl.BlockSpec((tokens, TILE), column_index)],
        [
            pl.BlockSpec((tokens, TILE), column_index),
            pl.BlockSpec((tokens // 2, TILE), column_index),
        ],
        [
            jax.ShapeDtypeStruct((tokens, width), BF16),
            jax.ShapeDtypeStruct((tokens // 2, width), F32),
        ],
        [],
        (30 * tokens * width, 6 * tokens * width, tokens * width),
    )(flags, pre_all)


def arrange(pieces, places, rows, flags):
    width = pieces[0].shape[1]
    tokens = sum(piece.shape[0] for piece in pieces)
    tile = 2 * TILE if width % (2 * TILE) == 0 else TILE

    def kernel(flags_ref, *refs):
        for ref, place in zip(refs, places):
            refs[-1][pl.ds(aligned(place(flags_ref[1]) * rows), rows), :] = ref[...]

    return call(
        kernel,
        (width // tile,),
        [pl.BlockSpec((rows, tile), column_index)] * len(pieces),
        pl.BlockSpec((tokens, tile), column_index),
        jax.ShapeDtypeStruct((tokens, width), BF16),
        [],
        (0, 4 * tokens * width, 0),
    )(flags, *pieces)


def gram_inner(left, right, flags):
    tokens, width = left.shape
    tile = 2 * TILE if width % (2 * TILE) == 0 else TILE
    steps = width // tile

    def kernel(flags_ref, left_ref, right_ref, out_ref, left_gram, right_gram):
        step = pl.program_id(0)

        @pl.when(step == 0)
        def _():
            left_gram[...] = jnp.zeros_like(left_gram)
            right_gram[...] = jnp.zeros_like(right_gram)

        for ref, total in ((left_ref, left_gram), (right_ref, right_gram)):
            total[...] += lax.dot_general(
                ref[...], ref[...], LAST, preferred_element_type=F32
            )

        @pl.when(step == steps - 1)
        def _():
            out_ref[...] = jnp.sum(left_gram[...] * right_gram[...], axis=0, keepdims=True)

    out = call(
        kernel,
        (steps,),
        [pl.BlockSpec((tokens, tile), column_index)] * 2,
        pl.BlockSpec((1, tokens), whole_index),
        jax.ShapeDtypeStruct((1, tokens), F32),
        [pltpu.VMEM((tokens, tokens), F32)] * 2,
        (4 * tokens * tokens * width, 4 * tokens * width, 0),
    )(flags, left, right)
    return jnp.sum(out)


def after(value, *events):
    return lax.optimization_barrier((value, *events))[0]


def on_device(inputs, pre_act, out_grad, token_valid, poison, w_up, w_down):
    n_row = lax.axis_size("row")
    n_col = lax.axis_size("col")
    rows = inputs.shape[0]
    tokens = rows * n_row
    slots = n_row // 2
    row, col = lax.axis_index("row"), lax.axis_index("col")
    core = col % 2
    flags = jnp.stack([row, core]).astype(jnp.int32)
    row_bits, col_bits = bits_of(n_row), bits_of(n_col)

    def exchange(own, x_own):
        blocks = {0: own, 1: swap(x_own, "row", 1)}
        for bit in reversed(row_bits[1:]):
            for index in sorted(blocks):
                if index % 2 == 0:
                    source = own if index == 0 else after(blocks[index], blocks[1], blocks[bit])
                    blocks[index | bit] = swap(source, "row", bit)
        even = [index for index in sorted(blocks) if index % 2 == 0 and index > 0]
        for index in even:
            if not index & 2:
                blocks[index | 1] = swap(blocks[index], "row", 1)
        last = max(index for index in blocks if index & 1)
        for index in even:
            if index & 2:
                blocks[index | 1] = swap(after(blocks[index], blocks[last]), "row", 1)
        return [blocks[index] for index in range(n_row)]

    groups = 2 if slots % 2 == 0 else 1
    per_group = slots // groups
    count = per_group * rows
    by_group = [[] for _ in range(groups)]
    for index in range(n_row):
        by_group[turned(index // 2, slots) // per_group].append(index)

    def place_of(index, group):
        order = turned(index // 2, slots)
        return lambda core: token_place(index % 2, order, core, per_group) - (
            group * 2 * per_group
        )

    pre_all = lax.all_gather(pre_act, "col", axis=0, tiled=True)
    own = out_grad * token_valid.astype(BF16)[:, None]
    masked = exchange(own, own)
    own = after(inputs, masked[-2])
    inputs_blocks = exchange(own, after(own, masked[-1]))

    blocks, totals = [], []
    for group, indices in enumerate(by_group):
        block = arrange(
            [masked[index] for index in indices],
            [place_of(index, group) for index in indices],
            rows,
            flags,
        )
        blocks.append(block)
        block = after(block, masked[-2], pre_all, *totals)
        partial = lax.dot_general(block, w_down, LAST, preferred_element_type=F32)
        send = partial[count:].astype(BF16)
        if group == 0:
            send = after(send, *[masked[index] for index in by_group[-1] if index & 1])
        other = swap(send, "col", 1)
        totals.append(partial[:count] + other.astype(F32))
    act, slope = gelu_all(
        after(pre_all, *totals, inputs_blocks[1], inputs_blocks[2], inputs_blocks[n_row // 2]),
        flags,
        n_row,
        per_group,
        rows,
    )
    masked_all = jnp.concatenate(blocks, axis=0)
    square_down = gram_inner(
        masked_all, after(act, inputs_blocks[n_row // 2 + 1], inputs_blocks[-2]), flags
    )
    inputs_all = arrange(
        [after(inputs_blocks[0], square_down)] + inputs_blocks[1:],
        [place_of(index, 0) for index in range(n_row)],
        rows,
        flags,
    )
    hidden_blocks = []
    for group, total in enumerate(totals):
        for bit in col_bits[1:]:
            total = total + swap(total.astype(BF16), "col", bit).astype(F32)
        hidden = (total * slope[group * count : (group + 1) * count]).astype(BF16)
        hidden_blocks += [hidden, swap(hidden, "col", 1)]
    hidden_blocks[-1] = after(hidden_blocks[-1], inputs_all)
    hidden_all = jnp.concatenate(hidden_blocks, axis=0)

    square_up = gram_inner(inputs_all, hidden_all, flags)
    flag_value = poison[0, 0].astype(F32)
    keep_block = 1.0 - flag_value
    count_term = jnp.where(col == 0, jnp.sum(token_valid.astype(F32)), 0.0)
    scalars = jnp.stack([count_term, keep_block * (square_down + square_up), flag_value])
    hops = [("col", bit) for bit in col_bits] + [("row", bit) for bit in row_bits]

    def sides(product):
        split = product.reshape(groups, 2, count, product.shape[1])
        return [
            lax.dynamic_index_in_dim(split, side, 1, keepdims=False).reshape(
                groups * count, product.shape[1]
            )
            for side in (core, 1 - core)
        ]

    model = w_up.shape[0]
    parts = 3 if model % (3 * TILE) == 0 else 1
    step = model // parts
    stages = []
    operand = after(hidden_all, square_up)
    for part in range(parts):
        product = lax.dot_general(
            operand, w_up[part * step : (part + 1) * step], LAST, preferred_element_type=F32
        )
        mine, theirs = sides(product)
        total = mine + swap(theirs.astype(BF16), "row", 1).astype(F32)
        stages.append([total])
        for bit in row_bits[1:]:
            split = total.shape[0] // 2
            total = total[:split] + swap(total[split:].astype(BF16), "row", bit).astype(F32)
            stages[-1].append(total)
        axis, bit = hops.pop(0)
        scalars = scalars + swap(scalars, axis, bit)
        operand = after(operand, scalars)
        scalars = after(scalars, product)
    for axis, bit in hops:
        scalars = scalars + swap(scalars, axis, bit)
    count_all, square_all, flag_all = scalars[0], jnp.maximum(scalars[1], 0.0), scalars[2]

    token_total = jnp.maximum(count_all, 1.0)
    squares = square_all / (token_total * token_total)
    block_count = float(n_row * n_col)
    estimate = squares * block_count / jnp.maximum(block_count - flag_all, 1.0)
    limit = 0.25 * math.sqrt(
        (w_up.shape[1] * n_row) * (w_up.shape[0] * n_col) / tokens
    )
    clip_factor = jnp.minimum(1.0, limit / jnp.sqrt(estimate + 1e-06))
    scale = keep_block * clip_factor / token_total

    def gradient(left, right, scale):
        product = lax.dot_general(left, right, FIRST, preferred_element_type=F32)
        return (product * scale).astype(BF16)

    grad_down = gradient(act, masked_all, after(scale, stages[0][0]))
    events = [stage[0] for stage in stages] + [stages[0][1], grad_down]
    grad_up = gradient(inputs_all, hidden_all, after(scale, *events))
    input_sum = jnp.concatenate([stage[-1] for stage in stages], axis=1)
    return (input_sum / token_total).astype(BF16), grad_up, grad_down


def solution(mesh):
    placed = (
        P("row", "col"),
        P("col", "row"),
        P("row", "col"),
        P("row"),
        P("row", "col"),
        P("col", "row"),
        P("row", "col"),
    )
    return jax.shard_map(
        on_device,
        mesh=mesh,
        in_specs=placed,
        out_specs=(P("row", "col"), P("col", "row"), P("row", "col")),
        check_vma=False,
    )
```

time: 323 us -> 317 us (0.981)
  Pallas kernels: 99.1 us -> 50.2 us
  matrix products: 42 us -> 81.5 us
  other arithmetic: 20.6 us -> 30.4 us
  waiting for transfers between devices: 89.9 us -> 80.2 us
  starting transfers between devices: 41.8 us -> 47.1 us
    pallas_call x8 -> x5, Pallas kernels: 87.3 us -> 38.6 us  [the longest x2 20.9 us: gram_inner(): call(kernel, (steps,), [pl.BlockSpec((tokens, tile), column_index)] * 2,...]
    dot_general x3 -> x4, matrix products: 21 us -> 60.7 us  [the longest x2 39.8 us: gradient(): product = lax.dot_general(left, right, FIRST, preferred_element_type=F32)]
    concatenate x0 -> x2, other arithmetic: none -> 10.8 us  [the longest x1 6.5 us: on_device(): hidden_all = jnp.concatenate(hidden_blocks, axis=0)]
    ppermute x37 -> x34, waiting for transfers between devices: 89.2 us -> 79.5 us  [swap(): return lax.ppermute(value, axis, [(i, i ^ bit) for i in range(size)])]
    unnamed x44 -> x46, local copies, waits for them, and re-layouts: 5.78 us -> 0.46 us
    ppermute x37 -> x34, starting transfers between devices: 41.7 us -> 47 us  [swap(): return lax.ppermute(value, axis, [(i, i ^ bit) for i in range(size)])]
  transfers between devices with their start and end apart: 38 -> 35, of which waited for: 12 -> 13; matrix products, arithmetic and copies ran while one was open for 17% -> 31% of each run, Pallas kernels for 25% -> 13%
where the time goes in v5:
time: 317 us; the launch traced here: 315 us
  matrix products  81.5 us (26%)
  waiting for transfers between devices  80.2 us (25%)
  Pallas kernels  50.2 us (16%)
  starting transfers between devices  47.1 us (15%)
  other arithmetic  30.4 us (10%)
  between operations  19.1 us (6%)
  local copies, waits for them, and re-layouts  6.92 us (2%)
    ppermute x34, waiting for transfers between devices, swap(): return lax.ppermute(value, axis, [(i, i ^ bit) for i in range(size)])  79.5 us
    ppermute x34, starting transfers between devices, swap(): return lax.ppermute(value, axis, [(i, i ^ bit) for i in range(size)])  47 us
    dot_general x2, matrix products, gradient(): product = lax.dot_general(left, right, FIRST, preferred_element_type=F32)  39.8 us
    dot_general x2, matrix products, on_device(): partial = lax.dot_general(block, w_down, LAST, preferred_element_type=F32)  21 us
    pallas_call x2, Pallas kernels, gram_inner(): call(kernel, (steps,), [pl.BlockSpec((tokens, tile), column_index)] * 2,...  20.9 us
    dot_general x3, matrix products, on_device(): lax.dot_general(operand, w_up[part * step:(part + 1) * step], LAST, prefe...  20.8 us
    pallas_call x3, Pallas kernels, arrange(): call(kernel, (width // tile,), [pl.BlockSpec((rows, tile), column_index)]...  17.8 us
    pallas_call x1, Pallas kernels, gelu_all(): call(kernel, (width // TILE,), [pl.BlockSpec((tokens, TILE), column_index...  11.6 us
  transfers between devices with their start and end apart: 35, of which 13 were waited for; matrix products, arithmetic and copies ran while one was open for 31% of the time, Pallas kernels for 13%

profile of v5, /device:TPU:0, one launch (start us, length us, event | category | flops | bytes accessed | tf_op | source)
XLA Modules:
  0.0 315.4 jit_solution(18430582570598281302)
XLA Ops:
  9.7 4.1 %collective-permute-start.1 = (bf16[80,3072]{1,0:T(8,128)(2,1)S(1)}, bf16[80,3072]{1,0:T(8,128)(2,1)S(1)}, u32[]{:S(2)}, u32[]{:S(2)}) collective-permute-start(bf16[80,3072]{1,0:T(8,128)(2,1)S(1)} %broadcast_multiply_fusion.refs_0_), channel_id=1, source_target_pairs={{0,16},{4,20},{8,24},{12,28},{16,0},{20,4},{24,8},{28,12},{1,17},{... | collective-permute-start | bytes 1474568 | tf_op jit(solution)/shard_map/ppermute | solution.py:21
  16.9 18.8 %collective-permute-done.1.refs_2_ = bf16[80,3072]{1,0:T(8,128)(2,1)S(1)} collective-permute-done((bf16[80,3072]{1,0:T(8,128)(2,1)S(1)}, bf16[80,3072]{1,0:T(8,128)(2,1)S(1)}, u32[]{:S(2)}, u32[]{:S(2)}) %collective-permute-start.1) | collective-permute-done | bytes 491552 | tf_op jit(solution)/shard_map/ppermute | solution.py:21
  38.5 9.5 %collective-permute-done.2.refs_3_ = bf16[80,3072]{1,0:T(8,128)(2,1)S(1)} collective-permute-done((bf16[80,3072]{1,0:T(8,128)(2,1)S(1)}, bf16[80,3072]{1,0:T(8,128)(2,1)S(1)}, u32[]{:S(2)}, u32[]{:S(2)}) %collective-permute-start.2) | collective-permute-done | bytes 491552 | tf_op jit(solution)/shard_map/ppermute | solution.py:21
  50.1 5.6 %shard_map.94 = bf16[320,3072]{1,0:T(8,128)(2,1)} custom-call(s32[2]{0:T(128)} %pad_add_fusion.flags_ref, bf16[80,3072]{1,0:T(8,128)(2,1)} %copy-done.9, bf16[80,3072]{1,0:T(8,128)(2,1)} %copy-done.18, bf16[80,3072]{1,0:T(8,128)(2,1)} %copy-done.16, bf16[80,3072]{1,0:T(8,128)(2,1)} %copy-done.20), custom_call_target="tpu_custom_call" | custom-call | bytes 3932160 | tf_op jit(solution)/shard_map/pallas_call | solution.py:121
  55.7 10.8 %fusion.10 = f32[320,3072]{1,0:T(8,128)S(1)} fusion(bf16[320,3072]{1,0:T(8,128)(2,1)} %shard_map.94, bf16[3072,3072]{1,0:T(8,128)(2,1)} %param.13), kind=kOutput, calls=%fused_computation.46 | convolution fusion | flops 6039797760 | bytes 24772608 | tf_op jit(solution)/shard_map/dot_general | solution.py:227
  70.1 5.6 %shard_map.95 = bf16[320,3072]{1,0:T(8,128)(2,1)} custom-call(s32[2]{0:T(128)} %pad_add_fusion.flags_ref, bf16[80,3072]{1,0:T(8,128)(2,1)} %copy-done.15, bf16[80,3072]{1,0:T(8,128)(2,1)} %copy-done.21, bf16[80,3072]{1,0:T(8,128)(2,1)} %copy-done.17, bf16[80,3072]{1,0:T(8,128)(2,1)} %collective-permute-done.6.refs_3_), custom_call_target="tpu_custom_call" | custom-call | bytes 3932160 | tf_op jit(solution)/shard_map/pallas_call | solution.py:121
  77.6 10.2 %fusion.11 = f32[320,3072]{1,0:T(8,128)S(1)} fusion(bf16[320,3072]{1,0:T(8,128)(2,1)S(1)} %copy-done.2, bf16[3072,3072]{1,0:T(8,128)(2,1)} %param.13), kind=kOutput, calls=%fused_computation.47 | convolution fusion | flops 6039797760 | bytes 24772608 | tf_op jit(solution)/shard_map/dot_general | solution.py:227
  94.2 5.7 %collective-permute-start.11 = (bf16[80,3072]{1,0:T(8,128)(2,1)S(1)}, bf16[80,3072]{1,0:T(8,128)(2,1)}, u32[]{:S(2)}, u32[]{:S(2)}) collective-permute-start(bf16[80,3072]{1,0:T(8,128)(2,1)S(1)} %copy-done.14), channel_id=1, source_target_pairs={{0,8},{4,12},{8,0},{12,4},{16,24},{20,28},{24,16},{28,20},{1,9},{5... | collective-permute-start | bytes 1474568 | tf_op jit(solution)/shard_map/ppermute | solution.py:21
  102.0 16.5 %collective-permute-done.12.refs_4_ = bf16[80,3072]{1,0:T(8,128)(2,1)} collective-permute-done((bf16[80,3072]{1,0:T(8,128)(2,1)S(1)}, bf16[80,3072]{1,0:T(8,128)(2,1)}, u32[]{:S(2)}, u32[]{:S(2)}) %collective-permute-start.12) | collective-permute-done | bytes 491552 | tf_op jit(solution)/shard_map/ppermute | solution.py:21
  120.0 11.6 %shard_map.96 = (bf16[640,3072]{1,0:T(8,128)(2,1)}, f32[320,3072]{1,0:T(8,128)}) custom-call(s32[2]{0:T(128)} %pad_add_fusion.flags_ref, bf16[640,3072]{1,0:T(8,128)(2,1)} %all-gather.2.cloned.1.call-done.pre_ref), custom_call_target="tpu_custom_call" | custom-call | flops 58982400 | bytes 11796480 | tf_op jit(solution)/shard_map/pallas_call | solution.py:95
  133.4 4.6 %multiply_convert_fusion.3 = (bf16[160,3072]{1,0:T(8,128)(2,1)S(1)}, bf16[160,3072]{1,0:T(8,128)(2,1)}) fusion(f32[320,3072]{1,0:T(8,128)} %get-tuple-element.37, f32[160,3072]{1,0:T(8,128)S(1)} %get-tuple-element.54, bf16[160,3072]{1,0:T(8,128)(2,1)} %collective-permute-done.8, f32[160,3072]{1,0:T(8,128)S(1)} %copy-done, ...), kind=kLoop, calls=%fused_computation.15 | loop fusion | flops 3932160 | bytes 11796480 | tf_op jit(solution)/shard_map/convert_element_type | solution.py:254
  141.9 4.3 %pad_maximum_fusion.left_ref = bf16[640,3072]{1,0:T(8,128)(2,1)} fusion(bf16[320,3072]{1,0:T(8,128)(2,1)} %shard_map.95, bf16[320,3072]{1,0:T(8,128)(2,1)} %shard_map.94), kind=kLoop, calls=%fused_computation.8 | loop fusion | flops 7864320 | bytes 7864320 | tf_op jit(solution)/shard_map/concatenate | solution.py:240
  146.2 10.4 %shard_map.97 = f32[1,640]{1,0:T(1,128)} custom-call(s32[2]{0:T(128)} %pad_add_fusion.flags_ref, bf16[640,3072]{1,0:T(8,128)(2,1)} %pad_maximum_fusion.left_ref, bf16[640,3072]{1,0:T(8,128)(2,1)} %get-tuple-element.40.right_ref), custom_call_target="tpu_custom_call" | custom-call | flops 5033164800 | bytes 7864320 | tf_op jit(solution)/shard_map/pallas_call | solution.py:154
  158.0 5.8 %collective-permute-done.19.refs_7_ = bf16[80,3072]{1,0:T(8,128)(2,1)} collective-permute-done((bf16[80,3072]{1,0:T(8,128)(2,1)S(1)}, bf16[80,3072]{1,0:T(8,128)(2,1)}, u32[]{:S(2)}, u32[]{:S(2)}) %collective-permute-start.19) | collective-permute-done | bytes 491552 | tf_op jit(solution)/shard_map/ppermute | solution.py:21
  163.8 6.5 %shard_map.98.left_ref = bf16[640,3072]{1,0:T(8,128)(2,1)} custom-call(s32[2]{0:T(128)} %pad_add_fusion.flags_ref, bf16[80,3072]{1,0:T(8,128)(2,1)} %refs_0_, bf16[80,3072]{1,0:T(8,128)(2,1)} %collective-permute-done.10.refs_1_, bf16[80,3072]{1,0:T(8,128)(2,1)} %collective-permute-done.11.refs_2_, bf16[80,3072]{1,0:T(8,128)(2,1)} %collective-permute-done.18.refs_3_, ...), custom_call_target="tpu_custom_call" | custom-call | bytes 7864320 | tf_op jit(solution)/shard_map/pallas_call | solution.py:121
  170.4 6.5 %pad_maximum_fusion.1.right_ref = bf16[640,3072]{1,0:T(8,128)(2,1)} fusion(bf16[160,3072]{1,0:T(8,128)(2,1)S(1)} %collective-permute-done.15, bf16[160,3072]{1,0:T(8,128)(2,1)} %get-tuple-element.58, bf16[160,3072]{1,0:T(8,128)(2,1)S(1)} %collective-permute-done.13, bf16[160,3072]{1,0:T(8,128)(2,1)S(1)} %get-tuple-element.57), kind=kLoop, calls=%fused_computation.9 | loop fusion | flops 15728640 | bytes 7864320 | tf_op jit(solution)/shard_map/concatenate | solution.py:257
  176.9 10.4 %shard_map.99 = f32[1,640]{1,0:T(1,128)} custom-call(s32[2]{0:T(128)} %pad_add_fusion.flags_ref, bf16[640,3072]{1,0:T(8,128)(2,1)} %shard_map.98.left_ref, bf16[640,3072]{1,0:T(8,128)(2,1)} %pad_maximum_fusion.1.right_ref), custom_call_target="tpu_custom_call" | custom-call | flops 5033164800 | bytes 7864320 | tf_op jit(solution)/shard_map/pallas_call | solution.py:154
  189.9 7.6 %fusion.4 = f32[640,1024]{1,0:T(8,128)S(1)} fusion(bf16[640,3072]{1,0:T(8,128)(2,1)} %pad_maximum_fusion.1.right_ref, bf16[3072,3072]{1,0:T(8,128)(2,1)} %param.12), kind=kOutput, calls=%fused_computation.6 | convolution fusion | flops 4026531840 | bytes 12845056 | tf_op jit(solution)/shard_map/dot_general | solution.py:281
  199.8 6.6 %fusion.2 = f32[640,1024]{1,0:T(8,128)S(1)} fusion(bf16[640,3072]{1,0:T(8,128)(2,1)S(1)} %copy-done.6, bf16[3072,3072]{1,0:T(8,128)(2,1)} %param.12), kind=kOutput, calls=%fused_computation.4 | convolution fusion | flops 4026531840 | bytes 12845056 | tf_op jit(solution)/shard_map/dot_general | solution.py:281
  213.1 6.6 %fusion = f32[640,1024]{1,0:T(8,128)S(1)} fusion(bf16[640,3072]{1,0:T(8,128)(2,1)S(1)} %copy-done.6, bf16[3072,3072]{1,0:T(8,128)(2,1)} %param.12), kind=kOutput, calls=%fused_computation.2 | convolution fusion | flops 4026531840 | bytes 12845056 | tf_op jit(solution)/shard_map/dot_general | solution.py:281
  224.0 6.5 %collective-permute-done.31 = f32[3]{0:T(128)S(1)} collective-permute-done((f32[3]{0:T(128)S(1)}, f32[3]{0:T(128)S(1)}, u32[]{:S(2)}, u32[]{:S(2)}) %collective-permute-start.31) | collective-permute-done | bytes 44 | tf_op jit(solution)/shard_map/ppermute | solution.py:21
  245.4 20.4 %multiply_convert_fusion.1 = bf16[3072,3072]{1,0:T(8,128)(2,1)} fusion(f32[]{:T(128)S(6)} %div.23, bf16[640,3072]{1,0:T(8,128)(2,1)} %get-tuple-element.40.right_ref, bf16[320,3072]{1,0:T(8,128)(2,1)} %shard_map.95, bf16[320,3072]{1,0:T(8,128)(2,1)S(1)} %copy-done.1), kind=kOutput, calls=%fused_computation.1 | convolution fusion | flops 12106334208 | bytes 26738692 | tf_op jit(solution)/shard_map/dot_general | solution.py:310
  274.1 19.3 %multiply_convert_fusion = bf16[3072,3072]{1,0:T(8,128)(2,1)} fusion(f32[]{:T(128)S(6)} %div.23, bf16[640,3072]{1,0:T(8,128)(2,1)S(1)} %copy-done.5, bf16[160,3072]{1,0:T(8,128)(2,1)S(1)} %copy-done.13, bf16[160,3072]{1,0:T(8,128)(2,1)} %get-tuple-element.58, bf16[160,3072]{1,0:T(8,128)(2,1)S(1)} %copy-done.11, bf16[160,3072]{1,0:T(8,128)(2,1)S(1)} %copy-done.8), kind=kOutput, calls=%fused_computation | convolution fusion | flops 12114198528 | bytes 26738692 | tf_op jit(solution)/shard_map/dot_general | solution.py:310
  296.8 8.4 %collective-permute-done.26 = bf16[80,1024]{1,0:T(8,128)(2,1)S(1)} collective-permute-done((bf16[80,1024]{1,0:T(8,128)(2,1)S(1)}, bf16[80,1024]{1,0:T(8,128)(2,1)S(1)}, u32[]{:S(2)}, u32[]{:S(2)}) %collective-permute-start.26) | collective-permute-done | bytes 163872 | tf_op jit(solution)/shard_map/ppermute | solution.py:21
  (148 shorter events, 74.0 us)
Async XLA Ops:
  7.2 48.5 %all-gather.2.cloned.1.call-start = ((), (), s32[]{:S(2)}) async-start(), calls=%async_computation | async-start | bytes 4915200 | tf_op jit(solution)/shard_map/all_gather | solution.py:211
  9.7 26.0 %collective-permute-start.1 = (bf16[80,3072]{1,0:T(8,128)(2,1)S(1)}, bf16[80,3072]{1,0:T(8,128)(2,1)S(1)}, u32[]{:S(2)}, u32[]{:S(2)}) collective-permute-start(bf16[80,3072]{1,0:T(8,128)(2,1)S(1)} %broadcast_multiply_fusion.refs_0_), channel_id=1, source_target_pairs={{0,16},{4,20},{8,24},{12,28},{16,0},{20,4},{24,8},{28,12},{1,17},{... | collective-permute-start | bytes 1474568 | tf_op jit(solution)/shard_map/ppermute | solution.py:21
  13.8 23.4 %collective-permute-start.3 = (bf16[80,3072]{1,0:T(8,128)(2,1)S(1)}, bf16[80,3072]{1,0:T(8,128)(2,1)S(1)}, u32[]{:S(2)}, u32[]{:S(2)}) collective-permute-start(bf16[80,3072]{1,0:T(8,128)(2,1)S(1)} %broadcast_multiply_fusion.refs_0_), channel_id=1, source_target_pairs={{0,8},{4,12},{8,0},{12,4},{16,24},{20,28},{24,16},{28,20},{1,9},{5... | collective-permute-start | bytes 1474568 | tf_op jit(solution)/shard_map/ppermute | solution.py:21
  15.4 21.8 %collective-permute-start = (bf16[80,3072]{1,0:T(8,128)(2,1)S(1)}, bf16[80,3072]{1,0:T(8,128)(2,1)S(1)}, u32[]{:S(2)}, u32[]{:S(2)}) collective-permute-start(bf16[80,3072]{1,0:T(8,128)(2,1)S(1)} %broadcast_multiply_fusion.refs_0_), channel_id=1, source_target_pairs={{0,4},{4,0},{8,12},{12,8},{16,20},{20,16},{24,28},{28,24},{1,5},{5... | collective-permute-start | bytes 1474568 | tf_op jit(solution)/shard_map/ppermute | solution.py:21
  48.0 18.6 %collective-permute-start.5 = (bf16[80,3072]{1,0:T(8,128)(2,1)S(1)}, bf16[80,3072]{1,0:T(8,128)(2,1)S(1)}, u32[]{:S(2)}, u32[]{:S(2)}) collective-permute-start(bf16[80,3072]{1,0:T(8,128)(2,1)S(1)} %collective-permute-done.3.refs_0_), channel_id=1, source_target_pairs={{0,4},{4,0},{8,12},{12,8},{16,20},{20,16},{24,28},{28,24},{1,5},{5... | collective-permute-start | bytes 1474568 | tf_op jit(solution)/shard_map/ppermute | solution.py:21
  49.3 20.8 %collective-permute-start.6 = (bf16[80,3072]{1,0:T(8,128)(2,1)S(1)}, bf16[80,3072]{1,0:T(8,128)(2,1)}, u32[]{:S(2)}, u32[]{:S(2)}) collective-permute-start(bf16[80,3072]{1,0:T(8,128)(2,1)S(1)} %collective-permute-done.4.refs_2_), channel_id=1, source_target_pairs={{0,4},{4,0},{8,12},{12,8},{16,20},{20,16},{24,28},{28,24},{1,5},{5... | collective-permute-start | bytes 1474568 | tf_op jit(solution)/shard_map/ppermute | solution.py:21
  88.5 43.1 %collective-permute-start.8 = (bf16[160,3072]{1,0:T(8,128)(2,1)S(1)}, bf16[160,3072]{1,0:T(8,128)(2,1)}, u32[]{:S(2)}, u32[]{:S(2)}) collective-permute-start(bf16[160,3072]{1,0:T(8,128)(2,1)S(1)} %get-tuple-element.53), channel_id=1, source_target_pairs={{0,2},{1,3},{2,0},{3,1},{4,6},{5,7},{6,4},{7,5},{8,10},{9,11},{10,... | collective-permute-start | bytes 2949128 | tf_op jit(solution)/shard_map/ppermute | solution.py:21
  92.6 40.7 %collective-permute-start.14 = (bf16[160,3072]{1,0:T(8,128)(2,1)}, bf16[160,3072]{1,0:T(8,128)(2,1)}, u32[]{:S(2)}, u32[]{:S(2)}) collective-permute-start(bf16[160,3072]{1,0:T(8,128)(2,1)} %get-tuple-element.55), channel_id=1, source_target_pairs={{0,2},{1,3},{2,0},{3,1},{4,6},{5,7},{6,4},{7,5},{8,10},{9,11},{10,... | collective-permute-start | bytes 2949128 | tf_op jit(solution)/shard_map/ppermute | solution.py:21
  93.6 24.8 %collective-permute-start.12 = (bf16[80,3072]{1,0:T(8,128)(2,1)S(1)}, bf16[80,3072]{1,0:T(8,128)(2,1)}, u32[]{:S(2)}, u32[]{:S(2)}) collective-permute-start(bf16[80,3072]{1,0:T(8,128)(2,1)S(1)} %copy-done.14), channel_id=1, source_target_pairs={{0,16},{4,20},{8,24},{12,28},{16,0},{20,4},{24,8},{28,12},{1,17},{... | collective-permute-start | bytes 1474568 | tf_op jit(solution)/shard_map/ppermute | solution.py:21
  94.2 25.8 %collective-permute-start.11 = (bf16[80,3072]{1,0:T(8,128)(2,1)S(1)}, bf16[80,3072]{1,0:T(8,128)(2,1)}, u32[]{:S(2)}, u32[]{:S(2)}) collective-permute-start(bf16[80,3072]{1,0:T(8,128)(2,1)S(1)} %copy-done.14), channel_id=1, source_target_pairs={{0,8},{4,12},{8,0},{12,4},{16,24},{20,28},{24,16},{28,20},{1,9},{5... | collective-permute-start | bytes 1474568 | tf_op jit(solution)/shard_map/ppermute | solution.py:21
  99.9 20.1 %collective-permute-start.10 = (bf16[80,3072]{1,0:T(8,128)(2,1)S(1)}, bf16[80,3072]{1,0:T(8,128)(2,1)}, u32[]{:S(2)}, u32[]{:S(2)}) collective-permute-start(bf16[80,3072]{1,0:T(8,128)(2,1)S(1)} %copy-done.14), channel_id=1, source_target_pairs={{0,4},{4,0},{8,12},{12,8},{16,20},{20,16},{24,28},{28,24},{1,5},{5... | collective-permute-start | bytes 1474568 | tf_op jit(solution)/shard_map/ppermute | solution.py:21
  118.5 21.3 %collective-permute-start.16 = (bf16[80,3072]{1,0:T(8,128)(2,1)}, bf16[80,3072]{1,0:T(8,128)(2,1)}, u32[]{:S(2)}, u32[]{:S(2)}) collective-permute-start(bf16[80,3072]{1,0:T(8,128)(2,1)} %collective-permute-done.12.refs_4_), channel_id=1, source_target_pairs={{0,4},{4,0},{8,12},{12,8},{16,20},{20,16},{24,28},{28,24},{1,5},{5... | collective-permute-start | bytes 1474568 | tf_op jit(solution)/shard_map/ppermute | solution.py:21
  120.0 20.8 %collective-permute-start.17 = (bf16[80,3072]{1,0:T(8,128)(2,1)}, bf16[80,3072]{1,0:T(8,128)(2,1)S(1)}, u32[]{:S(2)}, u32[]{:S(2)}) collective-permute-start(bf16[80,3072]{1,0:T(8,128)(2,1)} %collective-permute-done.12.refs_4_), channel_id=1, source_target_pairs={{0,8},{4,12},{8,0},{12,4},{16,24},{20,28},{24,16},{28,20},{1,9},{5... | collective-permute-start | bytes 1474568 | tf_op jit(solution)/shard_map/ppermute | solution.py:21
  138.0 32.3 %collective-permute-start.13 = (bf16[160,3072]{1,0:T(8,128)(2,1)S(1)}, bf16[160,3072]{1,0:T(8,128)(2,1)S(1)}, u32[]{:S(2)}, u32[]{:S(2)}) collective-permute-start(bf16[160,3072]{1,0:T(8,128)(2,1)S(1)} %get-tuple-element.57), channel_id=1, source_target_pairs={{0,1},{1,0},{2,3},{3,2},{4,5},{5,4},{6,7},{7,6},{8,9},{9,8},{10,11... | collective-permute-start | bytes 2949128 | tf_op jit(solution)/shard_map/ppermute | solution.py:21
  138.0 32.3 %collective-permute-start.15 = (bf16[160,3072]{1,0:T(8,128)(2,1)}, bf16[160,3072]{1,0:T(8,128)(2,1)S(1)}, u32[]{:S(2)}, u32[]{:S(2)}) collective-permute-start(bf16[160,3072]{1,0:T(8,128)(2,1)} %get-tuple-element.58), channel_id=1, source_target_pairs={{0,1},{1,0},{2,3},{3,2},{4,5},{5,4},{6,7},{7,6},{8,9},{9,8},{10,11... | collective-permute-start | bytes 2949128 | tf_op jit(solution)/shard_map/ppermute | solution.py:21
  139.8 18.2 %collective-permute-start.18 = (bf16[80,3072]{1,0:T(8,128)(2,1)}, bf16[80,3072]{1,0:T(8,128)(2,1)}, u32[]{:S(2)}, u32[]{:S(2)}) collective-permute-start(bf16[80,3072]{1,0:T(8,128)(2,1)} %collective-permute-done.11.refs_2_), channel_id=1, source_target_pairs={{0,4},{4,0},{8,12},{12,8},{16,20},{20,16},{24,28},{28,24},{1,5},{5... | collective-permute-start | bytes 1474568 | tf_op jit(solution)/shard_map/ppermute | solution.py:21
  140.8 23.0 %collective-permute-start.19 = (bf16[80,3072]{1,0:T(8,128)(2,1)S(1)}, bf16[80,3072]{1,0:T(8,128)(2,1)}, u32[]{:S(2)}, u32[]{:S(2)}) collective-permute-start(bf16[80,3072]{1,0:T(8,128)(2,1)S(1)} %collective-permute-done.17.refs_6_), channel_id=1, source_target_pairs={{0,4},{4,0},{8,12},{12,8},{16,20},{20,16},{24,28},{28,24},{1,5},{5... | collective-permute-start | bytes 1474568 | tf_op jit(solution)/shard_map/ppermute | solution.py:21
  198.5 43.4 %collective-permute-start.20 = (bf16[320,1024]{1,0:T(8,128)(2,1)}, bf16[320,1024]{1,0:T(8,128)(2,1)}, u32[]{:S(2)}, u32[]{:S(2)}) collective-permute-start(bf16[320,1024]{1,0:T(8,128)(2,1)} %bitcast.4), channel_id=1, source_target_pairs={{0,4},{4,0},{8,12},{12,8},{16,20},{20,16},{24,28},{28,24},{1,5},{5... | collective-permute-start | bytes 1966088 | tf_op jit(solution)/shard_map/ppermute | solution.py:21
  208.6 57.2 %collective-permute-start.24 = (bf16[320,1024]{1,0:T(8,128)(2,1)}, bf16[320,1024]{1,0:T(8,128)(2,1)}, u32[]{:S(2)}, u32[]{:S(2)}) collective-permute-start(bf16[320,1024]{1,0:T(8,128)(2,1)} %bitcast.11), channel_id=1, source_target_pairs={{0,4},{4,0},{8,12},{12,8},{16,20},{20,16},{24,28},{28,24},{1,5},{5... | collective-permute-start | bytes 1966088 | tf_op jit(solution)/shard_map/ppermute | solution.py:21
  221.8 45.9 %collective-permute-start.28 = (bf16[320,1024]{1,0:T(8,128)(2,1)}, bf16[320,1024]{1,0:T(8,128)(2,1)}, u32[]{:S(2)}, u32[]{:S(2)}) collective-permute-start(bf16[320,1024]{1,0:T(8,128)(2,1)} %bitcast.14), channel_id=1, source_target_pairs={{0,4},{4,0},{8,12},{12,8},{16,20},{20,16},{24,28},{28,24},{1,5},{5... | collective-permute-start | bytes 1966088 | tf_op jit(solution)/shard_map/ppermute | solution.py:21
  243.3 27.6 %collective-permute-start.21 = (bf16[160,1024]{1,0:T(8,128)(2,1)S(1)}, bf16[160,1024]{1,0:T(8,128)(2,1)S(1)}, u32[]{:S(2)}, u32[]{:S(2)}) collective-permute-start(bf16[160,1024]{1,0:T(8,128)(2,1)S(1)} %slice.148), channel_id=1, source_target_pairs={{0,8},{4,12},{8,0},{12,4},{16,24},{20,28},{24,16},{28,20},{1,9},{5... | collective-permute-start | bytes 983048 | tf_op jit(solution)/shard_map/ppermute | solution.py:21
  267.4 26.0 %collective-permute-start.25 = (bf16[160,1024]{1,0:T(8,128)(2,1)S(1)}, bf16[160,1024]{1,0:T(8,128)(2,1)S(1)}, u32[]{:S(2)}, u32[]{:S(2)}) collective-permute-start(bf16[160,1024]{1,0:T(8,128)(2,1)S(1)} %slice.147), channel_id=1, source_target_pairs={{0,8},{4,12},{8,0},{12,4},{16,24},{20,28},{24,16},{28,20},{1,9},{5... | collective-permute-start | bytes 983048 | tf_op jit(solution)/shard_map/ppermute | solution.py:21
  269.4 24.3 %collective-permute-start.29 = (bf16[160,1024]{1,0:T(8,128)(2,1)S(1)}, bf16[160,1024]{1,0:T(8,128)(2,1)S(1)}, u32[]{:S(2)}, u32[]{:S(2)}) collective-permute-start(bf16[160,1024]{1,0:T(8,128)(2,1)S(1)} %slice.146), channel_id=1, source_target_pairs={{0,8},{4,12},{8,0},{12,4},{16,24},{20,28},{24,16},{28,20},{1,9},{5... | collective-permute-start | bytes 983048 | tf_op jit(solution)/shard_map/ppermute | solution.py:21
  271.1 25.6 %collective-permute-start.22 = (bf16[80,1024]{1,0:T(8,128)(2,1)S(1)}, bf16[80,1024]{1,0:T(8,128)(2,1)S(1)}, u32[]{:S(2)}, u32[]{:S(2)}) collective-permute-start(bf16[80,1024]{1,0:T(8,128)(2,1)S(1)} %slice.151), channel_id=1, source_target_pairs={{0,16},{4,20},{8,24},{12,28},{16,0},{20,4},{24,8},{28,12},{1,17},{... | collective-permute-start | bytes 491528 | tf_op jit(solution)/shard_map/ppermute | solution.py:21
  (34 other events, 385.4 us)
Sparse Core Ops, SparseCore 0:
  9.6 35.6 all-gather.1

commit v6 on v5

v6 whole, which is shorter than its diff:
```python
import math

import jax
import jax.numpy as jnp
from jax import lax
from jax.experimental import pallas as pl
from jax.experimental.pallas import tpu as pltpu
from jax.sharding import PartitionSpec as P

F32 = jnp.float32
BF16 = jnp.bfloat16
LAST = (((1,), (1,)), ((), ()))
FIRST = (((0,), (0,)), ((), ()))
FACTOR = math.sqrt(2.0 / math.pi)
TILE = 256
VMEM_LIMIT = 56 * 1024 * 1024


def swap(value, axis, bit):
    size = lax.axis_size(axis)
    return lax.ppermute(value, axis, [(i, i ^ bit) for i in range(size)])


def bits_of(size):
    return [1 << i for i in range(size.bit_length() - 1)]


def turned(index, size):
    return sum(((index // bit) % 2) * (size // 2 // bit) for bit in bits_of(size))


def call(kernel, grid, in_specs, out_specs, out_shape, scratch, moved=1000):
    return pl.pallas_call(
        kernel,
        grid_spec=pltpu.PrefetchScalarGridSpec(
            num_scalar_prefetch=1,
            grid=grid,
            in_specs=in_specs,
            out_specs=out_specs,
            scratch_shapes=scratch,
        ),
        out_shape=out_shape,
        compiler_params=pltpu.CompilerParams(
            dimension_semantics=("arbitrary",), vmem_limit_bytes=VMEM_LIMIT
        ),
        cost_estimate=pl.CostEstimate(
            flops=1000, bytes_accessed=moved, transcendentals=0
        ),
    )


def whole_index(i, flags):
    return (0, 0)


def column_index(i, flags):
    return (0, i)


def aligned(start):
    return pl.multiple_of(start, 16)


def token_place(side, order, core, per_group):
    group, k = order // per_group, order % per_group
    return (2 * group + (side ^ core)) * per_group + k


def widest(width, limit):
    return max(tile for tile in range(128, limit + 1, 128) if width % tile == 0)


def gelu_all(pieces, offsets, flags, n_row, per_group, rows):
    width = pieces[0].shape[1]
    per_col = pieces[0].shape[0] // rows
    slots = n_row // 2
    tokens = n_row * rows
    tile = widest(width, 256)

    def kernel(flags_ref, *refs):
        act_ref, slope_ref = refs[-2:]
        row, core, col = flags_ref[0], flags_ref[1], flags_ref[2]
        for ref, offset in zip(refs[:-2], offsets):
            for part in range(per_col):
                index = row ^ ((col ^ offset) * per_col + part)
                hval = ref[part * rows : (part + 1) * rows, :].astype(F32)
                tanh_part = jnp.tanh(FACTOR * (hval + 0.044715 * hval * hval * hval))
                order = turned(index // 2, slots)
                place = token_place(index % 2, order, core, per_group)
                act_ref[pl.ds(aligned(place * rows), rows), :] = (
                    0.5 * hval * (1.0 + tanh_part)
                ).astype(BF16)

                @pl.when(index % 2 == core)
                def _():
                    slope_ref[pl.ds(aligned(order * rows), rows), :] = 0.5 * (
                        1.0 + tanh_part
                    ) + 0.5 * hval * (1.0 - tanh_part * tanh_part) * FACTOR * (
                        1.0 + 3.0 * 0.044715 * hval * hval
                    )

    return call(
        kernel,
        (width // tile,),
        [pl.BlockSpec((piece.shape[0], tile), column_index) for piece in pieces],
        [
            pl.BlockSpec((tokens, tile), column_index),
            pl.BlockSpec((tokens // 2, tile), column_index),
        ],
        [
            jax.ShapeDtypeStruct((tokens, width), BF16),
            jax.ShapeDtypeStruct((tokens // 2, width), F32),
        ],
        [],
        16 * tokens * width,
    )(flags, *pieces)


def arrange(pieces, places, flags):
    rows, width = pieces[0].shape
    tokens = rows * len(pieces)
    tile = widest(width, width // 2)

    def kernel(flags_ref, *refs):
        for ref, place in zip(refs, places):
            refs[-1][pl.ds(aligned(place(flags_ref[1]) * rows), rows), :] = ref[...]

    return call(
        kernel,
        (width // tile,),
        [pl.BlockSpec((rows, tile), column_index)] * len(pieces),
        pl.BlockSpec((tokens, tile), column_index),
        jax.ShapeDtypeStruct((tokens, width), BF16),
        [],
    )(flags, *pieces)


def stack(pieces, flags):
    return arrange(pieces, [lambda core, i=i: i for i in range(len(pieces))], flags)


def gram(value, flags):
    tokens, width = value.shape
    tile = widest(width, 1024)

    def kernel(flags_ref, value_ref, out_ref):
        @pl.when(pl.program_id(0) == 0)
        def _():
            out_ref[...] = jnp.zeros_like(out_ref)

        out_ref[...] += lax.dot_general(
            value_ref[...], value_ref[...], LAST, preferred_element_type=F32
        )

    return call(
        kernel,
        (width // tile,),
        [pl.BlockSpec((tokens, tile), column_index)],
        pl.BlockSpec((tokens, tokens), whole_index),
        jax.ShapeDtypeStruct((tokens, tokens), F32),
        [],
    )(flags, value)


def gram_inner(left_gram, right, flags):
    tokens, width = right.shape
    tile = widest(width, 1024)
    steps = width // tile

    def kernel(flags_ref, left_ref, right_ref, out_ref, right_gram):
        step = pl.program_id(0)

        @pl.when(step == 0)
        def _():
            right_gram[...] = jnp.zeros_like(right_gram)

        right_gram[...] += lax.dot_general(
            right_ref[...], right_ref[...], LAST, preferred_element_type=F32
        )

        @pl.when(step == steps - 1)
        def _():
            out_ref[...] = jnp.sum(left_ref[...] * right_gram[...], axis=0, keepdims=True)

    out = call(
        kernel,
        (steps,),
        [
            pl.BlockSpec((tokens, tokens), whole_index),
            pl.BlockSpec((tokens, tile), column_index),
        ],
        pl.BlockSpec((1, tokens), whole_index),
        jax.ShapeDtypeStruct((1, tokens), F32),
        [pltpu.VMEM((tokens, tokens), F32)],
    )(flags, left_gram, right)
    return jnp.sum(out)


def after(value, *events):
    return lax.optimization_barrier((value, *events))[0]


def on_device(inputs, pre_act, out_grad, token_valid, poison, w_up, w_down):
    n_row = lax.axis_size("row")
    n_col = lax.axis_size("col")
    rows = inputs.shape[0]
    tokens = rows * n_row
    slots = n_row // 2
    row, col = lax.axis_index("row"), lax.axis_index("col")
    core = col % 2
    flags = jnp.stack([row, core, col]).astype(jnp.int32)
    row_bits, col_bits = bits_of(n_row), bits_of(n_col)

    def exchange(own, x_own, early, late):
        blocks = {0: own, 1: swap(x_own, "row", 1)}
        for bit in reversed(row_bits[1:]):
            for index in sorted(blocks):
                if index % 2 == 0:
                    source = own if index == 0 else after(blocks[index], blocks[1], blocks[bit])
                    blocks[index | bit] = swap(source, "row", bit)
        even = [index for index in sorted(blocks) if index % 2 == 0 and index > 0]
        for index in even:
            if not index & 2:
                blocks[index | 1] = swap(after(blocks[index], early), "row", 1)
        last = max(index for index in blocks if index & 1)
        for index in even:
            if index & 2:
                blocks[index | 1] = swap(after(blocks[index], blocks[last], late), "row", 1)
        return [blocks[index] for index in range(n_row)]

    groups = 2 if slots % 2 == 0 else 1
    per_group = slots // groups
    count = per_group * rows
    by_group = [[] for _ in range(groups)]
    for index in range(n_row):
        by_group[turned(index // 2, slots) // per_group].append(index)

    def place_of(index, group):
        order = turned(index // 2, slots)
        return lambda core: token_place(index % 2, order, core, per_group) - (
            group * 2 * per_group
        )

    pieces, offsets = [pre_act], [0]
    for bit in reversed(col_bits):
        pieces = pieces + [swap(piece, "col", bit) for piece in pieces]
        offsets = offsets + [offset ^ bit for offset in offsets]

    own = out_grad * token_valid.astype(BF16)[:, None]
    act, slope = gelu_all(pieces, offsets, flags, n_row, per_group, rows)
    masked = exchange(own, own, pieces[1], act)
    own = after(inputs, masked[-2])
    inputs_blocks = exchange(own, after(own, masked[-1]), own, own)

    blocks, totals = [], []
    for group, indices in enumerate(by_group):
        block = arrange(
            [masked[index] for index in indices],
            [place_of(index, group) for index in indices],
            flags,
        )
        blocks.append(block)
        if group == 0:
            first = [masked[-2], act]
            second = [masked[index] for index in by_group[-1] if index & 1]
        else:
            first = totals
            second = [inputs_blocks[2], inputs_blocks[n_row // 2]]
        partial = lax.dot_general(
            after(block, *first), w_down, LAST, preferred_element_type=F32
        )
        other = swap(after(partial[count:].astype(BF16), *second), "col", 1)
        totals.append(partial[:count] + other.astype(F32))
    masked_all = stack(blocks, flags)
    square_down = gram_inner(
        gram(masked_all, flags),
        after(act, *inputs_blocks[1::2][: slots // 2], inputs_blocks[-2]),
        flags,
    )
    inputs_all = arrange(
        [after(inputs_blocks[0], square_down)] + inputs_blocks[1:],
        [place_of(index, 0) for index in range(n_row)],
        flags,
    )
    inputs_gram = gram(inputs_all, flags)
    hidden_blocks = []
    for group, total in enumerate(totals):
        for bit in col_bits[1:]:
            got = swap(total.astype(BF16), "col", bit)
            if hidden_blocks:
                got = after(got, hidden_blocks[-1], square_down)
            total = total + got.astype(F32)
        hidden = (total * slope[group * count : (group + 1) * count]).astype(BF16)
        hidden_blocks += [hidden, swap(hidden, "col", 1)]
    hidden_blocks[-1] = after(hidden_blocks[-1], inputs_gram)
    hidden_all = stack(hidden_blocks, flags)

    flag_value = poison[0, 0].astype(F32)
    keep_block = 1.0 - flag_value
    count_term = jnp.where(col == 0, jnp.sum(token_valid.astype(F32)), 0.0)

    def sides(product):
        split = product.reshape(groups, 2, count, product.shape[1])
        return [
            lax.dynamic_index_in_dim(split, side, 1, keepdims=False).reshape(
                groups * count, product.shape[1]
            )
            for side in (core, 1 - core)
        ]

    model = w_up.shape[0]
    parts = 3 if model % (3 * TILE) == 0 else 1
    step = model // parts
    stages = []
    operand = hidden_all
    for part in range(parts):
        product = lax.dot_general(
            operand, w_up[part * step : (part + 1) * step], LAST, preferred_element_type=F32
        )
        mine, theirs = sides(product)
        theirs = theirs.astype(BF16)
        total = mine + swap(theirs, "row", 1).astype(F32)
        stages.append([total])
        for bit in row_bits[1:]:
            split = total.shape[0] // 2
            total = total[:split] + swap(total[split:].astype(BF16), "row", bit).astype(F32)
            stages[-1].append(total)
        if part == 0:
            square_up = gram_inner(inputs_gram, after(hidden_all, theirs), flags)
        operand = after(operand, square_up, theirs)
    scalars = jnp.stack([count_term, keep_block * (square_down + square_up), flag_value])
    scalars = after(scalars, product)
    for axis, bits in (("col", col_bits), ("row", row_bits)):
        for bit in bits:
            scalars = scalars + swap(scalars, axis, bit)
    count_all, square_all, flag_all = scalars[0], jnp.maximum(scalars[1], 0.0), scalars[2]

    token_total = jnp.maximum(count_all, 1.0)
    squares = square_all / (token_total * token_total)
    block_count = float(n_row * n_col)
    estimate = squares * block_count / jnp.maximum(block_count - flag_all, 1.0)
    limit = 0.25 * math.sqrt(
        (w_up.shape[1] * n_row) * (w_up.shape[0] * n_col) / tokens
    )
    clip_factor = jnp.minimum(1.0, limit / jnp.sqrt(estimate + 1e-06))
    scale = keep_block * clip_factor / token_total

    def gradient(left, right, scale):
        product = lax.dot_general(left, right, FIRST, preferred_element_type=F32)
        return (product * scale).astype(BF16)

    grad_down = gradient(act, masked_all, after(scale, *[stage[0] for stage in stages]))
    events = [stage[1] for stage in stages] + [grad_down]
    grad_up = gradient(inputs_all, hidden_all, after(scale, *events))
    input_sum = jnp.concatenate([stage[-1] for stage in stages], axis=1)
    return (input_sum / token_total).astype(BF16), grad_up, grad_down


def solution(mesh):
    placed = (
        P("row", "col"),
        P("col", "row"),
        P("row", "col"),
        P("row"),
        P("row", "col"),
        P("col", "row"),
        P("row", "col"),
    )
    return jax.shard_map(
        on_device,
        mesh=mesh,
        in_specs=placed,
        out_specs=(P("row", "col"), P("col", "row"), P("row", "col")),
        check_vma=False,
    )
```

time: 317 us -> 316 us (level)
  between operations: 19.1 us -> 5.65 us
  other arithmetic: 30.4 us -> 19.8 us
  Pallas kernels: 50.2 us -> 59.9 us
  waiting for transfers between devices: 80.2 us -> 89.4 us
  local copies, waits for them, and re-layouts: 6.92 us -> 15 us
    concatenate x2 -> x0, other arithmetic: 10.8 us -> none  [the longest x1 6.5 us: on_device(): hidden_all = jnp.concatenate(hidden_blocks, axis=0)]
    ppermute x34 -> x37, waiting for transfers between devices: 79.5 us -> 89.4 us  [swap(): return lax.ppermute(value, axis, [(i, i ^ bit) for i in range(size)])]
    pallas_call x3 -> x5, Pallas kernels: 32.5 us -> 40.2 us  [the longest x2 14.2 us: gram_inner(): call(kernel, (steps,), [pl.BlockSpec((tokens, tokens), whole_index), pl.B...]
    unnamed x46 -> x58, local copies, waits for them, and re-layouts: 0.46 us -> 6.37 us
    dot_general x3, matrix products: 20.8 us -> 24.7 us  [on_device(): lax.dot_general(operand, w_up[part * step:(part + 1) * step], LAST, prefe...]
    dot_general x2, matrix products: 39.8 us -> 35.8 us  [gradient(): product = lax.dot_general(left, right, FIRST, preferred_element_type=F32)]
    ppermute x34 -> x37, starting transfers between devices: 47 us -> 44 us  [swap(): return lax.ppermute(value, axis, [(i, i ^ bit) for i in range(size)])]
    pallas_call x3 -> x5, Pallas kernels: 17.8 us -> 19.6 us  [arrange(): call(kernel, (width // tile,), [pl.BlockSpec((rows, tile), column_index)]...]
  transfers between devices with their start and end apart: 35 -> 37, of which waited for: 13 -> 16; matrix products, arithmetic and copies ran while one was open for 31% -> 31% of each run, Pallas kernels for 13% -> 15%
where the time goes in v6:
time: 316 us; the launch traced here: 315 us
  waiting for transfers between devices  89.4 us (28%)
  matrix products  80.9 us (26%)
  Pallas kernels  59.9 us (19%)
  starting transfers between devices  44 us (14%)
  other arithmetic  19.8 us (6%)
  local copies, waits for them, and re-layouts  15 us (5%)
  between operations  5.65 us (2%)
    ppermute x37, waiting for transfers between devices, swap(): return lax.ppermute(value, axis, [(i, i ^ bit) for i in range(size)])  89.4 us
    ppermute x37, starting transfers between devices, swap(): return lax.ppermute(value, axis, [(i, i ^ bit) for i in range(size)])  44 us
    dot_general x2, matrix products, gradient(): product = lax.dot_general(left, right, FIRST, preferred_element_type=F32)  35.8 us
    dot_general x3, matrix products, on_device(): lax.dot_general(operand, w_up[part * step:(part + 1) * step], LAST, prefe...  24.7 us
    dot_general x2, matrix products, on_device(): lax.dot_general(after(block, *first), w_down, LAST, preferred_element_typ...  20.4 us
    pallas_call x5, Pallas kernels, arrange(): call(kernel, (width // tile,), [pl.BlockSpec((rows, tile), column_index)]...  19.6 us
    pallas_call x2, Pallas kernels, gram_inner(): call(kernel, (steps,), [pl.BlockSpec((tokens, tokens), whole_index), pl.B...  14.2 us
    pallas_call x2, Pallas kernels, gram(): call(kernel, (width // tile,), [pl.BlockSpec((tokens, tile), column_index...  14.1 us
  transfers between devices with their start and end apart: 37, of which 16 were waited for; matrix products, arithmetic and copies ran while one was open for 31% of the time, Pallas kernels for 15%

profile of v6, /device:TPU:0, one launch (start us, length us, event | category | flops | bytes accessed | tf_op | source)
XLA Modules:
  0.0 314.6 jit_solution(968556396658168058)
XLA Ops:
  11.2 14.4 %collective-permute-done.2.refs_1_ = bf16[160,3072]{1,0:T(8,128)(2,1)S(1)} collective-permute-done((bf16[160,3072]{1,0:T(8,128)(2,1)}, bf16[160,3072]{1,0:T(8,128)(2,1)S(1)}, u32[]{:S(2)}, u32[]{:S(2)}) %collective-permute-start.2) | collective-permute-done | bytes 983072 | tf_op jit(solution)/shard_map/ppermute | solution.py:21
  25.6 4.2 %collective-permute-done.1.refs_2_ = bf16[80,3072]{1,0:T(8,128)(2,1)} collective-permute-done((bf16[80,3072]{1,0:T(8,128)(2,1)S(1)}, bf16[80,3072]{1,0:T(8,128)(2,1)}, u32[]{:S(2)}, u32[]{:S(2)}) %collective-permute-start.1) | collective-permute-done | bytes 491552 | tf_op jit(solution)/shard_map/ppermute | solution.py:21
  33.6 8.6 %collective-permute-done.3.refs_3_ = bf16[80,3072]{1,0:T(8,128)(2,1)} collective-permute-done((bf16[80,3072]{1,0:T(8,128)(2,1)}, bf16[80,3072]{1,0:T(8,128)(2,1)}, u32[]{:S(2)}, u32[]{:S(2)}) %collective-permute-start.3) | collective-permute-done | bytes 491552 | tf_op jit(solution)/shard_map/ppermute | solution.py:21
  47.5 11.9 %shard_map.95 = (bf16[640,3072]{1,0:T(8,128)(2,1)}, f32[320,3072]{1,0:T(8,128)}) custom-call(s32[3]{0:T(128)} %pad_add_fusion.flags_ref, bf16[160,3072]{1,0:T(8,128)(2,1)} %refs_0_.1, bf16[160,3072]{1,0:T(8,128)(2,1)} %copy-done.16, bf16[160,3072]{1,0:T(8,128)(2,1)} %copy-done.17, bf16[160,3072]{1,0:T(8,128)(2,1)} %copy-done.18), custom_call_target="tpu_custom_call" | custom-call | flops 1000 | bytes 31457280 | tf_op jit(solution)/shard_map/pallas_call | solution.py:102
  61.5 10.2 %fusion.10 = f32[320,3072]{1,0:T(8,128)S(1)} fusion(bf16[320,3072]{1,0:T(8,128)(2,1)S(1)} %copy-done.4, bf16[3072,3072]{1,0:T(8,128)(2,1)} %param.13), kind=kOutput, calls=%fused_computation.44 | convolution fusion | flops 6039797760 | bytes 24772608 | tf_op jit(solution)/shard_map/dot_general | solution.py:269
  73.6 7.4 %collective-permute-done.9.refs_3_ = bf16[80,3072]{1,0:T(8,128)(2,1)S(1)} collective-permute-done((bf16[80,3072]{1,0:T(8,128)(2,1)}, bf16[80,3072]{1,0:T(8,128)(2,1)S(1)}, u32[]{:S(2)}, u32[]{:S(2)}) %collective-permute-start.9) | collective-permute-done | bytes 491552 | tf_op jit(solution)/shard_map/ppermute | solution.py:21
  82.1 5.2 %collective-permute-start.13 = (bf16[80,3072]{1,0:T(8,128)(2,1)}, bf16[80,3072]{1,0:T(8,128)(2,1)}, u32[]{:S(2)}, u32[]{:S(2)}) collective-permute-start(bf16[80,3072]{1,0:T(8,128)(2,1)} %refs_0_.2), channel_id=1, source_target_pairs={{0,8},{4,12},{8,0},{12,4},{16,24},{20,28},{24,16},{28,20},{1,9},{5... | collective-permute-start | bytes 1474568 | tf_op jit(solution)/shard_map/ppermute | solution.py:21
  92.9 10.2 %fusion.11 = f32[320,3072]{1,0:T(8,128)S(1)} fusion(bf16[320,3072]{1,0:T(8,128)(2,1)S(1)} %copy-done.5, bf16[3072,3072]{1,0:T(8,128)(2,1)} %param.13), kind=kOutput, calls=%fused_computation.45 | convolution fusion | flops 6039797760 | bytes 24772608 | tf_op jit(solution)/shard_map/dot_general | solution.py:269
  108.7 7.4 %collective-permute-done.11 = bf16[160,3072]{1,0:T(8,128)(2,1)S(1)} collective-permute-done((bf16[160,3072]{1,0:T(8,128)(2,1)S(1)}, bf16[160,3072]{1,0:T(8,128)(2,1)S(1)}, u32[]{:S(2)}, u32[]{:S(2)}) %collective-permute-start.11) | collective-permute-done | bytes 983072 | tf_op jit(solution)/shard_map/ppermute | solution.py:21
  122.4 9.0 %collective-permute-done.17.refs_1_ = bf16[80,3072]{1,0:T(8,128)(2,1)S(1)} collective-permute-done((bf16[80,3072]{1,0:T(8,128)(2,1)}, bf16[80,3072]{1,0:T(8,128)(2,1)S(1)}, u32[]{:S(2)}, u32[]{:S(2)}) %collective-permute-start.17) | collective-permute-done | bytes 491552 | tf_op jit(solution)/shard_map/ppermute | solution.py:21
  131.4 4.3 %shard_map.97.value_ref = bf16[640,3072]{1,0:T(8,128)(2,1)} custom-call(s32[3]{0:T(128)} %pad_add_fusion.flags_ref, bf16[320,3072]{1,0:T(8,128)(2,1)} %shard_map.94.refs_0_, bf16[320,3072]{1,0:T(8,128)(2,1)} %shard_map.96.refs_1_), custom_call_target="tpu_custom_call" | custom-call | flops 1000 | bytes 1000 | tf_op jit(solution)/shard_map/pallas_call | solution.py:128
  135.7 7.1 %shard_map.98.left_ref = f32[640,640]{1,0:T(8,128)} custom-call(s32[3]{0:T(128)} %pad_add_fusion.flags_ref, bf16[640,3072]{1,0:T(8,128)(2,1)} %shard_map.97.value_ref), custom_call_target="tpu_custom_call" | custom-call | flops 1000 | bytes 1000 | tf_op jit(solution)/shard_map/pallas_call | solution.py:155
  144.3 7.1 %shard_map.99 = f32[1,640]{1,0:T(1,128)} custom-call(s32[3]{0:T(128)} %pad_add_fusion.flags_ref, f32[640,640]{1,0:T(8,128)} %shard_map.98.left_ref, bf16[640,3072]{1,0:T(8,128)(2,1)} %get-tuple-element.44.right_ref), custom_call_target="tpu_custom_call" | custom-call | flops 1000 | bytes 1000 | tf_op jit(solution)/shard_map/pallas_call | solution.py:185
  159.0 11.0 %collective-permute-done.22.refs_7_ = bf16[80,3072]{1,0:T(8,128)(2,1)S(1)} collective-permute-done((bf16[80,3072]{1,0:T(8,128)(2,1)}, bf16[80,3072]{1,0:T(8,128)(2,1)S(1)}, u32[]{:S(2)}, u32[]{:S(2)}) %collective-permute-start.22) | collective-permute-done | bytes 491552 | tf_op jit(solution)/shard_map/ppermute | solution.py:21
  170.8 4.4 %shard_map.100.value_ref = bf16[640,3072]{1,0:T(8,128)(2,1)} custom-call(s32[3]{0:T(128)} %pad_add_fusion.flags_ref, bf16[80,3072]{1,0:T(8,128)(2,1)} %refs_0_.2, bf16[80,3072]{1,0:T(8,128)(2,1)} %copy-done.22, bf16[80,3072]{1,0:T(8,128)(2,1)} %collective-permute-done.13.refs_2_, bf16[80,3072]{1,0:T(8,128)(2,1)} %copy-done.23, ...), custom_call_target="tpu_custom_call" | custom-call | flops 1000 | bytes 1000 | tf_op jit(solution)/shard_map/pallas_call | solution.py:128
  175.8 7.1 %shard_map.101.left_ref = f32[640,640]{1,0:T(8,128)} custom-call(s32[3]{0:T(128)} %pad_add_fusion.flags_ref, bf16[640,3072]{1,0:T(8,128)(2,1)} %shard_map.100.value_ref), custom_call_target="tpu_custom_call" | custom-call | flops 1000 | bytes 1000 | tf_op jit(solution)/shard_map/pallas_call | solution.py:155
  183.9 4.2 %shard_map.102.right_ref = bf16[640,3072]{1,0:T(8,128)(2,1)} custom-call(s32[3]{0:T(128)} %pad_add_fusion.flags_ref, bf16[160,3072]{1,0:T(8,128)(2,1)} %copy-done.8, bf16[160,3072]{1,0:T(8,128)(2,1)} %copy-done.14, bf16[160,3072]{1,0:T(8,128)(2,1)} %copy-done.9, bf16[160,3072]{1,0:T(8,128)(2,1)} %copy-done.15), custom_call_target="tpu_custom_call" | custom-call | flops 1000 | bytes 1000 | tf_op jit(solution)/shard_map/pallas_call | solution.py:128
  188.1 7.6 %fusion.4 = f32[640,1024]{1,0:T(8,128)S(1)} fusion(bf16[640,3072]{1,0:T(8,128)(2,1)} %shard_map.102.right_ref, bf16[3072,3072]{1,0:T(8,128)(2,1)} %param.12), kind=kOutput, calls=%fused_computation.6 | convolution fusion | flops 4026531840 | bytes 12845056 | tf_op jit(solution)/shard_map/dot_general | solution.py:317
  197.3 7.1 %shard_map.103 = f32[1,640]{1,0:T(1,128)} custom-call(s32[3]{0:T(128)} %pad_add_fusion.flags_ref, f32[640,640]{1,0:T(8,128)} %shard_map.101.left_ref, bf16[640,3072]{1,0:T(8,128)(2,1)} %shard_map.102.right_ref), custom_call_target="tpu_custom_call" | custom-call | flops 1000 | bytes 1000 | tf_op jit(solution)/shard_map/pallas_call | solution.py:185
  208.4 8.5 %fusion.2 = f32[640,1024]{1,0:T(8,128)S(1)} fusion(bf16[640,3072]{1,0:T(8,128)(2,1)} %shard_map.102.right_ref, bf16[3072,3072]{1,0:T(8,128)(2,1)} %param.12), kind=kOutput, calls=%fused_computation.4 | convolution fusion | flops 4026531840 | bytes 12845056 | tf_op jit(solution)/shard_map/dot_general | solution.py:317
  218.5 8.7 %fusion = f32[640,1024]{1,0:T(8,128)} fusion(bf16[640,3072]{1,0:T(8,128)(2,1)S(1)} %copy-done.2, bf16[3072,3072]{1,0:T(8,128)(2,1)} %param.12), kind=kOutput, calls=%fused_computation.2 | convolution fusion | flops 4026531840 | bytes 12845056 | tf_op jit(solution)/shard_map/dot_general | solution.py:317
  239.3 12.1 %collective-permute-done.34 = f32[3]{0:T(128)S(1)} collective-permute-done((f32[3]{0:T(128)S(1)}, f32[3]{0:T(128)S(1)}, u32[]{:S(2)}, u32[]{:S(2)}) %collective-permute-start.34) | collective-permute-done | bytes 44 | tf_op jit(solution)/shard_map/ppermute | solution.py:21
  271.3 17.9 %multiply_convert_fusion.1 = bf16[3072,3072]{1,0:T(8,128)(2,1)} fusion(f32[]{:T(128)S(6)} %div.23, bf16[640,3072]{1,0:T(8,128)(2,1)S(1)} %copy-done.7, bf16[640,3072]{1,0:T(8,128)(2,1)S(1)} %copy-done), kind=kOutput, calls=%fused_computation.1 | convolution fusion | flops 12098469888 | bytes 26738692 | tf_op jit(solution)/shard_map/dot_general | solution.py:349
  295.7 17.9 %multiply_convert_fusion = bf16[3072,3072]{1,0:T(8,128)(2,1)} fusion(f32[]{:T(128)S(6)} %div.23, bf16[640,3072]{1,0:T(8,128)(2,1)S(1)} %copy-done.1, bf16[640,3072]{1,0:T(8,128)(2,1)S(1)} %copy-done.3), kind=kOutput, calls=%fused_computation | convolution fusion | flops 12098469888 | bytes 26738692 | tf_op jit(solution)/shard_map/dot_general | solution.py:349
  (165 shorter events, 95.4 us)
Async XLA Ops:
  0.6 25.0 %collective-permute-start.2 = (bf16[160,3072]{1,0:T(8,128)(2,1)}, bf16[160,3072]{1,0:T(8,128)(2,1)S(1)}, u32[]{:S(2)}, u32[]{:S(2)}) collective-permute-start(bf16[160,3072]{1,0:T(8,128)(2,1)} %refs_0_.1), channel_id=1, source_target_pairs={{0,2},{1,3},{2,0},{3,1},{4,6},{5,7},{6,4},{7,5},{8,10},{9,11},{10,... | collective-permute-start | bytes 2949128 | tf_op jit(solution)/shard_map/ppermute | solution.py:21
  5.5 24.4 %collective-permute-start.1 = (bf16[80,3072]{1,0:T(8,128)(2,1)S(1)}, bf16[80,3072]{1,0:T(8,128)(2,1)}, u32[]{:S(2)}, u32[]{:S(2)}) collective-permute-start(bf16[80,3072]{1,0:T(8,128)(2,1)S(1)} %broadcast_multiply_fusion.refs_0_), channel_id=1, source_target_pairs={{0,16},{4,20},{8,24},{12,28},{16,0},{20,4},{24,8},{28,12},{1,17},{... | collective-permute-start | bytes 1474568 | tf_op jit(solution)/shard_map/ppermute | solution.py:21
  8.1 23.2 %collective-permute-start.4 = (bf16[80,3072]{1,0:T(8,128)(2,1)S(1)}, bf16[80,3072]{1,0:T(8,128)(2,1)S(1)}, u32[]{:S(2)}, u32[]{:S(2)}) collective-permute-start(bf16[80,3072]{1,0:T(8,128)(2,1)S(1)} %broadcast_multiply_fusion.refs_0_), channel_id=1, source_target_pairs={{0,8},{4,12},{8,0},{12,4},{16,24},{20,28},{24,16},{28,20},{1,9},{5... | collective-permute-start | bytes 1474568 | tf_op jit(solution)/shard_map/ppermute | solution.py:21
  9.7 21.7 %collective-permute-start = (bf16[80,3072]{1,0:T(8,128)(2,1)S(1)}, bf16[80,3072]{1,0:T(8,128)(2,1)S(1)}, u32[]{:S(2)}, u32[]{:S(2)}) collective-permute-start(bf16[80,3072]{1,0:T(8,128)(2,1)S(1)} %broadcast_multiply_fusion.refs_0_), channel_id=1, source_target_pairs={{0,4},{4,0},{8,12},{12,8},{16,20},{20,16},{24,28},{28,24},{1,5},{5... | collective-permute-start | bytes 1474568 | tf_op jit(solution)/shard_map/ppermute | solution.py:21
  11.2 34.4 %collective-permute-start.6 = (bf16[160,3072]{1,0:T(8,128)(2,1)}, bf16[160,3072]{1,0:T(8,128)(2,1)S(1)}, u32[]{:S(2)}, u32[]{:S(2)}) collective-permute-start(bf16[160,3072]{1,0:T(8,128)(2,1)} %refs_0_.1), channel_id=1, source_target_pairs={{0,1},{1,0},{2,3},{3,2},{4,5},{5,4},{6,7},{7,6},{8,9},{9,8},{10,11... | collective-permute-start | bytes 2949128 | tf_op jit(solution)/shard_map/ppermute | solution.py:21
  32.2 27.2 %collective-permute-start.5 = (bf16[80,3072]{1,0:T(8,128)(2,1)}, bf16[80,3072]{1,0:T(8,128)(2,1)}, u32[]{:S(2)}, u32[]{:S(2)}) collective-permute-start(bf16[80,3072]{1,0:T(8,128)(2,1)} %collective-permute-done.1.refs_2_), channel_id=1, source_target_pairs={{0,8},{4,12},{8,0},{12,4},{16,24},{20,28},{24,16},{28,20},{1,9},{5... | collective-permute-start | bytes 1474568 | tf_op jit(solution)/shard_map/ppermute | solution.py:21
  60.9 20.1 %collective-permute-start.9 = (bf16[80,3072]{1,0:T(8,128)(2,1)}, bf16[80,3072]{1,0:T(8,128)(2,1)S(1)}, u32[]{:S(2)}, u32[]{:S(2)}) collective-permute-start(bf16[80,3072]{1,0:T(8,128)(2,1)} %collective-permute-done.5.refs_2_), channel_id=1, source_target_pairs={{0,4},{4,0},{8,12},{12,8},{16,20},{20,16},{24,28},{28,24},{1,5},{5... | collective-permute-start | bytes 1474568 | tf_op jit(solution)/shard_map/ppermute | solution.py:21
  81.0 25.5 %collective-permute-start.14 = (bf16[80,3072]{1,0:T(8,128)(2,1)}, bf16[80,3072]{1,0:T(8,128)(2,1)}, u32[]{:S(2)}, u32[]{:S(2)}) collective-permute-start(bf16[80,3072]{1,0:T(8,128)(2,1)} %refs_0_.2), channel_id=1, source_target_pairs={{0,16},{4,20},{8,24},{12,28},{16,0},{20,4},{24,8},{28,12},{1,17},{... | collective-permute-start | bytes 1474568 | tf_op jit(solution)/shard_map/ppermute | solution.py:21
  82.1 24.5 %collective-permute-start.13 = (bf16[80,3072]{1,0:T(8,128)(2,1)}, bf16[80,3072]{1,0:T(8,128)(2,1)}, u32[]{:S(2)}, u32[]{:S(2)}) collective-permute-start(bf16[80,3072]{1,0:T(8,128)(2,1)} %refs_0_.2), channel_id=1, source_target_pairs={{0,8},{4,12},{8,0},{12,4},{16,24},{20,28},{24,16},{28,20},{1,9},{5... | collective-permute-start | bytes 1474568 | tf_op jit(solution)/shard_map/ppermute | solution.py:21
  92.4 23.7 %collective-permute-start.11 = (bf16[160,3072]{1,0:T(8,128)(2,1)S(1)}, bf16[160,3072]{1,0:T(8,128)(2,1)S(1)}, u32[]{:S(2)}, u32[]{:S(2)}) collective-permute-start(bf16[160,3072]{1,0:T(8,128)(2,1)S(1)} %get-tuple-element.55), channel_id=1, source_target_pairs={{0,2},{1,3},{2,0},{3,1},{4,6},{5,7},{6,4},{7,5},{8,10},{9,11},{10,... | collective-permute-start | bytes 2949128 | tf_op jit(solution)/shard_map/ppermute | solution.py:21
  108.1 23.3 %collective-permute-start.17 = (bf16[80,3072]{1,0:T(8,128)(2,1)}, bf16[80,3072]{1,0:T(8,128)(2,1)S(1)}, u32[]{:S(2)}, u32[]{:S(2)}) collective-permute-start(bf16[80,3072]{1,0:T(8,128)(2,1)} %refs_0_.2), channel_id=1, source_target_pairs={{0,4},{4,0},{8,12},{12,8},{16,20},{20,16},{24,28},{28,24},{1,5},{5... | collective-permute-start | bytes 1474568 | tf_op jit(solution)/shard_map/ppermute | solution.py:21
  118.0 34.8 %collective-permute-start.12 = (bf16[160,3072]{1,0:T(8,128)(2,1)S(1)}, bf16[160,3072]{1,0:T(8,128)(2,1)S(1)}, u32[]{:S(2)}, u32[]{:S(2)}) collective-permute-start(bf16[160,3072]{1,0:T(8,128)(2,1)S(1)} %multiply_convert_fusion.3.refs_0_), channel_id=1, source_target_pairs={{0,1},{1,0},{2,3},{3,2},{4,5},{5,4},{6,7},{7,6},{8,9},{9,8},{10,11... | collective-permute-start | bytes 2949128 | tf_op jit(solution)/shard_map/ppermute | solution.py:21
  119.2 33.5 %collective-permute-start.16 = (bf16[160,3072]{1,0:T(8,128)(2,1)}, bf16[160,3072]{1,0:T(8,128)(2,1)}, u32[]{:S(2)}, u32[]{:S(2)}) collective-permute-start(bf16[160,3072]{1,0:T(8,128)(2,1)} %fusion.6), channel_id=1, source_target_pairs={{0,2},{1,3},{2,0},{3,1},{4,6},{5,7},{6,4},{7,5},{8,10},{9,11},{10,... | collective-permute-start | bytes 2949128 | tf_op jit(solution)/shard_map/ppermute | solution.py:21
  120.9 21.9 %collective-permute-start.19 = (bf16[80,3072]{1,0:T(8,128)(2,1)}, bf16[80,3072]{1,0:T(8,128)(2,1)S(1)}, u32[]{:S(2)}, u32[]{:S(2)}) collective-permute-start(bf16[80,3072]{1,0:T(8,128)(2,1)} %collective-permute-done.13.refs_2_), channel_id=1, source_target_pairs={{0,4},{4,0},{8,12},{12,8},{16,20},{20,16},{24,28},{28,24},{1,5},{5... | collective-permute-start | bytes 1474568 | tf_op jit(solution)/shard_map/ppermute | solution.py:21
  156.1 26.8 %collective-permute-start.21 = (bf16[160,3072]{1,0:T(8,128)(2,1)S(1)}, bf16[160,3072]{1,0:T(8,128)(2,1)S(1)}, u32[]{:S(2)}, u32[]{:S(2)}) collective-permute-start(bf16[160,3072]{1,0:T(8,128)(2,1)S(1)} %multiply_convert_fusion.2.refs_2_), channel_id=1, source_target_pairs={{0,1},{1,0},{2,3},{3,2},{4,5},{5,4},{6,7},{7,6},{8,9},{9,8},{10,11... | collective-permute-start | bytes 2949128 | tf_op jit(solution)/shard_map/ppermute | solution.py:21
  206.9 56.1 %collective-permute-start.23 = (bf16[320,1024]{1,0:T(8,128)(2,1)S(1)}, bf16[320,1024]{1,0:T(8,128)(2,1)}, u32[]{:S(2)}, u32[]{:S(2)}) collective-permute-start(bf16[320,1024]{1,0:T(8,128)(2,1)S(1)} %bitcast.39), channel_id=1, source_target_pairs={{0,4},{4,0},{8,12},{12,8},{16,20},{20,16},{24,28},{28,24},{1,5},{5... | collective-permute-start | bytes 1966088 | tf_op jit(solution)/shard_map/ppermute | solution.py:21
  218.0 48.3 %collective-permute-start.26 = (bf16[320,1024]{1,0:T(8,128)(2,1)}, bf16[320,1024]{1,0:T(8,128)(2,1)}, u32[]{:S(2)}, u32[]{:S(2)}) collective-permute-start(bf16[320,1024]{1,0:T(8,128)(2,1)} %bitcast.8), channel_id=1, source_target_pairs={{0,4},{4,0},{8,12},{12,8},{16,20},{20,16},{24,28},{28,24},{1,5},{5... | collective-permute-start | bytes 1966088 | tf_op jit(solution)/shard_map/ppermute | solution.py:21
  231.1 37.2 %collective-permute-start.29 = (bf16[320,1024]{1,0:T(8,128)(2,1)}, bf16[320,1024]{1,0:T(8,128)(2,1)}, u32[]{:S(2)}, u32[]{:S(2)}) collective-permute-start(bf16[320,1024]{1,0:T(8,128)(2,1)} %bitcast.11), channel_id=1, source_target_pairs={{0,4},{4,0},{8,12},{12,8},{16,20},{20,16},{24,28},{28,24},{1,5},{5... | collective-permute-start | bytes 1966088 | tf_op jit(solution)/shard_map/ppermute | solution.py:21
  264.6 24.6 %collective-permute-start.24 = (bf16[160,1024]{1,0:T(8,128)(2,1)S(1)}, bf16[160,1024]{1,0:T(8,128)(2,1)S(1)}, u32[]{:S(2)}, u32[]{:S(2)}) collective-permute-start(bf16[160,1024]{1,0:T(8,128)(2,1)S(1)} %slice.152), channel_id=1, source_target_pairs={{0,8},{4,12},{8,0},{12,4},{16,24},{20,28},{24,16},{28,20},{1,9},{5... | collective-permute-start | bytes 983048 | tf_op jit(solution)/shard_map/ppermute | solution.py:21
  267.8 24.6 %collective-permute-start.27 = (bf16[160,1024]{1,0:T(8,128)(2,1)S(1)}, bf16[160,1024]{1,0:T(8,128)(2,1)S(1)}, u32[]{:S(2)}, u32[]{:S(2)}) collective-permute-start(bf16[160,1024]{1,0:T(8,128)(2,1)S(1)} %slice.151), channel_id=1, source_target_pairs={{0,8},{4,12},{8,0},{12,4},{16,24},{20,28},{24,16},{28,20},{1,9},{5... | collective-permute-start | bytes 983048 | tf_op jit(solution)/shard_map/ppermute | solution.py:21
  270.1 22.5 %collective-permute-start.30 = (bf16[160,1024]{1,0:T(8,128)(2,1)S(1)}, bf16[160,1024]{1,0:T(8,128)(2,1)S(1)}, u32[]{:S(2)}, u32[]{:S(2)}) collective-permute-start(bf16[160,1024]{1,0:T(8,128)(2,1)S(1)} %slice.150), channel_id=1, source_target_pairs={{0,8},{4,12},{8,0},{12,4},{16,24},{20,28},{24,16},{28,20},{1,9},{5... | collective-permute-start | bytes 983048 | tf_op jit(solution)/shard_map/ppermute | solution.py:21
  289.4 24.2 %collective-permute-start.25 = (bf16[80,1024]{1,0:T(8,128)(2,1)S(1)}, bf16[80,1024]{1,0:T(8,128)(2,1)S(1)}, u32[]{:S(2)}, u32[]{:S(2)}) collective-permute-start(bf16[80,1024]{1,0:T(8,128)(2,1)S(1)} %slice.155), channel_id=1, source_target_pairs={{0,16},{4,20},{8,24},{12,28},{16,0},{20,4},{24,8},{28,12},{1,17},{... | collective-permute-start | bytes 491528 | tf_op jit(solution)/shard_map/ppermute | solution.py:21
  292.5 21.1 %collective-permute-start.28 = (bf16[80,1024]{1,0:T(8,128)(2,1)S(1)}, bf16[80,1024]{1,0:T(8,128)(2,1)S(1)}, u32[]{:S(2)}, u32[]{:S(2)}) collective-permute-start(bf16[80,1024]{1,0:T(8,128)(2,1)S(1)} %slice.154), channel_id=1, source_target_pairs={{0,16},{4,20},{8,24},{12,28},{16,0},{20,4},{24,8},{28,12},{1,17},{... | collective-permute-start | bytes 491528 | tf_op jit(solution)/shard_map/ppermute | solution.py:21
  292.7 21.0 %collective-permute-start.31 = (bf16[80,1024]{1,0:T(8,128)(2,1)S(1)}, bf16[80,1024]{1,0:T(8,128)(2,1)S(1)}, u32[]{:S(2)}, u32[]{:S(2)}) collective-permute-start(bf16[80,1024]{1,0:T(8,128)(2,1)S(1)} %slice.153), channel_id=1, source_target_pairs={{0,16},{4,20},{8,24},{12,28},{16,0},{20,4},{24,8},{28,12},{1,17},{... | collective-permute-start | bytes 491528 | tf_op jit(solution)/shard_map/ppermute | solution.py:21
  (42 other events, 450.7 us)
